TPU v7x, 512 devices: a whole 4x8x8 slice. The times are simulated.
512 devices in a mesh: dp: 16 (over y_lo, z), expert: 32 (over x, y_hi, core).
Axes of the slice: x: 4, y: 8 (y_hi: 4, y_lo: 2; y = y_hi * 2 + y_lo), z: 8, core: 2. Of those that a mesh axis runs over, the one named last changes fastest.
Arguments:
- routes: int32 [65536, 6], P(('dp', 'expert')), may hold values from 0 to 159, all different within a row
- route_weights: float32 [65536, 6], P(('dp', 'expert')), may hold values from 0.02 to 0.5
- hidden_grads: bfloat16 [32, 3072, 1536], P('expert', 'dp'), may hold values from -6 to 6
- expert_weight: bfloat16 [32, 5120, 1536], P('expert', 'dp'), may hold values from -0.15625 to 0.15625
- normed: bfloat16 [65536, 5120], P(('dp', 'expert')), may hold values from -24 to 24
- key_grad: bfloat16 [65536, 64], P(('dp', 'expert')), may hold values from -6 to 6
- rope_weight: bfloat16 [64, 5120], replicated, may hold values from -0.75 to 0.75
Outputs:
- token_grad: bfloat16 [65536, 5120], P(('dp', 'expert'))
- rope_grad: float32 [64, 5120], P(None, 'expert')
Inputs may be any that keep to these rules, and one draw needn't show every extreme that they name: `routes`: each token names 6 different experts.
All inputs are finite; a program needn't handle non-finite values.
Results may differ from a plain program's by a relative error of at most 0.0017.
Values may be sent and summed in bfloat16 or wider, within the bound.
No kernel may reach another device: no remote copies, remote signals or barrier semaphores. Data moves between devices by JAX's collectives and lax.ppermute only.
A program may use at most 64 MiB of HBM per device.

v0:
```python
import jax
import jax.numpy as jnp
from jax import lax
from jax.sharding import PartitionSpec as P

TOPK = 6
EXP_DEV = 5


def combine_matrix(block_routes, block_weights, experts_here, capacity):
    inside = block_routes % EXP_DEV == 0
    column = block_routes // EXP_DEV
    chosen = (
        (column[:, None] == jnp.arange(experts_here, dtype=jnp.int32)[None, :]) & inside[:, None]
    ).astype(jnp.int32)
    earlier = jnp.cumsum(chosen, axis=0) - chosen
    slot = jnp.sum(earlier * chosen, axis=1)
    kept = inside & (slot < capacity)
    target = column * capacity + slot
    places = (
        target[:, None] == jnp.arange(experts_here * capacity, dtype=jnp.int32)[None, :]
    ) & kept[:, None]
    weighted = jnp.where(places, block_weights[:, None], jnp.float32(0.0))
    tokens_here = block_routes.shape[0] // TOPK
    return (
        weighted.reshape(tokens_here, TOPK, experts_here * capacity)
        .sum(axis=1)
        .astype(jnp.bfloat16)
    )


def body(routes, route_weights, hidden_grads, expert_weight, normed, key_grad, rope_weight):
    groups = lax.axis_size("dp")
    experts_here = lax.axis_size("expert")
    slot_rows = hidden_grads[0]
    projection = expert_weight[0]
    capacity = slot_rows.shape[0] // experts_here
    slice_width = projection.shape[0]
    width = slice_width * groups
    product = lax.dot_general(
        lax.all_gather(slot_rows, "dp", axis=0, tiled=True),
        projection,
        (((1,), (1,)), ((), ())),
        preferred_element_type=jnp.float32,
    )
    computed = product.astype(jnp.bfloat16)
    arranged = computed.reshape(groups, experts_here, capacity, slice_width)
    widened = lax.all_to_all(arranged, "dp", split_axis=0, concat_axis=3, tiled=True)
    returned = lax.all_to_all(widened, "expert", split_axis=1, concat_axis=1, tiled=True)
    returned = returned.reshape(experts_here * capacity, width)
    combine = combine_matrix(routes.reshape(-1), route_weights.reshape(-1), experts_here, capacity)
    routed = jnp.dot(combine, returned, preferred_element_type=jnp.float32)
    attention = jnp.dot(key_grad, rope_weight, preferred_element_type=jnp.float32)
    token_grad = (routed + attention).astype(jnp.bfloat16)
    partial_grad = lax.dot_general(
        key_grad, normed, (((0,), (0,)), ((), ())), preferred_element_type=jnp.float32
    )
    scale_factor = (key_grad.shape[0] * groups * experts_here) ** (-0.5)
    share = width // experts_here
    summed = lax.psum(partial_grad, ("dp", "expert"))
    mine = lax.dynamic_slice_in_dim(summed, lax.axis_index("expert") * share, share, 1)
    rope_grad = mine * scale_factor
    return (token_grad, rope_grad)


def solution(mesh):
    return jax.shard_map(
        body,
        mesh=mesh,
        in_specs=(
            P(("dp", "expert"), None),
            P(("dp", "expert"), None),
            P("expert", "dp", None),
            P("expert", "dp", None),
            P(("dp", "expert"), None),
            P(("dp", "expert"), None),
            P(),
        ),
        out_specs=(P(("dp", "expert"), None), P(None, "expert")),
        check_vma=False,
    )
```

profile of v0, /device:TPU:1, one launch (start us, length us, event | category | flops | bytes accessed | tf_op | source)
XLA Modules:
  0.0 533.2 jit_solution(17359742109522759625)
XLA Ops:
  8.1 0.7 all-gather.3.cloned.1.call-update
  8.7 122.7 %all-gather.3.cloned.1.call-done = bf16[1,3072,1536]{2,1,0:T(8,128)(2,1)} async-done(((bf16[1,192,1536]{2,1,0:T(8,128)(2,1)}), bf16[1,3072,1536]{2,1,0:T(8,128)(2,1)}) %all-gather.3.cloned.1.call-update) | async-done | bytes 9437200 | tf_op jit(solution)/shard_map/all_gather | solution.py:41
  131.4 7.1 %fusion.3 = bf16[3072,320]{0,1:T(8,128)(2,1)S(1)} fusion(bf16[1,3072,1536]{2,1,0:T(8,128)(2,1)} %all-gather.3.cloned.1.call-done, bf16[1,320,1536]{2,1,0:T(8,128)(2,1)} %param.10), kind=kOutput, calls=%fused_computation.4 | convolution fusion | flops 3020881920 | bytes 12386304 | tf_op jit(solution)/shard_map/dot_general | solution.py:40
  138.6 2.4 copy.48
  141.0 5.3 reshape.113
  146.3 2.3 copy.49
  148.6 57.9 %all_to_all.23 = bf16[16,32,6,320]{3,1,2,0:T(8,128)(2,1)S(1)} all-to-all(bf16[16,32,6,320]{3,1,2,0:T(8,128)(2,1)S(1)} %copy.49), channel_id=1, replica_groups=mesh['dp'=16,'expert'=32] {'dp'}, dimensions={0} | all-to-all | bytes 3932160 | tf_op jit(solution)/shard_map/all_to_all | solution.py:48
  206.5 2.8 copy.52
  209.3 5.6 %reshape.116 = bf16[1,32,6,5120]{3,2,0,1:T(8,128)(2,1)} reshape(bf16[1,32,6,16,320]{4,3,2,1,0:T(8,128)(2,1)} %copy.52) | data formatting | bytes 3932160 | tf_op jit(solution)/shard_map/all_to_all | solution.py:48
  214.9 10.9 %all-to-all-start.1 = ((bf16[1,32,6,5120]{3,2,0,1:T(8,128)(2,1)}), bf16[1,32,6,5120]{3,2,0,1:T(8,128)(2,1)}, u32[]{:S(2)}, u32[]{:S(2)}) async-start(bf16[1,32,6,5120]{3,2,0,1:T(8,128)(2,1)} %reshape.116), calls=%async_computation.1 | async-start | bytes 5242880 | tf_op jit(solution)/shard_map/all_to_all | solution.py:49
  226.0 1.4 fusion.22
  227.4 0.1 copy.39
  227.5 0.1 ne.74
  227.7 0.1 ne.71
  227.9 0.1 copy.40
  228.0 0.1 rem.41
  228.1 0.1 rem.39
  228.2 0.1 copy.41
  228.4 0.1 div.22
  228.5 0.1 div.21
  228.7 1.7 reduce-window.6
  230.4 0.3 slice_reduce_fusion
  230.7 0.1 fusion.10
  230.9 0.1 reduce_sum.21
  231.0 0.1 copy.46
  231.1 0.1 select_reduce_fusion
  231.2 287.4 %all-reduce.2.cloned.1.call-done = f32[64,5120]{1,0:T(8,128)} async-done(((f32[64,5120]{1,0:T(8,128)}), f32[64,5120]{1,0:T(8,128)}) %all-reduce.2.cloned.1.call-update) | async-done | bytes 1310736 | tf_op jit(solution)/shard_map/psum | solution.py:60
  518.7 1.6 dynamic-slice_multiply_fusion
  520.3 2.8 reshape.114
  523.1 0.5 fusion.23
  523.6 0.5 copy-done.1
  524.2 1.6 fusion.2
  (23 shorter events, 0.3 us)
Async XLA Ops:
  8.0 217.9 %copy-start = (bf16[128,5120]{1,0:T(8,128)(2,1)S(1)}, bf16[128,5120]{1,0:T(8,128)(2,1)}, u32[]{:S(2)}) copy-start(bf16[128,5120]{1,0:T(8,128)(2,1)} %param.11) | copy-start | bytes 3932164
  8.0 123.4 %all-gather.3.cloned.1.call-start = ((), (), s32[]{:S(2)}) async-start(), calls=%async_computation.3 | async-start | bytes 10027008 | tf_op jit(solution)/shard_map/all_gather | solution.py:41
  214.9 11.0 %copy-start.2 = (bf16[128,64]{0,1:T(8,128)(2,1)S(1)}, bf16[128,64]{0,1:T(8,128)(2,1)}, u32[]{:S(2)}) copy-start(bf16[128,64]{0,1:T(8,128)(2,1)} %param.12) | copy-start | bytes 49156
  214.9 305.3 %all-to-all-start.1 = ((bf16[1,32,6,5120]{3,2,0,1:T(8,128)(2,1)}), bf16[1,32,6,5120]{3,2,0,1:T(8,128)(2,1)}, u32[]{:S(2)}, u32[]{:S(2)}) async-start(bf16[1,32,6,5120]{3,2,0,1:T(8,128)(2,1)} %reshape.116), calls=%async_computation.1 | async-start | bytes 5242880 | tf_op jit(solution)/shard_map/all_to_all | solution.py:49
  225.9 1.5 copy-start.3
  225.9 5.2 copy-start.4
  225.9 292.8 %all-reduce.2.cloned.1.call-start = ((), (), s32[]{:S(2)}) async-start(), calls=%async_computation.2 | async-start | bytes 2621440 | tf_op jit(solution)/shard_map/psum | solution.py:60
  523.1 1.1 copy-start.1
Sparse Core Ops, SparseCore 0:
  10.9 120.4 all-gather.2
Sparse Core Ops, SparseCore 1:
  232.0 286.7 all-reduce.1
where the time goes:
time: 535 us; the launch traced here: 533 us
  waiting for transfers between devices  411 us (77%)
  blocking collectives  57.9 us (11%)
  local copies, waits for them, and re-layouts  23.5 us (4%)
  between operations  15.7 us (3%)
  starting transfers between devices  11 us (2%)
  matrix products  10.6 us (2%)
    psum x1, waiting for transfers between devices, body(): summed = lax.psum(partial_grad, ('dp', 'expert'))  287 us
    all_gather x1, waiting for transfers between devices, body(): lax.all_gather(slot_rows, 'dp', axis=0, tiled=True)  123 us
    all_to_all x1, blocking collectives, body(): lax.all_to_all(arranged, 'dp', split_axis=0, concat_axis=3, tiled=True)  57.9 us
    all_to_all x1, starting transfers between devices, body(): lax.all_to_all(widened, 'expert', split_axis=1, concat_axis=1, tiled=True)  10.9 us
  transfers between devices with their start and end apart: 3, of which 2 were waited for; matrix products, arithmetic and copies ran while one was open for 1% of the time, Pallas kernels for 0%

commit v1 on v0

v1 whole, which is shorter than its diff:
```python
import jax
import jax.numpy as jnp
from jax import lax
from jax.sharding import Mesh
from jax.sharding import PartitionSpec as P

TOPK = 6
EXP_DEV = 5
PAD = 8

DP = ("ylo", "z")
EXPERT = ("x", "yhi", "core")
ALL = DP + EXPERT
PLANE = ("ylo",) + EXPERT


def combine_matrix(block_routes, block_weights, experts_here, capacity):
    inside = block_routes % EXP_DEV == 0
    column = block_routes // EXP_DEV
    chosen = (
        (column[:, None] == jnp.arange(experts_here, dtype=jnp.int32)[None, :]) & inside[:, None]
    ).astype(jnp.int32)
    earlier = jnp.cumsum(chosen, axis=0) - chosen
    slot = jnp.sum(earlier * chosen, axis=1)
    kept = inside & (slot < capacity)
    target = column * PAD + slot
    places = (
        target[:, None] == jnp.arange(experts_here * PAD, dtype=jnp.int32)[None, :]
    ) & kept[:, None]
    weighted = jnp.where(places, block_weights[:, None], jnp.float32(0.0))
    tokens_here = block_routes.shape[0] // TOPK
    return (
        weighted.reshape(tokens_here, TOPK, experts_here * PAD)
        .sum(axis=1)
        .astype(jnp.bfloat16)
    )


def body(routes, route_weights, hidden_grads, expert_weight, normed, key_grad, rope_weight):
    groups = lax.axis_size(DP)
    experts_here = lax.axis_size(EXPERT)
    pairs = lax.axis_size("ylo")
    slot_rows = hidden_grads[0]
    projection = expert_weight[0]
    depth = slot_rows.shape[1]
    capacity = slot_rows.shape[0] // experts_here
    width = projection.shape[0] * groups

    partial_grad = lax.dot_general(
        normed, key_grad, (((0,), (0,)), ((), ())), preferred_element_type=jnp.float32
    )
    scale_factor = (key_grad.shape[0] * groups * experts_here) ** (-0.5)
    mine = lax.psum_scatter(partial_grad, EXPERT, scatter_dimension=0, tiled=True)
    terms = lax.all_gather(mine, DP, axis=0)
    rope_grad = jnp.sum(terms, axis=0).T * scale_factor

    other = lax.ppermute(slot_rows, "ylo", [(0, 1), (1, 0)])
    low = lax.axis_index("ylo") == 0
    both = jnp.stack([jnp.where(low, slot_rows, other), jnp.where(low, other, slot_rows)])
    both = both.reshape(pairs * experts_here, capacity, depth)
    both = jnp.pad(both, ((0, 0), (0, PAD - capacity), (0, 0)))
    both = both.reshape(pairs * experts_here * PAD, depth)
    gathered = lax.all_gather(projection, "z", axis=0, tiled=True)
    product = lax.dot_general(
        both, gathered, (((1,), (1,)), ((), ())), preferred_element_type=jnp.float32
    )
    computed = product.astype(jnp.bfloat16).reshape(pairs * experts_here, PAD, -1)
    returned = lax.all_to_all(computed, PLANE, split_axis=0, concat_axis=0, tiled=True)
    returned = returned.reshape(pairs, experts_here * PAD, -1)
    combine = combine_matrix(routes.reshape(-1), route_weights.reshape(-1), experts_here, capacity)
    routed = jnp.concatenate(
        [jnp.dot(combine, returned[g], preferred_element_type=jnp.float32) for g in range(pairs)],
        axis=1,
    )
    attention = jnp.dot(key_grad, rope_weight, preferred_element_type=jnp.float32)
    token_grad = (routed + attention).astype(jnp.bfloat16)
    return (token_grad, rope_grad)


def solution(mesh):
    wide = Mesh(mesh.devices.reshape(2, 8, 4, 4, 2), ALL)
    return jax.shard_map(
        body,
        mesh=wide,
        in_specs=(
            P(ALL, None),
            P(ALL, None),
            P(EXPERT, DP, None),
            P(EXPERT, DP, None),
            P(ALL, None),
            P(ALL, None),
            P(),
        ),
        out_specs=(P(ALL, None), P(None, EXPERT)),
        check_vma=False,
    )
```

time: 535 us -> 287 us (0.54)
  the two profiles are of different devices: /device:TPU:1 before, /device:TPU:8 now
where the time goes in v1:
time: 287 us
  waiting for transfers between devices  186 us (65%)
  blocking collectives  40.4 us (14%)
  starting transfers between devices  18.5 us (6%)
  matrix products  16.7 us (6%)
  between operations  15.7 us (5%)
  local copies, waits for them, and re-layouts  4.65 us (2%)
  other arithmetic  4.31 us (2%)
    unnamed x3, waiting for transfers between devices  97.4 us
    all_gather x1, waiting for transfers between devices, body(): gathered = lax.all_gather(projection, 'z', axis=0, tiled=True)  79.6 us
    all_gather x1, blocking collectives, body(): terms = lax.all_gather(mine, DP, axis=0)  40.4 us
    all_to_all x1, starting transfers between devices, body(): lax.all_to_all(computed, PLANE, split_axis=0, concat_axis=0, tiled=True)  10.6 us
    dot_general x1, matrix products, body(): lax.dot_general(both, gathered, (((1,), (1,)), ((), ())), preferred_eleme...  9.54 us
    ppermute x1, waiting for transfers between devices, body(): other = lax.ppermute(slot_rows, 'ylo', [(0, 1), (1, 0)])  9.43 us
    ppermute x1, starting transfers between devices, body(): other = lax.ppermute(slot_rows, 'ylo', [(0, 1), (1, 0)])  7.73 us
  transfers between devices with their start and end apart: 4, of which 3 were waited for; matrix products, arithmetic and copies ran while one was open for 4% of the time, Pallas kernels for 0%

profile of v1, /device:TPU:8, one launch (start us, length us, event | category | flops | bytes accessed | tf_op | source)
XLA Modules:
  0.0 286.6 jit_solution(7069855976261895054)
XLA Ops:
  8.1 0.7 all-gather.5.cloned.1.call-update
  8.7 7.7 %collective-permute-start = (bf16[192,1536]{1,0:T(8,128)(2,1)}, bf16[192,1536]{1,0:T(8,128)(2,1)S(1)}, u32[]{:S(2)}, u32[]{:S(2)}) collective-permute-start(bf16[192,1536]{1,0:T(8,128)(2,1)} %bitcast.55), channel_id=1, source_target_pairs={{0,256},{256,0},{1,257},{257,1},{2,258},{258,2},{3,259},{259,3},{4... | collective-permute-start | bytes 1769480 | tf_op jit(solution)/shard_map/ppermute | solution.py:57
  16.5 9.4 %collective-permute-done = bf16[192,1536]{1,0:T(8,128)(2,1)S(1)} collective-permute-done((bf16[192,1536]{1,0:T(8,128)(2,1)}, bf16[192,1536]{1,0:T(8,128)(2,1)S(1)}, u32[]{:S(2)}, u32[]{:S(2)}) %collective-permute-start) | collective-permute-done | bytes 589856 | tf_op jit(solution)/shard_map/ppermute | solution.py:57
  25.9 1.1 select_bitcast_fusion.1
  27.1 0.1 pad_maximum_fusion
  27.2 1.4 reshape.121
  28.5 79.6 %all-gather.5.cloned.1.call-done = bf16[1,2560,1536]{2,1,0:T(8,128)(2,1)} async-done(((bf16[1,320,1536]{2,1,0:T(8,128)(2,1)}), bf16[1,2560,1536]{2,1,0:T(8,128)(2,1)}) %all-gather.5.cloned.1.call-update) | async-done | bytes 7864336 | tf_op jit(solution)/shard_map/all_gather | solution.py:63
  108.2 9.5 %fusion.6 = bf16[64,8,2560]{2,1,0:T(8,128)(2,1)} fusion(bf16[1,2560,1536]{2,1,0:T(8,128)(2,1)} %all-gather.5.cloned.1.call-done, bf16[64,6,1536]{2,1,0:T(8,128)(2,1)} %reshape.121), kind=kOutput, calls=%fused_computation.5 | convolution fusion | flops 4027842560 | bytes 11665408 | tf_op jit(solution)/shard_map/dot_general | solution.py:64
  117.7 10.6 %all-to-all-start = ((bf16[64,8,2560]{2,1,0:T(8,128)(2,1)}), bf16[64,8,2560]{2,1,0:T(8,128)(2,1)}, u32[]{:S(2)}, u32[]{:S(2)}) async-start(bf16[64,8,2560]{2,1,0:T(8,128)(2,1)} %fusion.6), calls=%async_computation | async-start | bytes 5242880 | tf_op jit(solution)/shard_map/all_to_all | solution.py:68
  128.5 2.2 fusion.29
  130.7 0.7 copy-done.3
  131.3 0.1 copy.30
  131.4 0.1 div.21
  131.6 0.1 div.22
  131.7 0.1 copy.28
  131.9 0.1 ne.71
  132.0 0.1 ne.74
  132.2 0.1 copy.29
  132.3 0.1 rem.39
  132.4 0.1 rem.41
  132.6 1.7 reduce-window.6
  134.4 0.3 slice_reduce_fusion
  134.7 0.1 fusion.16
  134.8 0.1 reduce_sum.30
  135.0 0.4 select_reduce_fusion
  135.4 96.7 %reduce-scatter.4.cloned.1.call-done = f32[160,64]{1,0:T(8,128)} async-done(((f32[5120,64]{1,0:T(8,128)}), f32[160,64]{1,0:T(8,128)}) %reduce-scatter.4.cloned.1.call-update) | async-done | bytes 40976
  232.1 1.0 copy.38
  233.1 40.4 %all-gather.2 = f32[16,160,64]{1,2,0:T(8,128)S(1)} all-gather(f32[1,160,64]{1,2,0:T(8,128)S(1)} %bitcast.56), channel_id=3, replica_groups=mesh['ylo'=2,'z'=8,'x'=4,'yhi'=4,'core'=2] {'ylo','z'}, dimensions={0}, use_global_device_ids=true | all-gather | bytes 696320 | tf_op jit(solution)/shard_map/all_gather | solution.py:54
  273.6 0.6 multiply_bitcast_fusion
  274.2 1.7 fusion.11
  275.9 1.7 fusion.12
  277.6 1.6 fusion.2
  (25 shorter events, 0.4 us)
Async XLA Ops:
  8.0 120.4 %copy-start = (bf16[128,5120]{1,0:T(8,128)(2,1)S(1)}, bf16[128,5120]{1,0:T(8,128)(2,1)}, u32[]{:S(2)}) copy-start(bf16[128,5120]{1,0:T(8,128)(2,1)} %param.11) | copy-start | bytes 3932164
  8.0 100.2 %all-gather.5.cloned.1.call-start = ((), (), s32[]{:S(2)}) async-start(), calls=%async_computation.2 | async-start | bytes 8847360 | tf_op jit(solution)/shard_map/all_gather | solution.py:63
  8.7 17.2 %collective-permute-start = (bf16[192,1536]{1,0:T(8,128)(2,1)}, bf16[192,1536]{1,0:T(8,128)(2,1)S(1)}, u32[]{:S(2)}, u32[]{:S(2)}) collective-permute-start(bf16[192,1536]{1,0:T(8,128)(2,1)} %bitcast.55), channel_id=1, source_target_pairs={{0,256},{256,0},{1,257},{257,1},{2,258},{258,2},{3,259},{259,3},{4... | collective-permute-start | bytes 1769480 | tf_op jit(solution)/shard_map/ppermute | solution.py:57
  117.7 10.7 %copy-start.2 = (bf16[128,64]{0,1:T(8,128)(2,1)S(1)}, bf16[128,64]{0,1:T(8,128)(2,1)}, u32[]{:S(2)}) copy-start(bf16[128,64]{0,1:T(8,128)(2,1)} %param.12) | copy-start | bytes 49156
  117.7 156.5 %all-to-all-start = ((bf16[64,8,2560]{2,1,0:T(8,128)(2,1)}), bf16[64,8,2560]{2,1,0:T(8,128)(2,1)}, u32[]{:S(2)}, u32[]{:S(2)}) async-start(bf16[64,8,2560]{2,1,0:T(8,128)(2,1)} %fusion.6), calls=%async_computation | async-start | bytes 5242880 | tf_op jit(solution)/shard_map/all_to_all | solution.py:68
  128.4 103.7 %reduce-scatter.4.cloned.1.call-start = ((), (), s32[]{:S(2)}) async-start(), calls=%async_computation.3 | async-start | bytes 2703360
  130.6 0.7 copy-start.3
  130.6 4.4 %copy-start.4 = (f32[128,6]{0,1:T(8,128)S(1)}, f32[128,6]{0,1:T(8,128)}, u32[]{:S(2)}) copy-start(f32[128,6]{0,1:T(8,128)} %param.8) | copy-start | bytes 9220
  275.9 1.7 copy-start.1
Sparse Core Ops, SparseCore 0:
  10.9 97.2 all-gather.4
Sparse Core Ops, SparseCore 1:
  133.3 98.7 reduce-scatter.3

commit v2 on v1

v2 whole, which is shorter than its diff:
```python
import functools

import jax
import jax.numpy as jnp
from jax import lax
from jax.experimental import pallas as pl
from jax.experimental.pallas import tpu as pltpu
from jax.sharding import Mesh
from jax.sharding import PartitionSpec as P

EXP_DEV = 5
PAD = 8

DP = ("ylo", "z")
EXPERT = ("x", "yhi", "core")
ALL = DP + EXPERT
PLANE = ("ylo",) + EXPERT

VMEM = pl.BlockSpec(memory_space=pltpu.VMEM)
SMEM = pl.BlockSpec(memory_space=pltpu.SMEM)


def call(kernel, out_shape, in_specs, flops, moved, scratch=(), after=()):
    taken = len(in_specs)

    def without(*refs):
        kernel(*refs[:taken], *refs[taken + len(after) :])

    run = pl.pallas_call(
        without,
        out_shape=out_shape,
        in_specs=list(in_specs) + [pl.BlockSpec(memory_space=pl.ANY)] * len(after),
        out_specs=jax.tree.map(lambda _: VMEM, out_shape),
        scratch_shapes=list(scratch),
        compiler_params=pltpu.CompilerParams(vmem_limit_bytes=32 * 1024 * 1024),
        cost_estimate=pl.CostEstimate(flops=flops, bytes_accessed=moved, transcendentals=0),
    )
    return lambda *args: run(*args, *after)


def struct(shape, dtype):
    return jax.ShapeDtypeStruct(shape, dtype)


def partial_kernel(order, normed_ref, key_ref, out_ref):
    product = lax.dot_general(
        key_ref[...], normed_ref[...], (((0,), (0,)), ((), ())), preferred_element_type=jnp.float32
    )
    key, width = product.shape
    share = width // len(order)
    rest = share - 128
    group = key * rest // 128
    rows = key + group
    for e, place in enumerate(order):
        out_ref[place * rows : place * rows + key, :] = product[:, e * share : e * share + 128]
        tail = product[:, e * share + 128 : (e + 1) * share]
        out_ref[place * rows + key : (place + 1) * rows, :] = jnp.concatenate(
            [tail[a * group : (a + 1) * group] for a in range(key // group)], axis=1
        )


def rope_kernel(key, share, scale_factor, total_ref, out_ref):
    total = total_ref[...] * scale_factor
    rest = share - 128
    tail = jnp.concatenate([total[key:, a * rest : (a + 1) * rest] for a in range(128 // rest)], axis=0)
    out_ref[...] = jnp.concatenate([total[:key, :], tail], axis=1)


def combine_kernel(experts, capacity, routes_ref, weights_ref, out_ref):
    tokens, topk = routes_ref.shape
    expert = lax.broadcasted_iota(jnp.int32, (tokens, experts), 1)
    chosen = jnp.zeros((tokens, experts), jnp.float32)
    weight = jnp.zeros((tokens, experts), jnp.float32)
    for k in range(topk):
        here = routes_ref[:, k : k + 1] == expert * EXP_DEV
        chosen = jnp.where(here, 1.0, chosen)
        weight = jnp.where(here, weights_ref[:, k : k + 1], weight)
    row = lax.broadcasted_iota(jnp.int32, (tokens, tokens), 0)
    column = lax.broadcasted_iota(jnp.int32, (tokens, tokens), 1)
    before = (column < row).astype(jnp.bfloat16)
    slot = jnp.dot(before, chosen.astype(jnp.bfloat16), preferred_element_type=jnp.float32)
    slot = jnp.where(chosen > 0.0, slot, 128.0)
    spread = (
        lax.broadcasted_iota(jnp.int32, (experts, experts * PAD), 1) // PAD
        == lax.broadcasted_iota(jnp.int32, (experts, experts * PAD), 0)
    ).astype(jnp.bfloat16)
    slots = jnp.dot(slot.astype(jnp.bfloat16), spread, preferred_element_type=jnp.float32)
    weights = jnp.dot(weight.astype(jnp.bfloat16), spread, preferred_element_type=jnp.float32)
    place = lax.rem(lax.broadcasted_iota(jnp.int32, slots.shape, 1), PAD)
    kept = (slots == place.astype(jnp.float32)) & (place < capacity)
    out_ref[...] = jnp.where(kept, weights, 0.0).astype(out_ref.dtype)


def rows_kernel(capacity, low_ref, own_ref, other_ref, out_ref):
    own, other = own_ref[...], other_ref[...]
    low = low_ref[0] == 1
    rows, depth = own.shape
    empty = jnp.zeros((rows // capacity, PAD - capacity, depth), own.dtype)
    for g, part in enumerate((jnp.where(low, own, other), jnp.where(low, other, own))):
        spaced = jnp.concatenate([part.reshape(rows // capacity, capacity, depth), empty], axis=1)
        out_ref[g] = spaced.reshape(rows // capacity * PAD, depth)


def products_kernel(capacity, rows_ref, *refs):
    weights, (out_ref, lines_ref) = refs[:-2], refs[-2:]
    targets, lines, lanes = out_ref.shape
    products = [
        lax.dot_general(
            rows_ref[...], ref[...], (((1,), (1,)), ((), ())), preferred_element_type=jnp.float32
        )
        for ref in weights
    ]
    width = sum(product.shape[1] for product in products)
    blocks = -(-width // lanes)
    if blocks * lanes > width:
        products.append(jnp.zeros((targets * PAD, blocks * lanes - width), jnp.float32))
    product = jnp.concatenate(products, axis=1).reshape(targets, PAD, blocks * lanes)
    for j in range(blocks):
        lines_ref[:, j * capacity : (j + 1) * capacity, :] = product[
            :, :capacity, j * lanes : (j + 1) * lanes
        ]
    if lines > blocks * capacity:
        lines_ref[:, blocks * capacity :, :] = jnp.zeros(
            (targets, lines - blocks * capacity, lanes), jnp.float32
        )
    out_ref[...] = lines_ref[...].astype(out_ref.dtype)


def routed_sums(capacity, combine, chunk_ref, lines_ref):
    targets, lines, lanes = chunk_ref.shape
    blocks = lines // capacity
    lines_ref[:, :lines, :] = chunk_ref[...].astype(jnp.float32)
    lines_ref[:, lines : lines + PAD, :] = jnp.zeros((targets, PAD, lanes), jnp.float32)
    columns = [
        lines_ref[:, j * capacity : j * capacity + PAD, :].reshape(targets * PAD, lanes)
        for j in range(blocks)
    ]
    rows = jnp.concatenate(columns, axis=1).astype(jnp.bfloat16)
    half = combine.shape[1]
    return [
        jnp.dot(combine, rows[g * half : (g + 1) * half], preferred_element_type=jnp.float32)
        for g in range(rows.shape[0] // half)
    ]


def halves_kernel(half, low_ref, high_ref, low_out, high_out):
    low_out[...] = low_ref[:half, :]
    high_out[...] = high_ref[half:, :]


def early_kernel(capacity, layout, late, z_ref, combine_ref, key_ref, rope_ref, *refs):
    chunks, (held_ref, rest_ref, attention_ref, lines_ref) = refs[:-4], refs[-4:]
    groups, tokens, piece = attention_ref.shape
    pairs, ring = held_ref.shape[:2]
    attention = jnp.dot(key_ref[...], rope_ref[...], preferred_element_type=jnp.float32)
    for d in range(groups):
        attention_ref[d] = attention[:, d * piece : (d + 1) * piece]
    z = z_ref[0]

    def here(g, distance):
        return attention_ref[g * ring + lax.rem(z + distance + ring, ring)]

    for chunk, distances in zip(chunks, layout):
        for g, routed in enumerate(routed_sums(capacity, combine_ref[...], chunk, lines_ref)):
            for i, distance in enumerate(distances):
                held_ref[g, distance % ring] = (
                    routed[:, i * piece : (i + 1) * piece] + here(g, distance)
                ).astype(held_ref.dtype)
    for g in range(pairs):
        for i, distance in enumerate(late):
            held_ref[g, distance % ring] = jnp.zeros((tokens, piece), held_ref.dtype)
            rest_ref[g, i] = here(g, distance)


def late_kernel(
    capacity, distances, early, z_ref, combine_ref, chunk_ref, held_ref, rest_ref, out_ref, pieces_ref, lines_ref
):
    pairs, ring, tokens, piece = held_ref.shape
    z = z_ref[0]
    for g, routed in enumerate(routed_sums(capacity, combine_ref[...], chunk_ref, lines_ref)):
        for distance in early:
            pieces_ref[distance % ring] = held_ref[g, distance % ring]
        for i, distance in enumerate(distances):
            pieces_ref[distance % ring] = (
                routed[:, i * piece : (i + 1) * piece] + rest_ref[g, i]
            ).astype(pieces_ref.dtype)
        for h in range(ring // 2):
            left = pieces_ref[lax.rem(2 * h - z + ring, ring)]
            right = pieces_ref[lax.rem(2 * h + 1 - z + ring, ring)]
            columns = slice((g * ring + 2 * h) * piece, (g * ring + 2 * h + 2) * piece)
            out_ref[:, columns] = jnp.concatenate([left, right], axis=1)


def body(routes, route_weights, hidden_grads, expert_weight, normed, key_grad, rope_weight):
    groups = lax.axis_size(DP)
    experts_here = lax.axis_size(EXPERT)
    pairs = lax.axis_size("ylo")
    ring = lax.axis_size("z")
    slot_rows = hidden_grads[0]
    projection = expert_weight[0]
    depth = slot_rows.shape[1]
    capacity = slot_rows.shape[0] // experts_here
    piece = projection.shape[0]
    tokens, key_size = key_grad.shape
    width = piece * groups
    share = width // experts_here
    last = ring // 2
    rows = experts_here * PAD
    z = lax.axis_index("z").astype(jnp.int32).reshape(1)
    low = (lax.axis_index("ylo") == 0).astype(jnp.int32).reshape(1)
    up = [(i, (i + 1) % ring) for i in range(ring)]
    down = [(i, (i - 1) % ring) for i in range(ring)]

    packed = key_size * share // 128
    columns, cores = lax.axis_size("yhi"), lax.axis_size("core")
    order = tuple(
        (e // (columns * cores) * cores + e % cores) * columns + e // cores % columns
        for e in range(experts_here)
    )
    partial_grad = call(
        functools.partial(partial_kernel, order),
        struct((experts_here * packed, 128), jnp.float32),
        [VMEM, VMEM],
        2 * tokens * key_size * width,
        3 * 10**6,
    )(normed, key_grad)
    mine = lax.psum_scatter(partial_grad, ("x", "core"), scatter_dimension=0, tiled=True)

    slot_rows, partial_grad = lax.optimization_barrier((slot_rows, partial_grad))
    other = lax.ppermute(slot_rows, "ylo", [(0, 1), (1, 0)])

    def spaced_rows(other):
        return call(
            functools.partial(rows_kernel, capacity),
            struct((pairs, rows, depth), jnp.bfloat16),
            [SMEM, VMEM, VMEM],
            0,
            3 * 10**6,
        )(low, slot_rows, other).reshape(pairs * rows, depth)

    def products(weights, flops, after=()):
        columns = sum(w.shape[0] for w in weights)
        lines = -(-(-(-columns // 128) * capacity) // 16) * 16
        shape = (pairs * experts_here, lines, 128)
        return call(
            functools.partial(products_kernel, capacity),
            struct(shape, jnp.bfloat16),
            [VMEM] * (1 + len(weights)),
            flops,
            4 * 10**6,
            [pltpu.VMEM(shape, jnp.float32)],
            after,
        )(both, *weights)

    def send(computed):
        return lax.all_to_all(computed, PLANE, split_axis=0, concat_axis=0, tiled=True)

    layout = ((0, -1, 1), (-2, 2), (-3, 3, 4))
    below, above = [projection], [projection]
    below.append(lax.ppermute(below[-1], "z", up))
    above.append(lax.ppermute(above[-1], "z", down))
    below[1], other = lax.optimization_barrier((below[1], other))
    both = spaced_rows(other)
    first = products([projection, below[1], above[1]], 25 * 10**9)
    below.append(lax.ppermute(below[-1], "z", up))
    above.append(lax.ppermute(above[-1], "z", down))
    below[2], _, mine = lax.optimization_barrier((below[2], first, mine))
    second = products([below[2], above[2]], 25 * 10**9)
    below.append(lax.ppermute(below[-1], "z", up))
    above.append(lax.ppermute(above[-1], "z", down))
    sent = [send(first)]
    half = piece // 2
    half_low, half_high = call(
        functools.partial(halves_kernel, half),
        [struct((half, depth), jnp.bfloat16)] * 2,
        [VMEM] * 2,
        0,
        3 * 10**6,
        after=[second] + sent,
    )(below[-1], above[-1])
    last_low = lax.ppermute(half_low, "z", up)
    last_high = lax.ppermute(half_high, "z", down)
    sent.append(send(second))
    terms = lax.all_gather(mine, ("yhi", "ylo"), axis=0, tiled=True)
    terms = terms.reshape(columns * pairs, columns, packed, 128)
    summed = jnp.sum(lax.dynamic_index_in_dim(terms, lax.axis_index("yhi"), 1, False), axis=0)
    third = products([below[3], above[3], last_low, last_high], 15 * 10**9, [summed] + sent[1:])
    chunks = sent + [send(third)]

    bit = 1
    while bit < ring:
        summed = summed + lax.ppermute(summed, "z", [(i, i ^ bit) for i in range(ring)])
        bit *= 2
    scale_factor = (tokens * groups * experts_here) ** (-0.5)
    rope_grad = call(
        functools.partial(rope_kernel, key_size, share, scale_factor),
        struct((key_size, share), jnp.float32),
        [VMEM],
        0,
        10**6,
    )(summed)

    combine = call(
        functools.partial(combine_kernel, experts_here, capacity),
        struct((tokens, rows), jnp.bfloat16),
        [VMEM, VMEM],
        10**7,
        10**6,
    )(routes, route_weights)
    most = max(chunk.shape[1] for chunk in chunks)
    lines = pltpu.VMEM((pairs * experts_here, most + PAD, 128), jnp.float32)
    held, rest = call(
        functools.partial(early_kernel, capacity, layout[:-1], layout[-1]),
        [
            struct((pairs, ring, tokens, piece), jnp.bfloat16),
            struct((pairs, len(layout[-1]), tokens, piece), jnp.float32),
        ],
        [SMEM] + [VMEM] * (3 + len(chunks[:-1])),
        4 * 10**8,
        8 * 10**6,
        [pltpu.VMEM((groups, tokens, piece), jnp.float32), lines],
    )(z, combine, key_grad, rope_weight, *chunks[:-1])
    token_grad = call(
        functools.partial(late_kernel, capacity, layout[-1], sum(layout[:-1], ())),
        struct((tokens, width), jnp.bfloat16),
        [SMEM] + [VMEM] * 4,
        4 * 10**7,
        3 * 10**6,
        [pltpu.VMEM((ring, tokens, piece), jnp.bfloat16), lines],
    )(z, combine, chunks[-1], held, rest)
    return (token_grad, rope_grad)


def solution(mesh):
    wide = Mesh(mesh.devices.reshape(2, 8, 4, 4, 2), ALL)
    return jax.shard_map(
        body,
        mesh=wide,
        in_specs=(
            P(ALL, None),
            P(ALL, None),
            P(EXPERT, DP, None),
            P(EXPERT, DP, None),
            P(ALL, None),
            P(ALL, None),
            P(),
        ),
        out_specs=(P(ALL, None), P(None, EXPERT)),
        check_vma=False,
    )
```

time: 287 us -> 176 us (0.61)
  the two profiles are of different devices: /device:TPU:8 before, /device:TPU:1 now
where the time goes in v2:
time: 176 us; the launch traced here: 174 us
  starting transfers between devices  81.8 us (46%)
  waiting for transfers between devices  43.7 us (25%)
  Pallas kernels  22.8 us (13%)
  between operations  14.4 us (8%)
  local copies, waits for them, and re-layouts  10.1 us (6%)
    all_to_all x3, starting transfers between devices, send(): lax.all_to_all(computed, PLANE, split_axis=0, concat_axis=0, tiled=True)  29.9 us
    pallas_call x10, Pallas kernels, call(): return lambda *args: run(*args, *after)  22.8 us
    ppermute x3, starting transfers between devices, body(): above.append(lax.ppermute(above[-1], 'z', down))  18.5 us
    ppermute x3, starting transfers between devices, body(): lax.ppermute(summed, 'z', [(i, i ^ bit) for i in range(ring)])  15 us
    all_gather x1, waiting for transfers between devices, body(): terms = lax.all_gather(mine, ('yhi', 'ylo'), axis=0, tiled=True)  14 us
    ppermute x1, waiting for transfers between devices, body(): other = lax.ppermute(slot_rows, 'ylo', [(0, 1), (1, 0)])  12.6 us
    all_to_all x3, waiting for transfers between devices, send(): lax.all_to_all(computed, PLANE, split_axis=0, concat_axis=0, tiled=True)  10.2 us
    unnamed x29, local copies, waits for them, and re-layouts  10.1 us
  transfers between devices with their start and end apart: 17, of which 7 were waited for; matrix products, arithmetic and copies ran while one was open for 1% of the time, Pallas kernels for 10%

profile of v2, /device:TPU:1, one launch (start us, length us, event | category | flops | bytes accessed | tf_op | source)
XLA Modules:
  0.0 173.9 jit_solution(4924408997371776056)
XLA Ops:
  7.2 4.8 %collective-permute-start = (bf16[320,1536]{1,0:T(8,128)(2,1)}, bf16[320,1536]{1,0:T(8,128)(2,1)}, u32[]{:S(2)}, u32[]{:S(2)}) collective-permute-start(bf16[320,1536]{1,0:T(8,128)(2,1)} %bitcast.11), channel_id=1, source_target_pairs={{0,32},{32,64},{64,96},{96,128},{128,160},{160,192},{192,224},{224... | collective-permute-start | bytes 2949128 | tf_op jit(solution)/shard_map/ppermute | solution.py:260
  12.0 8.6 %collective-permute-start.3 = (bf16[320,1536]{1,0:T(8,128)(2,1)}, bf16[320,1536]{1,0:T(8,128)(2,1)}, u32[]{:S(2)}, u32[]{:S(2)}) collective-permute-start(bf16[320,1536]{1,0:T(8,128)(2,1)} %bitcast.12), channel_id=1, source_target_pairs={{0,224},{32,0},{64,32},{96,64},{128,96},{160,128},{192,160},{224,1... | collective-permute-start | bytes 2949128 | tf_op jit(solution)/shard_map/ppermute | solution.py:261
  21.5 1.3 copy-done.4
  22.8 1.8 %shard_map.87 = f32[2560,128]{1,0:T(8,128)} custom-call(bf16[128,5120]{1,0:T(8,128)(2,1)S(1)} %copy-done.4, bf16[128,64]{1,0:T(8,128)(2,1)S(1)} %copy.11.refs_1_.refs_2_), custom_call_target="tpu_custom_call" | custom-call | flops 83886080 | bytes 3000000 | tf_op jit(solution)/shard_map/pallas_call | solution.py:38
  24.6 3.2 %collective-permute-start.1 = (bf16[192,1536]{1,0:T(8,128)(2,1)S(1)}, bf16[192,1536]{1,0:T(8,128)(2,1)S(1)}, u32[]{:S(2)}, u32[]{:S(2)}) collective-permute-start(bf16[192,1536]{1,0:T(8,128)(2,1)S(1)} %bitcast.9), channel_id=1, source_target_pairs={{0,256},{256,0},{1,257},{257,1},{2,258},{258,2},{3,259},{259,3},{4... | collective-permute-start | bytes 1769480 | tf_op jit(solution)/shard_map/ppermute | solution.py:230
  27.9 12.6 %collective-permute-done.1.refs_2_ = bf16[192,1536]{1,0:T(8,128)(2,1)S(1)} collective-permute-done((bf16[192,1536]{1,0:T(8,128)(2,1)S(1)}, bf16[192,1536]{1,0:T(8,128)(2,1)S(1)}, u32[]{:S(2)}, u32[]{:S(2)}) %collective-permute-start.1) | collective-permute-done | bytes 589856 | tf_op jit(solution)/shard_map/ppermute | solution.py:230
  40.5 1.9 %collective-permute-start.2 = (bf16[320,1536]{1,0:T(8,128)(2,1)}, bf16[320,1536]{1,0:T(8,128)(2,1)}, u32[]{:S(2)}, u32[]{:S(2)}) collective-permute-start(bf16[320,1536]{1,0:T(8,128)(2,1)} %collective-permute-done.refs_2_), channel_id=1, source_target_pairs={{0,32},{32,64},{64,96},{96,128},{128,160},{160,192},{192,224},{224... | collective-permute-start | bytes 2949128 | tf_op jit(solution)/shard_map/ppermute | solution.py:265
  43.0 4.6 %collective-permute-start.5 = (bf16[320,1536]{1,0:T(8,128)(2,1)}, bf16[320,1536]{1,0:T(8,128)(2,1)}, u32[]{:S(2)}, u32[]{:S(2)}) collective-permute-start(bf16[320,1536]{1,0:T(8,128)(2,1)} %collective-permute-done.3.refs_3_), channel_id=1, source_target_pairs={{0,224},{32,0},{64,32},{96,64},{128,96},{160,128},{192,160},{224,1... | collective-permute-start | bytes 2949128 | tf_op jit(solution)/shard_map/ppermute | solution.py:266
  47.6 5.1 %shard_map.89 = bf16[64,48,128]{2,1,0:T(8,128)(2,1)} custom-call(bf16[512,1536]{1,0:T(8,128)(2,1)S(1)} %bitcast.6, bf16[320,1536]{1,0:T(8,128)(2,1)S(1)} %bitcast.13, bf16[320,1536]{1,0:T(8,128)(2,1)} %collective-permute-done.refs_2_, bf16[320,1536]{1,0:T(8,128)(2,1)} %collective-permute-done.3.refs_3_), custom_call_target="tpu_custom_call" | custom-call | flops 24999999488 | bytes 4000000 | tf_op jit(solution)/shard_map/pallas_call | solution.py:38
  52.7 12.5 %all-to-all-start = ((bf16[64,48,128]{2,1,0:T(8,128)(2,1)}), bf16[64,48,128]{2,1,0:T(8,128)(2,1)S(1)}, u32[]{:S(2)}, u32[]{:S(2)}) async-start(bf16[64,48,128]{2,1,0:T(8,128)(2,1)} %shard_map.89), calls=%async_computation.1 | async-start | bytes 1572864 | tf_op jit(solution)/shard_map/all_to_all | solution.py:256
  65.2 1.7 collective-permute-done.5.refs_2_
  66.9 5.3 %collective-permute-start.6 = (bf16[320,1536]{1,0:T(8,128)(2,1)}, bf16[320,1536]{1,0:T(8,128)(2,1)S(1)}, u32[]{:S(2)}, u32[]{:S(2)}) collective-permute-start(bf16[320,1536]{1,0:T(8,128)(2,1)} %collective-permute-done.5.refs_2_), channel_id=1, source_target_pairs={{0,224},{32,0},{64,32},{96,64},{128,96},{160,128},{192,160},{224,1... | collective-permute-start | bytes 2949128 | tf_op jit(solution)/shard_map/ppermute | solution.py:270
  72.3 1.9 %collective-permute-start.4 = (bf16[320,1536]{1,0:T(8,128)(2,1)}, bf16[320,1536]{1,0:T(8,128)(2,1)}, u32[]{:S(2)}, u32[]{:S(2)}) collective-permute-start(bf16[320,1536]{1,0:T(8,128)(2,1)} %collective-permute-done.2.refs_1_), channel_id=1, source_target_pairs={{0,32},{32,64},{64,96},{96,128},{128,160},{160,192},{192,224},{224... | collective-permute-start | bytes 2949128 | tf_op jit(solution)/shard_map/ppermute | solution.py:269
  74.2 4.3 %shard_map.90.refs_2_ = bf16[64,32,128]{2,1,0:T(8,128)(2,1)} custom-call(bf16[512,1536]{1,0:T(8,128)(2,1)S(1)} %bitcast.7, bf16[320,1536]{1,0:T(8,128)(2,1)} %collective-permute-done.2.refs_1_, bf16[320,1536]{1,0:T(8,128)(2,1)} %collective-permute-done.5.refs_2_), custom_call_target="tpu_custom_call" | custom-call | flops 24999999488 | bytes 4000000 | tf_op jit(solution)/shard_map/pallas_call | solution.py:38
  78.5 10.2 %all-to-all-done.refs_3_.refs_4_ = bf16[64,48,128]{2,1,0:T(8,128)(2,1)S(1)} async-done(((bf16[64,48,128]{2,1,0:T(8,128)(2,1)}), bf16[64,48,128]{2,1,0:T(8,128)(2,1)S(1)}, u32[]{:S(2)}, u32[]{:S(2)}) %all-to-all-start) | async-done | bytes 786464 | tf_op jit(solution)/shard_map/all_to_all | solution.py:256
  88.7 5.8 %all-to-all-start.1 = ((bf16[64,32,128]{2,1,0:T(8,128)(2,1)}), bf16[64,32,128]{2,1,0:T(8,128)(2,1)S(1)}, u32[]{:S(2)}, u32[]{:S(2)}) async-start(bf16[64,32,128]{2,1,0:T(8,128)(2,1)} %shard_map.90.refs_2_), calls=%async_computation.2 | async-start | bytes 1048576 | tf_op jit(solution)/shard_map/all_to_all | solution.py:256
  95.7 2.3 %shard_map.91 = (bf16[160,1536]{1,0:T(8,128)(2,1)}, bf16[160,1536]{1,0:T(8,128)(2,1)}) custom-call(bf16[320,1536]{1,0:T(8,128)(2,1)} %collective-permute-done.4.refs_0_.refs_1_, bf16[320,1536]{1,0:T(8,128)(2,1)S(1)} %collective-permute-done.6.refs_1_.refs_2_, bf16[64,32,128]{2,1,0:T(8,128)(2,1)} %shard_map.90.refs_2_, ...), custom_call_target="tpu_custom_call" | custom-call | bytes 3000000 | tf_op jit(solution)/shard_map/pallas_call | solution.py:38
  98.0 1.9 %collective-permute-start.7 = (bf16[160,1536]{1,0:T(8,128)(2,1)}, bf16[160,1536]{1,0:T(8,128)(2,1)S(1)}, u32[]{:S(2)}, u32[]{:S(2)}) collective-permute-start(bf16[160,1536]{1,0:T(8,128)(2,1)} %get-tuple-element.15), channel_id=1, source_target_pairs={{0,32},{32,64},{64,96},{96,128},{128,160},{160,192},{192,224},{224... | collective-permute-start | bytes 1474568 | tf_op jit(solution)/shard_map/ppermute | solution.py:281
  99.9 4.6 %collective-permute-start.8 = (bf16[160,1536]{1,0:T(8,128)(2,1)}, bf16[160,1536]{1,0:T(8,128)(2,1)}, u32[]{:S(2)}, u32[]{:S(2)}) collective-permute-start(bf16[160,1536]{1,0:T(8,128)(2,1)} %get-tuple-element.16), channel_id=1, source_target_pairs={{0,224},{32,0},{64,32},{96,64},{128,96},{160,128},{192,160},{224,1... | collective-permute-start | bytes 1474568 | tf_op jit(solution)/shard_map/ppermute | solution.py:282
  104.5 14.0 %all-gather.2.cloned.1.call-done = f32[2560,128]{1,0:T(8,128)} async-done(((f32[320,128]{1,0:T(8,128)}), f32[2560,128]{1,0:T(8,128)}) %all-gather.2.cloned.1.call-update) | async-done | bytes 1310736 | tf_op jit(solution)/shard_map/all_gather | solution.py:284
  120.3 1.4 copy-done.3
  122.8 4.1 %shard_map.92 = bf16[64,48,128]{2,1,0:T(8,128)(2,1)S(1)} custom-call(bf16[512,1536]{1,0:T(8,128)(2,1)S(1)} %bitcast.8, bf16[320,1536]{1,0:T(8,128)(2,1)} %collective-permute-done.4.refs_0_.refs_1_, bf16[320,1536]{1,0:T(8,128)(2,1)S(1)} %collective-permute-done.6.refs_1_.refs_2_, bf16[160,1536]{1,0:T(8,128)(2,1)S(1)} %copy-done.10, ...), custom_call_target="tpu_custom_call" | custom-call | flops 15000000512 | bytes 4000000 | tf_op jit(solution)/shard_map/pallas_call | solution.py:38
  127.8 11.7 %all-to-all-start.2 = ((bf16[64,48,128]{2,1,0:T(8,128)(2,1)}), bf16[64,48,128]{2,1,0:T(8,128)(2,1)S(1)}, u32[]{:S(2)}, u32[]{:S(2)}) async-start(bf16[64,48,128]{2,1,0:T(8,128)(2,1)} %copy-done.5), calls=%async_computation.3 | async-start | bytes 1572864 | tf_op jit(solution)/shard_map/all_to_all | solution.py:256
  139.4 3.2 %collective-permute-start.9 = (f32[80,128]{1,0:T(8,128)S(1)}, f32[80,128]{1,0:T(8,128)S(1)}, u32[]{:S(2)}, u32[]{:S(2)}) collective-permute-start(f32[80,128]{1,0:T(8,128)S(1)} %dynamic-slice_reduce_fusion.refs_5_), channel_id=1, source_target_pairs={{0,32},{32,0},{64,96},{96,64},{128,160},{160,128},{192,224},{224,1... | collective-permute-start | bytes 122888 | tf_op jit(solution)/shard_map/ppermute | solution.py:292
  142.7 1.8 %collective-permute-done.9 = f32[80,128]{1,0:T(8,128)S(1)} collective-permute-done((f32[80,128]{1,0:T(8,128)S(1)}, f32[80,128]{1,0:T(8,128)S(1)}, u32[]{:S(2)}, u32[]{:S(2)}) %collective-permute-start.9) | collective-permute-done | bytes 40992 | tf_op jit(solution)/shard_map/ppermute | solution.py:292
  144.5 3.8 %collective-permute-start.10 = (f32[80,128]{1,0:T(8,128)S(1)}, f32[80,128]{1,0:T(8,128)S(1)}, u32[]{:S(2)}, u32[]{:S(2)}) collective-permute-start(f32[80,128]{1,0:T(8,128)S(1)} %add.16), channel_id=1, source_target_pairs={{0,64},{32,96},{64,0},{96,32},{128,192},{160,224},{192,128},{224,1... | collective-permute-start | bytes 122888 | tf_op jit(solution)/shard_map/ppermute | solution.py:292
  148.3 2.1 %collective-permute-done.10 = f32[80,128]{1,0:T(8,128)S(1)} collective-permute-done((f32[80,128]{1,0:T(8,128)S(1)}, f32[80,128]{1,0:T(8,128)S(1)}, u32[]{:S(2)}, u32[]{:S(2)}) %collective-permute-start.10) | collective-permute-done | bytes 40992 | tf_op jit(solution)/shard_map/ppermute | solution.py:292
  150.4 7.9 %collective-permute-start.11 = (f32[80,128]{1,0:T(8,128)S(1)}, f32[80,128]{1,0:T(8,128)S(1)}, u32[]{:S(2)}, u32[]{:S(2)}) collective-permute-start(f32[80,128]{1,0:T(8,128)S(1)} %add.17), channel_id=1, source_target_pairs={{0,128},{32,160},{64,192},{96,224},{128,0},{160,32},{192,64},{224,... | collective-permute-start | bytes 122888 | tf_op jit(solution)/shard_map/ppermute | solution.py:292
  160.2 1.6 shard_map.93
  161.9 1.2 copy-done
  163.8 1.4 copy-done.1
  165.2 1.8 %shard_map.94 = bf16[128,5120]{1,0:T(8,128)(2,1)} custom-call(s32[1]{0:T(128)} %bitcast.refs_0_, bf16[128,256]{1,0:T(8,128)(2,1)S(1)} %shard_map.86.refs_1_, bf16[64,48,128]{2,1,0:T(8,128)(2,1)S(1)} %all-to-all-done.2.refs_2_, bf16[2,8,128,320]{3,2,1,0:T(8,128)(2,1)S(1)} %copy-done.1, f32[2,3,128,320]{3,2,1,0:T(8,128)S(1)} %get-tuple-element.19.refs_4_), custom_call_target="tpu_custom_call" | custom-call | flops 40000000 | bytes 3000000 | tf_op jit(solution)/shard_map/pallas_call | solution.py:38
  (47 shorter events, 9.0 us)
Async XLA Ops:
  7.2 65.1 %reduce-scatter.2.cloned.1.call-start = ((), (), s32[]{:S(2)}) async-start(), calls=%async_computation.4 | async-start | bytes 1474560 | tf_op jit(solution)/shard_map/reduce_scatter | solution.py:227
  7.2 33.3 %collective-permute-start = (bf16[320,1536]{1,0:T(8,128)(2,1)}, bf16[320,1536]{1,0:T(8,128)(2,1)}, u32[]{:S(2)}, u32[]{:S(2)}) collective-permute-start(bf16[320,1536]{1,0:T(8,128)(2,1)} %bitcast.11), channel_id=1, source_target_pairs={{0,32},{32,64},{64,96},{96,128},{128,160},{160,192},{192,224},{224... | collective-permute-start | bytes 2949128 | tf_op jit(solution)/shard_map/ppermute | solution.py:260
  12.0 31.0 %collective-permute-start.3 = (bf16[320,1536]{1,0:T(8,128)(2,1)}, bf16[320,1536]{1,0:T(8,128)(2,1)}, u32[]{:S(2)}, u32[]{:S(2)}) collective-permute-start(bf16[320,1536]{1,0:T(8,128)(2,1)} %bitcast.12), channel_id=1, source_target_pairs={{0,224},{32,0},{64,32},{96,64},{128,96},{160,128},{192,160},{224,1... | collective-permute-start | bytes 2949128 | tf_op jit(solution)/shard_map/ppermute | solution.py:261
  21.5 1.3 copy-start.4
  22.8 1.8 %copy-start.7 = (bf16[1,192,1536]{2,1,0:T(8,128)(2,1)S(1)}, bf16[1,192,1536]{2,1,0:T(8,128)(2,1)}, u32[]{:S(2)}) copy-start(bf16[1,192,1536]{2,1,0:T(8,128)(2,1)} %param.9) | copy-start | bytes 1769476
  24.6 15.9 %collective-permute-start.1 = (bf16[192,1536]{1,0:T(8,128)(2,1)S(1)}, bf16[192,1536]{1,0:T(8,128)(2,1)S(1)}, u32[]{:S(2)}, u32[]{:S(2)}) collective-permute-start(bf16[192,1536]{1,0:T(8,128)(2,1)S(1)} %bitcast.9), channel_id=1, source_target_pairs={{0,256},{256,0},{1,257},{257,1},{2,258},{258,2},{3,259},{259,3},{4... | collective-permute-start | bytes 1769480 | tf_op jit(solution)/shard_map/ppermute | solution.py:230
  40.5 31.7 %collective-permute-start.2 = (bf16[320,1536]{1,0:T(8,128)(2,1)}, bf16[320,1536]{1,0:T(8,128)(2,1)}, u32[]{:S(2)}, u32[]{:S(2)}) collective-permute-start(bf16[320,1536]{1,0:T(8,128)(2,1)} %collective-permute-done.refs_2_), channel_id=1, source_target_pairs={{0,32},{32,64},{64,96},{96,128},{128,160},{160,192},{192,224},{224... | collective-permute-start | bytes 2949128 | tf_op jit(solution)/shard_map/ppermute | solution.py:265
  42.4 5.2 %copy-start.8 = (bf16[1,320,1536]{2,1,0:T(8,128)(2,1)S(1)}, bf16[1,320,1536]{2,1,0:T(8,128)(2,1)}, u32[]{:S(2)}) copy-start(bf16[1,320,1536]{2,1,0:T(8,128)(2,1)} %param.10) | copy-start | bytes 2949124
  43.0 31.2 %copy-start.2 = (bf16[2,256,1536]{2,1,0:T(8,128)(2,1)}, bf16[2,256,1536]{2,1,0:T(8,128)(2,1)S(1)}, u32[]{:S(2)}) copy-start(bf16[2,256,1536]{2,1,0:T(8,128)(2,1)S(1)} %shard_map.88) | copy-start | bytes 4718596
  43.0 23.9 %collective-permute-start.5 = (bf16[320,1536]{1,0:T(8,128)(2,1)}, bf16[320,1536]{1,0:T(8,128)(2,1)}, u32[]{:S(2)}, u32[]{:S(2)}) collective-permute-start(bf16[320,1536]{1,0:T(8,128)(2,1)} %collective-permute-done.3.refs_3_), channel_id=1, source_target_pairs={{0,224},{32,0},{64,32},{96,64},{128,96},{160,128},{192,160},{224,1... | collective-permute-start | bytes 2949128 | tf_op jit(solution)/shard_map/ppermute | solution.py:266
  52.7 36.0 %all-to-all-start = ((bf16[64,48,128]{2,1,0:T(8,128)(2,1)}), bf16[64,48,128]{2,1,0:T(8,128)(2,1)S(1)}, u32[]{:S(2)}, u32[]{:S(2)}) async-start(bf16[64,48,128]{2,1,0:T(8,128)(2,1)} %shard_map.89), calls=%async_computation.1 | async-start | bytes 1572864 | tf_op jit(solution)/shard_map/all_to_all | solution.py:256
  65.2 53.3 %all-gather.2.cloned.1.call-start = ((), (), s32[]{:S(2)}) async-start(), calls=%async_computation.5 | async-start | bytes 1474560 | tf_op jit(solution)/shard_map/all_gather | solution.py:284
  66.9 27.6 %collective-permute-start.6 = (bf16[320,1536]{1,0:T(8,128)(2,1)}, bf16[320,1536]{1,0:T(8,128)(2,1)S(1)}, u32[]{:S(2)}, u32[]{:S(2)}) collective-permute-start(bf16[320,1536]{1,0:T(8,128)(2,1)} %collective-permute-done.5.refs_2_), channel_id=1, source_target_pairs={{0,224},{32,0},{64,32},{96,64},{128,96},{160,128},{192,160},{224,1... | collective-permute-start | bytes 2949128 | tf_op jit(solution)/shard_map/ppermute | solution.py:270
  72.3 23.4 %collective-permute-start.4 = (bf16[320,1536]{1,0:T(8,128)(2,1)}, bf16[320,1536]{1,0:T(8,128)(2,1)}, u32[]{:S(2)}, u32[]{:S(2)}) collective-permute-start(bf16[320,1536]{1,0:T(8,128)(2,1)} %collective-permute-done.2.refs_1_), channel_id=1, source_target_pairs={{0,32},{32,64},{64,96},{96,128},{128,160},{160,192},{192,224},{224... | collective-permute-start | bytes 2949128 | tf_op jit(solution)/shard_map/ppermute | solution.py:269
  88.7 30.8 %all-to-all-start.1 = ((bf16[64,32,128]{2,1,0:T(8,128)(2,1)}), bf16[64,32,128]{2,1,0:T(8,128)(2,1)S(1)}, u32[]{:S(2)}, u32[]{:S(2)}) async-start(bf16[64,32,128]{2,1,0:T(8,128)(2,1)} %shard_map.90.refs_2_), calls=%async_computation.2 | async-start | bytes 1048576 | tf_op jit(solution)/shard_map/all_to_all | solution.py:256
  98.0 21.5 %collective-permute-start.7 = (bf16[160,1536]{1,0:T(8,128)(2,1)}, bf16[160,1536]{1,0:T(8,128)(2,1)S(1)}, u32[]{:S(2)}, u32[]{:S(2)}) collective-permute-start(bf16[160,1536]{1,0:T(8,128)(2,1)} %get-tuple-element.15), channel_id=1, source_target_pairs={{0,32},{32,64},{64,96},{96,128},{128,160},{160,192},{192,224},{224... | collective-permute-start | bytes 1474568 | tf_op jit(solution)/shard_map/ppermute | solution.py:281
  99.9 20.4 %collective-permute-start.8 = (bf16[160,1536]{1,0:T(8,128)(2,1)}, bf16[160,1536]{1,0:T(8,128)(2,1)}, u32[]{:S(2)}, u32[]{:S(2)}) collective-permute-start(bf16[160,1536]{1,0:T(8,128)(2,1)} %get-tuple-element.16), channel_id=1, source_target_pairs={{0,224},{32,0},{64,32},{96,64},{128,96},{160,128},{192,160},{224,1... | collective-permute-start | bytes 1474568 | tf_op jit(solution)/shard_map/ppermute | solution.py:282
  119.5 0.8 copy-start.9
  120.3 1.4 copy-start.3
  121.7 1.0 copy-start.10
  126.9 0.9 copy-start.5
  127.8 30.6 %copy-start.11 = (f32[128,6]{0,1:T(8,128)S(1)}, f32[128,6]{0,1:T(8,128)}, u32[]{:S(2)}) copy-start(f32[128,6]{0,1:T(8,128)} %param.8) | copy-start | bytes 9220
  127.8 30.7 %copy-start.12 = (s32[128,6]{0,1:T(8,128)S(1)}, s32[128,6]{0,1:T(8,128)}, u32[]{:S(2)}) copy-start(s32[128,6]{0,1:T(8,128)} %param.7) | copy-start | bytes 9220
  127.8 36.0 %all-to-all-start.2 = ((bf16[64,48,128]{2,1,0:T(8,128)(2,1)}), bf16[64,48,128]{2,1,0:T(8,128)(2,1)S(1)}, u32[]{:S(2)}, u32[]{:S(2)}) async-start(bf16[64,48,128]{2,1,0:T(8,128)(2,1)} %copy-done.5), calls=%async_computation.3 | async-start | bytes 1572864 | tf_op jit(solution)/shard_map/all_to_all | solution.py:256
  139.4 5.0 %collective-permute-start.9 = (f32[80,128]{1,0:T(8,128)S(1)}, f32[80,128]{1,0:T(8,128)S(1)}, u32[]{:S(2)}, u32[]{:S(2)}) collective-permute-start(f32[80,128]{1,0:T(8,128)S(1)} %dynamic-slice_reduce_fusion.refs_5_), channel_id=1, source_target_pairs={{0,32},{32,0},{64,96},{96,64},{128,160},{160,128},{192,224},{224,1... | collective-permute-start | bytes 122888 | tf_op jit(solution)/shard_map/ppermute | solution.py:292
  144.5 5.9 %collective-permute-start.10 = (f32[80,128]{1,0:T(8,128)S(1)}, f32[80,128]{1,0:T(8,128)S(1)}, u32[]{:S(2)}, u32[]{:S(2)}) collective-permute-start(f32[80,128]{1,0:T(8,128)S(1)} %add.16), channel_id=1, source_target_pairs={{0,64},{32,96},{64,0},{96,32},{128,192},{160,224},{192,128},{224,1... | collective-permute-start | bytes 122888 | tf_op jit(solution)/shard_map/ppermute | solution.py:292
  150.4 12.6 %collective-permute-start.11 = (f32[80,128]{1,0:T(8,128)S(1)}, f32[80,128]{1,0:T(8,128)S(1)}, u32[]{:S(2)}, u32[]{:S(2)}) collective-permute-start(f32[80,128]{1,0:T(8,128)S(1)} %add.17), channel_id=1, source_target_pairs={{0,128},{32,160},{64,192},{96,224},{128,0},{160,32},{192,64},{224,... | collective-permute-start | bytes 122888 | tf_op jit(solution)/shard_map/ppermute | solution.py:292
  159.1 1.1 copy-start.6
  161.9 1.2 copy-start
  163.8 1.4 copy-start.1
Sparse Core Ops, SparseCore 0:
  28.0 34.9 reduce-scatter.1
  72.4 46.0 all-gather.1

commit v3 on v2

--- a/solution.py
+++ b/solution.py
@@ -32,7 +32,7 @@
         in_specs=list(in_specs) + [pl.BlockSpec(memory_space=pl.ANY)] * len(after),
         out_specs=jax.tree.map(lambda _: VMEM, out_shape),
         scratch_shapes=list(scratch),
-        compiler_params=pltpu.CompilerParams(vmem_limit_bytes=32 * 1024 * 1024),
+        compiler_params=pltpu.CompilerParams(vmem_limit_bytes=16 * 1024 * 1024),
         cost_estimate=pl.CostEstimate(flops=flops, bytes_accessed=moved, transcendentals=0),
     )
     return lambda *args: run(*args, *after)
@@ -42,20 +42,27 @@
     return jax.ShapeDtypeStruct(shape, dtype)
 
 
-def partial_kernel(order, normed_ref, key_ref, out_ref):
+def partial_kernel(places, core_ref, normed_ref, key_ref, other_normed_ref, other_key_ref, out_ref):
+    dims = (((0,), (0,)), ((), ()))
     product = lax.dot_general(
-        key_ref[...], normed_ref[...], (((0,), (0,)), ((), ())), preferred_element_type=jnp.float32
+        key_ref[...], normed_ref[...], dims, preferred_element_type=jnp.float32
+    ) + lax.dot_general(
+        other_key_ref[...], other_normed_ref[...], dims, preferred_element_type=jnp.float32
     )
     key, width = product.shape
-    share = width // len(order)
+    share = width // (2 * len(places))
     rest = share - 128
     group = key * rest // 128
-    rows = key + group
-    for e, place in enumerate(order):
-        out_ref[place * rows : place * rows + key, :] = product[:, e * share : e * share + 128]
-        tail = product[:, e * share + 128 : (e + 1) * share]
-        out_ref[place * rows + key : (place + 1) * rows, :] = jnp.concatenate(
-            [tail[a * group : (a + 1) * group] for a in range(key // group)], axis=1
+    first = core_ref[0] == 0
+    for place, (low, high) in enumerate(places):
+        part = jnp.where(
+            first,
+            product[:, low * share : (low + 1) * share],
+            product[:, high * share : (high + 1) * share],
+        )
+        out_ref[place, :key, :] = part[:, :128]
+        out_ref[place, key:, :] = jnp.concatenate(
+            [part[a * group : (a + 1) * group, 128:] for a in range(key // group)], axis=1
         )
 
 
@@ -101,9 +108,8 @@
         out_ref[g] = spaced.reshape(rows // capacity * PAD, depth)
 
 
-def products_kernel(capacity, rows_ref, *refs):
-    weights, (out_ref, lines_ref) = refs[:-2], refs[-2:]
-    targets, lines, lanes = out_ref.shape
+def put_lines(capacity, rows_ref, weights, lines_ref, start, end):
+    targets, _, lanes = lines_ref.shape
     products = [
         lax.dot_general(
             rows_ref[...], ref[...], (((1,), (1,)), ((), ())), preferred_element_type=jnp.float32
@@ -116,13 +122,17 @@
         products.append(jnp.zeros((targets * PAD, blocks * lanes - width), jnp.float32))
     product = jnp.concatenate(products, axis=1).reshape(targets, PAD, blocks * lanes)
     for j in range(blocks):
-        lines_ref[:, j * capacity : (j + 1) * capacity, :] = product[
+        lines_ref[:, start + j * capacity : start + (j + 1) * capacity, :] = product[
             :, :capacity, j * lanes : (j + 1) * lanes
         ]
-    if lines > blocks * capacity:
-        lines_ref[:, blocks * capacity :, :] = jnp.zeros(
-            (targets, lines - blocks * capacity, lanes), jnp.float32
-        )
+    done = start + blocks * capacity
+    if end > done:
+        lines_ref[:, done:end, :] = jnp.zeros((targets, end - done, lanes), jnp.float32)
+
+
+def products_kernel(capacity, rows_ref, *refs):
+    weights, (out_ref, lines_ref) = refs[:-2], refs[-2:]
+    put_lines(capacity, rows_ref, weights, lines_ref, 0, out_ref.shape[1])
     out_ref[...] = lines_ref[...].astype(out_ref.dtype)
 
 
@@ -141,6 +151,15 @@
         jnp.dot(combine, rows[g * half : (g + 1) * half], preferred_element_type=jnp.float32)
         for g in range(rows.shape[0] // half)
     ]
+
+
+def more_products_kernel(capacity, rows_ref, begun_ref, *refs):
+    weights, (out_ref, lines_ref) = refs[:-2], refs[-2:]
+    targets, lines, lanes = out_ref.shape
+    held = begun_ref.shape[1] // capacity * capacity
+    lines_ref[:, : begun_ref.shape[1], :] = begun_ref[...].astype(jnp.float32)
+    put_lines(capacity, rows_ref, weights, lines_ref, held, lines)
+    out_ref[...] = lines_ref[...].astype(out_ref.dtype)
 
 
 def halves_kernel(half, low_ref, high_ref, low_out, high_out):
@@ -212,22 +231,28 @@
     down = [(i, (i - 1) % ring) for i in range(ring)]
 
     packed = key_size * share // 128
-    columns, cores = lax.axis_size("yhi"), lax.axis_size("core")
-    order = tuple(
-        (e // (columns * cores) * cores + e % cores) * columns + e // cores % columns
-        for e in range(experts_here)
-    )
-    partial_grad = call(
-        functools.partial(partial_kernel, order),
-        struct((experts_here * packed, 128), jnp.float32),
-        [VMEM, VMEM],
-        2 * tokens * key_size * width,
-        3 * 10**6,
-    )(normed, key_grad)
-    mine = lax.psum_scatter(partial_grad, ("x", "core"), scatter_dimension=0, tiled=True)
-
-    slot_rows, partial_grad = lax.optimization_barrier((slot_rows, partial_grad))
-    other = lax.ppermute(slot_rows, "ylo", [(0, 1), (1, 0)])
+    cores = lax.axis_size("core")
+    places = tuple(
+        tuple(place * cores + core for core in range(cores)) for place in range(experts_here // cores)
+    )
+    swap = [(0, 1), (1, 0)]
+    mine = call(
+        functools.partial(partial_kernel, places),
+        struct((len(places), packed, 128), jnp.float32),
+        [SMEM] + [VMEM] * 4,
+        4 * tokens * key_size * width,
+        4 * 10**6,
+    )(
+        lax.axis_index("core").astype(jnp.int32).reshape(1),
+        normed,
+        key_grad,
+        lax.ppermute(normed, "core", swap),
+        lax.ppermute(key_grad, "core", swap),
+    )
+    terms = lax.all_to_all(mine, ("x", "yhi"), split_axis=0, concat_axis=0, tiled=True)
+    mine = jnp.sum(terms, axis=0)
+
+    other = lax.ppermute(slot_rows, "ylo", swap)
 
     def spaced_rows(other):
         return call(
@@ -252,6 +277,9 @@
             after,
         )(both, *weights)
 
+    def added(sums, bit):
+        return sums + lax.ppermute(sums, "z", [(i, i ^ bit) for i in range(ring)])
+
     def send(computed):
         return lax.all_to_all(computed, PLANE, split_axis=0, concat_axis=0, tiled=True)
 
@@ -259,12 +287,14 @@
     below, above = [projection], [projection]
     below.append(lax.ppermute(below[-1], "z", up))
     above.append(lax.ppermute(above[-1], "z", down))
-    below[1], other = lax.optimization_barrier((below[1], other))
+    below[1], above[1], other = lax.optimization_barrier((below[1], above[1], other))
     both = spaced_rows(other)
-    first = products([projection, below[1], above[1]], 25 * 10**9)
+    first = products([projection, below[1], above[1]], 2 * 10**9)
+    first, mine = lax.optimization_barrier((first, mine))
     below.append(lax.ppermute(below[-1], "z", up))
     above.append(lax.ppermute(above[-1], "z", down))
-    below[2], _, mine = lax.optimization_barrier((below[2], first, mine))
+    below[2], _ = lax.optimization_barrier((below[2], first))
+    above[2], _ = lax.optimization_barrier((above[2], first))
     second = products([below[2], above[2]], 25 * 10**9)
     below.append(lax.ppermute(below[-1], "z", up))
     above.append(lax.ppermute(above[-1], "z", down))
@@ -281,24 +311,19 @@
     last_low = lax.ppermute(half_low, "z", up)
     last_high = lax.ppermute(half_high, "z", down)
     sent.append(send(second))
-    terms = lax.all_gather(mine, ("yhi", "ylo"), axis=0, tiled=True)
-    terms = terms.reshape(columns * pairs, columns, packed, 128)
-    summed = jnp.sum(lax.dynamic_index_in_dim(terms, lax.axis_index("yhi"), 1, False), axis=0)
-    third = products([below[3], above[3], last_low, last_high], 15 * 10**9, [summed] + sent[1:])
+    two = added(added(mine, 1), 2)
+    begun = products([below[3], above[3]], 10 * 10**9)
+    shape = (pairs * experts_here, 48, 128)
+    third = call(
+        functools.partial(more_products_kernel, capacity),
+        struct(shape, jnp.bfloat16),
+        [VMEM] * 4,
+        1 * 10**9,
+        3 * 10**6,
+        [pltpu.VMEM(shape, jnp.float32)],
+        [two],
+    )(both, begun, last_low, last_high)
     chunks = sent + [send(third)]
-
-    bit = 1
-    while bit < ring:
-        summed = summed + lax.ppermute(summed, "z", [(i, i ^ bit) for i in range(ring)])
-        bit *= 2
-    scale_factor = (tokens * groups * experts_here) ** (-0.5)
-    rope_grad = call(
-        functools.partial(rope_kernel, key_size, share, scale_factor),
-        struct((key_size, share), jnp.float32),
-        [VMEM],
-        0,
-        10**6,
-    )(summed)
 
     combine = call(
         functools.partial(combine_kernel, experts_here, capacity),
@@ -320,6 +345,17 @@
         8 * 10**6,
         [pltpu.VMEM((groups, tokens, piece), jnp.float32), lines],
     )(z, combine, key_grad, rope_weight, *chunks[:-1])
+    summed = added(two, 4)
+    summed = summed + lax.ppermute(summed, "ylo", swap)
+    scale_factor = (tokens * groups * experts_here) ** (-0.5)
+    rope_grad = call(
+        functools.partial(rope_kernel, key_size, share, scale_factor),
+        struct((key_size, share), jnp.float32),
+        [VMEM],
+        0,
+        10**6,
+    )(summed)
+
     token_grad = call(
         functools.partial(late_kernel, capacity, layout[-1], sum(layout[:-1], ())),
         struct((tokens, width), jnp.bfloat16),

time: 176 us -> 160 us (0.909)
  between operations: 14.4 us -> 0.95 us
  waiting for transfers between devices: 43.7 us -> 37.2 us
  starting transfers between devices: 81.8 us -> 88.2 us
  local copies, waits for them, and re-layouts: 10.1 us -> 7.87 us
    all_gather x1 -> x0, waiting for transfers between devices: 14 us -> none  [body(): terms = lax.all_gather(mine, ('yhi', 'ylo'), axis=0, tiled=True)]
    all_to_all x0 -> x1, starting transfers between devices: none -> 8.67 us  [body(): lax.all_to_all(mine, ('x', 'yhi'), split_axis=0, concat_axis=0, tiled=True)]
    ppermute x3, starting transfers between devices: 18.5 us -> 11 us  [body(): above.append(lax.ppermute(above[-1], 'z', down))]
    ppermute x4 -> x7, starting transfers between devices: 18.2 us -> 25.5 us  [the longest x1 8.79 us: body(): lax.ppermute(normed, 'core', swap)]
    ppermute x3, waiting for transfers between devices: 1.17 us -> 6 us  [body(): below.append(lax.ppermute(below[-1], 'z', up))]
    ppermute x4 -> x7, waiting for transfers between devices: 16.5 us -> 12.7 us  [the longest x1 6.53 us: body(): summed = summed + lax.ppermute(summed, 'ylo', swap)]
    ppermute x1, waiting for transfers between devices: 0.01 us -> 3.76 us  [body(): last_low = lax.ppermute(half_low, 'z', up)]
    ppermute x1, waiting for transfers between devices: 0.01 us -> 3.68 us  [body(): last_high = lax.ppermute(half_high, 'z', down)]
  transfers between devices with their start and end apart: 17 -> 19, of which waited for: 7 -> 10; matrix products, arithmetic and copies ran while one was open for 1% -> 1% of each run, Pallas kernels for 10% -> 14%
where the time goes in v3:
time: 160 us; the launch traced here: 159 us
  starting transfers between devices  88.2 us (55%)
  waiting for transfers between devices  37.2 us (23%)
  Pallas kernels  23.5 us (15%)
  local copies, waits for them, and re-layouts  7.87 us (5%)
    all_to_all x3, starting transfers between devices, send(): lax.all_to_all(computed, PLANE, split_axis=0, concat_axis=0, tiled=True)  28.5 us
    pallas_call x11, Pallas kernels, call(): return lambda *args: run(*args, *after)  23.5 us
    ppermute x3, starting transfers between devices, body(): above.append(lax.ppermute(above[-1], 'z', down))  11 us
    all_to_all x3, waiting for transfers between devices, send(): lax.all_to_all(computed, PLANE, split_axis=0, concat_axis=0, tiled=True)  9.79 us
    ppermute x1, starting transfers between devices, body(): lax.ppermute(normed, 'core', swap)  8.79 us
    all_to_all x1, starting transfers between devices, body(): lax.all_to_all(mine, ('x', 'yhi'), split_axis=0, concat_axis=0, tiled=True)  8.67 us
    ppermute x3, starting transfers between devices, body(): below.append(lax.ppermute(below[-1], 'z', up))  7.96 us
    unnamed x23, local copies, waits for them, and re-layouts  7.87 us
  transfers between devices with their start and end apart: 19, of which 10 were waited for; matrix products, arithmetic and copies ran while one was open for 1% of the time, Pallas kernels for 14%

profile of v3, /device:TPU:1, one launch (start us, length us, event | category | flops | bytes accessed | tf_op | source)
XLA Modules:
  0.0 158.9 jit_solution(1092840692516816538)
XLA Ops:
  0.6 8.8 %collective-permute-start.4 = (bf16[128,5120]{1,0:T(8,128)(2,1)}, bf16[128,5120]{1,0:T(8,128)(2,1)S(1)}, u32[]{:S(2)}, u32[]{:S(2)}) collective-permute-start(bf16[128,5120]{1,0:T(8,128)(2,1)} %refs_1_.2), channel_id=1, source_target_pairs={{0,1},{1,0},{2,3},{3,2},{4,5},{5,4},{6,7},{7,6},{8,9},{9,8},{10,11... | collective-permute-start | bytes 3932168 | tf_op jit(solution)/shard_map/ppermute | solution.py:249
  9.4 5.3 %collective-permute-start.1 = (bf16[320,1536]{1,0:T(8,128)(2,1)}, bf16[320,1536]{1,0:T(8,128)(2,1)}, u32[]{:S(2)}, u32[]{:S(2)}) collective-permute-start(bf16[320,1536]{1,0:T(8,128)(2,1)} %bitcast.12), channel_id=1, source_target_pairs={{0,224},{32,0},{64,32},{96,64},{128,96},{160,128},{192,160},{224,1... | collective-permute-start | bytes 2949128 | tf_op jit(solution)/shard_map/ppermute | solution.py:289
  14.7 1.9 %collective-permute-start = (bf16[320,1536]{1,0:T(8,128)(2,1)}, bf16[320,1536]{1,0:T(8,128)(2,1)}, u32[]{:S(2)}, u32[]{:S(2)}) collective-permute-start(bf16[320,1536]{1,0:T(8,128)(2,1)} %bitcast.13), channel_id=1, source_target_pairs={{0,32},{32,64},{64,96},{96,128},{128,160},{160,192},{192,224},{224... | collective-permute-start | bytes 2949128 | tf_op jit(solution)/shard_map/ppermute | solution.py:288
  16.7 3.2 %collective-permute-start.2 = (bf16[192,1536]{1,0:T(8,128)(2,1)}, bf16[192,1536]{1,0:T(8,128)(2,1)S(1)}, u32[]{:S(2)}, u32[]{:S(2)}) collective-permute-start(bf16[192,1536]{1,0:T(8,128)(2,1)} %bitcast.10), channel_id=1, source_target_pairs={{0,256},{256,0},{1,257},{257,1},{2,258},{258,2},{3,259},{259,3},{4... | collective-permute-start | bytes 1769480 | tf_op jit(solution)/shard_map/ppermute | solution.py:255
  20.7 2.5 %collective-permute-start.5 = (bf16[128,64]{1,0:T(8,128)(2,1)S(1)}, bf16[128,64]{1,0:T(8,128)(2,1)S(1)}, u32[]{:S(2)}, u32[]{:S(2)}) collective-permute-start(bf16[128,64]{1,0:T(8,128)(2,1)S(1)} %copy.12.refs_2_), channel_id=1, source_target_pairs={{0,1},{1,0},{2,3},{3,2},{4,5},{5,4},{6,7},{7,6},{8,9},{9,8},{10,11... | collective-permute-start | bytes 49160 | tf_op jit(solution)/shard_map/ppermute | solution.py:250
  25.4 1.8 %shard_map.89 = f32[16,80,128]{2,1,0:T(8,128)} custom-call(s32[1]{0:T(128)} %bitcast.5.refs_0_, bf16[128,5120]{1,0:T(8,128)(2,1)S(1)} %copy-done.2, bf16[128,64]{1,0:T(8,128)(2,1)S(1)} %copy.12.refs_2_, bf16[128,5120]{1,0:T(8,128)(2,1)S(1)} %collective-permute-done.4.refs_3_, bf16[128,64]{1,0:T(8,128)(2,1)S(1)} %collective-permute-done.5.refs_4_), custom_call_target="tpu_custom_call" | custom-call | flops 167772160 | bytes 4000000 | tf_op jit(solution)/shard_map/pallas_call | solution.py:38
  27.1 8.7 %all-to-all-start = ((f32[16,80,128]{2,1,0:T(8,128)}), f32[16,80,128]{2,1,0:T(8,128)}, u32[]{:S(2)}, u32[]{:S(2)}) async-start(f32[16,80,128]{2,1,0:T(8,128)} %shard_map.89), calls=%async_computation | async-start | bytes 1310720 | tf_op jit(solution)/shard_map/all_to_all | solution.py:252
  36.2 5.0 %collective-permute-done.refs_2_ = bf16[320,1536]{1,0:T(8,128)(2,1)} collective-permute-done((bf16[320,1536]{1,0:T(8,128)(2,1)}, bf16[320,1536]{1,0:T(8,128)(2,1)}, u32[]{:S(2)}, u32[]{:S(2)}) %collective-permute-start) | collective-permute-done | bytes 983072 | tf_op jit(solution)/shard_map/ppermute | solution.py:288
  41.2 1.9 %collective-permute-start.7 = (bf16[320,1536]{1,0:T(8,128)(2,1)}, bf16[320,1536]{1,0:T(8,128)(2,1)}, u32[]{:S(2)}, u32[]{:S(2)}) collective-permute-start(bf16[320,1536]{1,0:T(8,128)(2,1)} %collective-permute-done.1.refs_3_), channel_id=1, source_target_pairs={{0,224},{32,0},{64,32},{96,64},{128,96},{160,128},{192,160},{224,1... | collective-permute-start | bytes 2949128 | tf_op jit(solution)/shard_map/ppermute | solution.py:295
  43.1 3.4 %collective-permute-start.3 = (bf16[320,1536]{1,0:T(8,128)(2,1)}, bf16[320,1536]{1,0:T(8,128)(2,1)}, u32[]{:S(2)}, u32[]{:S(2)}) collective-permute-start(bf16[320,1536]{1,0:T(8,128)(2,1)} %collective-permute-done.refs_2_), channel_id=1, source_target_pairs={{0,32},{32,64},{64,96},{96,128},{128,160},{160,192},{192,224},{224... | collective-permute-start | bytes 2949128 | tf_op jit(solution)/shard_map/ppermute | solution.py:294
  47.7 5.1 %shard_map.88 = bf16[64,48,128]{2,1,0:T(8,128)(2,1)} custom-call(bf16[512,1536]{1,0:T(8,128)(2,1)S(1)} %bitcast.6, bf16[320,1536]{1,0:T(8,128)(2,1)S(1)} %bitcast.14, bf16[320,1536]{1,0:T(8,128)(2,1)} %collective-permute-done.refs_2_, bf16[320,1536]{1,0:T(8,128)(2,1)} %collective-permute-done.1.refs_3_), custom_call_target="tpu_custom_call" | custom-call | flops 2000000000 | bytes 4000000 | tf_op jit(solution)/shard_map/pallas_call | solution.py:38
  54.9 1.9 %collective-permute-start.11 = (f32[80,128]{1,0:T(8,128)S(1)}, f32[80,128]{1,0:T(8,128)S(1)}, u32[]{:S(2)}, u32[]{:S(2)}) collective-permute-start(f32[80,128]{1,0:T(8,128)S(1)} %reduce_sum.9), channel_id=1, source_target_pairs={{0,32},{32,0},{64,96},{96,64},{128,160},{160,128},{192,224},{224,1... | collective-permute-start | bytes 122888 | tf_op jit(solution)/shard_map/ppermute | solution.py:281
  56.8 10.9 %all-to-all-start.1 = ((bf16[64,48,128]{2,1,0:T(8,128)(2,1)}), bf16[64,48,128]{2,1,0:T(8,128)(2,1)S(1)}, u32[]{:S(2)}, u32[]{:S(2)}) async-start(bf16[64,48,128]{2,1,0:T(8,128)(2,1)} %shard_map.88), calls=%async_computation.1 | async-start | bytes 1572864 | tf_op jit(solution)/shard_map/all_to_all | solution.py:284
  68.7 2.7 %collective-permute-start.6 = (bf16[320,1536]{1,0:T(8,128)(2,1)}, bf16[320,1536]{1,0:T(8,128)(2,1)}, u32[]{:S(2)}, u32[]{:S(2)}) collective-permute-start(bf16[320,1536]{1,0:T(8,128)(2,1)} %collective-permute-done.3.refs_1_), channel_id=1, source_target_pairs={{0,32},{32,64},{64,96},{96,128},{128,160},{160,192},{192,224},{224... | collective-permute-start | bytes 2949128 | tf_op jit(solution)/shard_map/ppermute | solution.py:299
  71.4 3.8 %collective-permute-start.8 = (bf16[320,1536]{1,0:T(8,128)(2,1)}, bf16[320,1536]{1,0:T(8,128)(2,1)}, u32[]{:S(2)}, u32[]{:S(2)}) collective-permute-start(bf16[320,1536]{1,0:T(8,128)(2,1)} %collective-permute-done.7.refs_2_), channel_id=1, source_target_pairs={{0,224},{32,0},{64,32},{96,64},{128,96},{160,128},{192,160},{224,1... | collective-permute-start | bytes 2949128 | tf_op jit(solution)/shard_map/ppermute | solution.py:300
  75.2 1.9 %collective-permute-start.12 = (f32[80,128]{1,0:T(8,128)S(1)}, f32[80,128]{1,0:T(8,128)S(1)}, u32[]{:S(2)}, u32[]{:S(2)}) collective-permute-start(f32[80,128]{1,0:T(8,128)S(1)} %add.12), channel_id=1, source_target_pairs={{0,64},{32,96},{64,0},{96,32},{128,192},{160,224},{192,128},{224,1... | collective-permute-start | bytes 122888 | tf_op jit(solution)/shard_map/ppermute | solution.py:281
  77.1 4.3 %shard_map.91.refs_2_ = bf16[64,32,128]{2,1,0:T(8,128)(2,1)} custom-call(bf16[512,1536]{1,0:T(8,128)(2,1)S(1)} %bitcast.7, bf16[320,1536]{1,0:T(8,128)(2,1)} %collective-permute-done.3.refs_1_, bf16[320,1536]{1,0:T(8,128)(2,1)} %collective-permute-done.7.refs_2_), custom_call_target="tpu_custom_call" | custom-call | flops 24999999488 | bytes 4000000 | tf_op jit(solution)/shard_map/pallas_call | solution.py:38
  81.4 9.8 %all-to-all-done.1.refs_3_.refs_4_ = bf16[64,48,128]{2,1,0:T(8,128)(2,1)S(1)} async-done(((bf16[64,48,128]{2,1,0:T(8,128)(2,1)}), bf16[64,48,128]{2,1,0:T(8,128)(2,1)S(1)}, u32[]{:S(2)}, u32[]{:S(2)}) %all-to-all-start.1) | async-done | bytes 786464 | tf_op jit(solution)/shard_map/all_to_all | solution.py:284
  91.2 5.8 %all-to-all-start.3 = ((bf16[64,32,128]{2,1,0:T(8,128)(2,1)}), bf16[64,32,128]{2,1,0:T(8,128)(2,1)S(1)}, u32[]{:S(2)}, u32[]{:S(2)}) async-start(bf16[64,32,128]{2,1,0:T(8,128)(2,1)} %shard_map.91.refs_2_), calls=%async_computation.3 | async-start | bytes 1048576 | tf_op jit(solution)/shard_map/all_to_all | solution.py:284
  98.7 3.6 %collective-permute-start.9 = (bf16[160,1536]{1,0:T(8,128)(2,1)S(1)}, bf16[160,1536]{1,0:T(8,128)(2,1)S(1)}, u32[]{:S(2)}, u32[]{:S(2)}) collective-permute-start(bf16[160,1536]{1,0:T(8,128)(2,1)S(1)} %get-tuple-element.19), channel_id=1, source_target_pairs={{0,32},{32,64},{64,96},{96,128},{128,160},{160,192},{192,224},{224... | collective-permute-start | bytes 1474568 | tf_op jit(solution)/shard_map/ppermute | solution.py:311
  102.3 2.9 %collective-permute-start.10 = (bf16[160,1536]{1,0:T(8,128)(2,1)S(1)}, bf16[160,1536]{1,0:T(8,128)(2,1)S(1)}, u32[]{:S(2)}, u32[]{:S(2)}) collective-permute-start(bf16[160,1536]{1,0:T(8,128)(2,1)S(1)} %get-tuple-element.20), channel_id=1, source_target_pairs={{0,224},{32,0},{64,32},{96,64},{128,96},{160,128},{192,160},{224,1... | collective-permute-start | bytes 1474568 | tf_op jit(solution)/shard_map/ppermute | solution.py:312
  105.2 3.5 %shard_map.90.refs_1_ = bf16[64,32,128]{2,1,0:T(8,128)(2,1)S(1)} custom-call(bf16[512,1536]{1,0:T(8,128)(2,1)S(1)} %bitcast.8, bf16[320,1536]{1,0:T(8,128)(2,1)} %collective-permute-done.6.refs_1_.refs_0_, bf16[320,1536]{1,0:T(8,128)(2,1)} %collective-permute-done.8.refs_2_.refs_1_), custom_call_target="tpu_custom_call" | custom-call | flops 10000000000 | bytes 4000000 | tf_op jit(solution)/shard_map/pallas_call | solution.py:38
  108.7 3.8 %collective-permute-done.9.refs_2_ = bf16[160,1536]{1,0:T(8,128)(2,1)S(1)} collective-permute-done((bf16[160,1536]{1,0:T(8,128)(2,1)S(1)}, bf16[160,1536]{1,0:T(8,128)(2,1)S(1)}, u32[]{:S(2)}, u32[]{:S(2)}) %collective-permute-start.9) | collective-permute-done | bytes 491552 | tf_op jit(solution)/shard_map/ppermute | solution.py:311
  112.4 3.7 %collective-permute-done.10.refs_3_ = bf16[160,1536]{1,0:T(8,128)(2,1)S(1)} collective-permute-done((bf16[160,1536]{1,0:T(8,128)(2,1)S(1)}, bf16[160,1536]{1,0:T(8,128)(2,1)S(1)}, u32[]{:S(2)}, u32[]{:S(2)}) %collective-permute-start.10) | collective-permute-done | bytes 491552 | tf_op jit(solution)/shard_map/ppermute | solution.py:312
  116.1 2.1 %shard_map.93 = bf16[64,48,128]{2,1,0:T(8,128)(2,1)} custom-call(bf16[512,1536]{1,0:T(8,128)(2,1)S(1)} %bitcast.9, bf16[64,32,128]{2,1,0:T(8,128)(2,1)S(1)} %shard_map.90.refs_1_, bf16[160,1536]{1,0:T(8,128)(2,1)S(1)} %collective-permute-done.9.refs_2_, bf16[160,1536]{1,0:T(8,128)(2,1)S(1)} %collective-permute-done.10.refs_3_, f32[80,128]{1,0:T(8,128)S(1)} %add.13.refs_4_), custom_call_target="tpu_custom_call" | custom-call | flops 1000000000 | bytes 3000000 | tf_op jit(solution)/shard_map/pallas_call | solution.py:38
  118.2 11.8 %all-to-all-start.2 = ((bf16[64,48,128]{2,1,0:T(8,128)(2,1)}), bf16[64,48,128]{2,1,0:T(8,128)(2,1)S(1)}, u32[]{:S(2)}, u32[]{:S(2)}) async-start(bf16[64,48,128]{2,1,0:T(8,128)(2,1)} %shard_map.93), calls=%async_computation.2 | async-start | bytes 1572864 | tf_op jit(solution)/shard_map/all_to_all | solution.py:284
  130.0 3.7 %collective-permute-start.13 = (f32[80,128]{1,0:T(8,128)S(1)}, f32[80,128]{1,0:T(8,128)S(1)}, u32[]{:S(2)}, u32[]{:S(2)}) collective-permute-start(f32[80,128]{1,0:T(8,128)S(1)} %add.13.refs_4_), channel_id=1, source_target_pairs={{0,128},{32,160},{64,192},{96,224},{128,0},{160,32},{192,64},{224,... | collective-permute-start | bytes 122888 | tf_op jit(solution)/shard_map/ppermute | solution.py:281
  133.7 5.3 %collective-permute-done.13 = f32[80,128]{1,0:T(8,128)S(1)} collective-permute-done((f32[80,128]{1,0:T(8,128)S(1)}, f32[80,128]{1,0:T(8,128)S(1)}, u32[]{:S(2)}, u32[]{:S(2)}) %collective-permute-start.13) | collective-permute-done | bytes 40992 | tf_op jit(solution)/shard_map/ppermute | solution.py:281
  139.0 3.6 %collective-permute-start.14 = (f32[80,128]{1,0:T(8,128)S(1)}, f32[80,128]{1,0:T(8,128)S(1)}, u32[]{:S(2)}, u32[]{:S(2)}) collective-permute-start(f32[80,128]{1,0:T(8,128)S(1)} %add.14), channel_id=1, source_target_pairs={{0,256},{256,0},{1,257},{257,1},{2,258},{258,2},{3,259},{259,3},{4... | collective-permute-start | bytes 122888 | tf_op jit(solution)/shard_map/ppermute | solution.py:349
  143.3 6.5 %collective-permute-done.14 = f32[80,128]{1,0:T(8,128)S(1)} collective-permute-done((f32[80,128]{1,0:T(8,128)S(1)}, f32[80,128]{1,0:T(8,128)S(1)}, u32[]{:S(2)}, u32[]{:S(2)}) %collective-permute-start.14) | collective-permute-done | bytes 40992 | tf_op jit(solution)/shard_map/ppermute | solution.py:349
  150.5 1.6 %shard_map.94 = (bf16[2,8,128,320]{3,2,1,0:T(8,128)(2,1)S(1)}, f32[2,3,128,320]{3,2,1,0:T(8,128)S(1)}) custom-call(s32[1]{0:T(128)} %bitcast.refs_0_, bf16[128,256]{1,0:T(8,128)(2,1)S(1)} %shard_map.86.refs_1_, bf16[128,64]{1,0:T(8,128)(2,1)S(1)} %copy.12.refs_2_, bf16[64,5120]{1,0:T(8,128)(2,1)S(1)} %copy-done.5, ...), custom_call_target="tpu_custom_call" | custom-call | flops 400000000 | bytes 8000000 | tf_op jit(solution)/shard_map/pallas_call | solution.py:38
  157.1 1.8 %shard_map.95 = bf16[128,5120]{1,0:T(8,128)(2,1)} custom-call(s32[1]{0:T(128)} %bitcast.refs_0_, bf16[128,256]{1,0:T(8,128)(2,1)S(1)} %shard_map.86.refs_1_, bf16[64,48,128]{2,1,0:T(8,128)(2,1)S(1)} %all-to-all-done.2.refs_2_, bf16[2,8,128,320]{3,2,1,0:T(8,128)(2,1)S(1)} %copy-done.1, f32[2,3,128,320]{3,2,1,0:T(8,128)S(1)} %copy-done.4), custom_call_target="tpu_custom_call" | custom-call | flops 40000000 | bytes 3000000 | tf_op jit(solution)/shard_map/pallas_call | solution.py:38
  (45 shorter events, 15.5 us)
Async XLA Ops:
  0.6 23.4 %collective-permute-start.4 = (bf16[128,5120]{1,0:T(8,128)(2,1)}, bf16[128,5120]{1,0:T(8,128)(2,1)S(1)}, u32[]{:S(2)}, u32[]{:S(2)}) collective-permute-start(bf16[128,5120]{1,0:T(8,128)(2,1)} %refs_1_.2), channel_id=1, source_target_pairs={{0,1},{1,0},{2,3},{3,2},{4,5},{5,4},{6,7},{7,6},{8,9},{9,8},{10,11... | collective-permute-start | bytes 3932168 | tf_op jit(solution)/shard_map/ppermute | solution.py:249
  9.4 26.8 %collective-permute-start.1 = (bf16[320,1536]{1,0:T(8,128)(2,1)}, bf16[320,1536]{1,0:T(8,128)(2,1)}, u32[]{:S(2)}, u32[]{:S(2)}) collective-permute-start(bf16[320,1536]{1,0:T(8,128)(2,1)} %bitcast.12), channel_id=1, source_target_pairs={{0,224},{32,0},{64,32},{96,64},{128,96},{160,128},{192,160},{224,1... | collective-permute-start | bytes 2949128 | tf_op jit(solution)/shard_map/ppermute | solution.py:289
  14.7 26.5 %collective-permute-start = (bf16[320,1536]{1,0:T(8,128)(2,1)}, bf16[320,1536]{1,0:T(8,128)(2,1)}, u32[]{:S(2)}, u32[]{:S(2)}) collective-permute-start(bf16[320,1536]{1,0:T(8,128)(2,1)} %bitcast.13), channel_id=1, source_target_pairs={{0,32},{32,64},{64,96},{96,128},{128,160},{160,192},{192,224},{224... | collective-permute-start | bytes 2949128 | tf_op jit(solution)/shard_map/ppermute | solution.py:288
  16.7 19.1 %collective-permute-start.2 = (bf16[192,1536]{1,0:T(8,128)(2,1)}, bf16[192,1536]{1,0:T(8,128)(2,1)S(1)}, u32[]{:S(2)}, u32[]{:S(2)}) collective-permute-start(bf16[192,1536]{1,0:T(8,128)(2,1)} %bitcast.10), channel_id=1, source_target_pairs={{0,256},{256,0},{1,257},{257,1},{2,258},{258,2},{3,259},{259,3},{4... | collective-permute-start | bytes 1769480 | tf_op jit(solution)/shard_map/ppermute | solution.py:255
  20.7 3.3 %collective-permute-start.5 = (bf16[128,64]{1,0:T(8,128)(2,1)S(1)}, bf16[128,64]{1,0:T(8,128)(2,1)S(1)}, u32[]{:S(2)}, u32[]{:S(2)}) collective-permute-start(bf16[128,64]{1,0:T(8,128)(2,1)S(1)} %copy.12.refs_2_), channel_id=1, source_target_pairs={{0,1},{1,0},{2,3},{3,2},{4,5},{5,4},{6,7},{7,6},{8,9},{9,8},{10,11... | collective-permute-start | bytes 49160 | tf_op jit(solution)/shard_map/ppermute | solution.py:250
  24.0 1.3 copy-start.2
  27.1 19.4 %copy-start.6 = (bf16[1,192,1536]{2,1,0:T(8,128)(2,1)S(1)}, bf16[1,192,1536]{2,1,0:T(8,128)(2,1)}, u32[]{:S(2)}) copy-start(bf16[1,192,1536]{2,1,0:T(8,128)(2,1)} %param.9) | copy-start | bytes 1769476
  27.1 26.6 %all-to-all-start = ((f32[16,80,128]{2,1,0:T(8,128)}), f32[16,80,128]{2,1,0:T(8,128)}, u32[]{:S(2)}, u32[]{:S(2)}) async-start(f32[16,80,128]{2,1,0:T(8,128)} %shard_map.89), calls=%async_computation | async-start | bytes 1310720 | tf_op jit(solution)/shard_map/all_to_all | solution.py:252
  41.2 26.5 %collective-permute-start.7 = (bf16[320,1536]{1,0:T(8,128)(2,1)}, bf16[320,1536]{1,0:T(8,128)(2,1)}, u32[]{:S(2)}, u32[]{:S(2)}) collective-permute-start(bf16[320,1536]{1,0:T(8,128)(2,1)} %collective-permute-done.1.refs_3_), channel_id=1, source_target_pairs={{0,224},{32,0},{64,32},{96,64},{128,96},{160,128},{192,160},{224,1... | collective-permute-start | bytes 2949128 | tf_op jit(solution)/shard_map/ppermute | solution.py:295
  43.1 25.6 %collective-permute-start.3 = (bf16[320,1536]{1,0:T(8,128)(2,1)}, bf16[320,1536]{1,0:T(8,128)(2,1)}, u32[]{:S(2)}, u32[]{:S(2)}) collective-permute-start(bf16[320,1536]{1,0:T(8,128)(2,1)} %collective-permute-done.refs_2_), channel_id=1, source_target_pairs={{0,32},{32,64},{64,96},{96,128},{128,160},{160,192},{192,224},{224... | collective-permute-start | bytes 2949128 | tf_op jit(solution)/shard_map/ppermute | solution.py:294
  46.5 1.2 copy-start.7
  54.9 20.3 %collective-permute-start.11 = (f32[80,128]{1,0:T(8,128)S(1)}, f32[80,128]{1,0:T(8,128)S(1)}, u32[]{:S(2)}, u32[]{:S(2)}) collective-permute-start(f32[80,128]{1,0:T(8,128)S(1)} %reduce_sum.9), channel_id=1, source_target_pairs={{0,32},{32,0},{64,96},{96,64},{128,160},{160,128},{192,224},{224,1... | collective-permute-start | bytes 122888 | tf_op jit(solution)/shard_map/ppermute | solution.py:281
  56.8 34.4 %all-to-all-start.1 = ((bf16[64,48,128]{2,1,0:T(8,128)(2,1)}), bf16[64,48,128]{2,1,0:T(8,128)(2,1)S(1)}, u32[]{:S(2)}, u32[]{:S(2)}) async-start(bf16[64,48,128]{2,1,0:T(8,128)(2,1)} %shard_map.88), calls=%async_computation.1 | async-start | bytes 1572864 | tf_op jit(solution)/shard_map/all_to_all | solution.py:284
  68.7 28.4 %collective-permute-start.6 = (bf16[320,1536]{1,0:T(8,128)(2,1)}, bf16[320,1536]{1,0:T(8,128)(2,1)}, u32[]{:S(2)}, u32[]{:S(2)}) collective-permute-start(bf16[320,1536]{1,0:T(8,128)(2,1)} %collective-permute-done.3.refs_1_), channel_id=1, source_target_pairs={{0,32},{32,64},{64,96},{96,128},{128,160},{160,192},{192,224},{224... | collective-permute-start | bytes 2949128 | tf_op jit(solution)/shard_map/ppermute | solution.py:299
  71.4 25.7 %collective-permute-start.8 = (bf16[320,1536]{1,0:T(8,128)(2,1)}, bf16[320,1536]{1,0:T(8,128)(2,1)}, u32[]{:S(2)}, u32[]{:S(2)}) collective-permute-start(bf16[320,1536]{1,0:T(8,128)(2,1)} %collective-permute-done.7.refs_2_), channel_id=1, source_target_pairs={{0,224},{32,0},{64,32},{96,64},{128,96},{160,128},{192,160},{224,1... | collective-permute-start | bytes 2949128 | tf_op jit(solution)/shard_map/ppermute | solution.py:300
  75.2 21.8 %collective-permute-start.12 = (f32[80,128]{1,0:T(8,128)S(1)}, f32[80,128]{1,0:T(8,128)S(1)}, u32[]{:S(2)}, u32[]{:S(2)}) collective-permute-start(f32[80,128]{1,0:T(8,128)S(1)} %add.12), channel_id=1, source_target_pairs={{0,64},{32,96},{64,0},{96,32},{128,192},{160,224},{192,128},{224,1... | collective-permute-start | bytes 122888 | tf_op jit(solution)/shard_map/ppermute | solution.py:281
  91.2 26.9 %all-to-all-start.3 = ((bf16[64,32,128]{2,1,0:T(8,128)(2,1)}), bf16[64,32,128]{2,1,0:T(8,128)(2,1)S(1)}, u32[]{:S(2)}, u32[]{:S(2)}) async-start(bf16[64,32,128]{2,1,0:T(8,128)(2,1)} %shard_map.91.refs_2_), calls=%async_computation.3 | async-start | bytes 1048576 | tf_op jit(solution)/shard_map/all_to_all | solution.py:284
  98.7 13.8 %collective-permute-start.9 = (bf16[160,1536]{1,0:T(8,128)(2,1)S(1)}, bf16[160,1536]{1,0:T(8,128)(2,1)S(1)}, u32[]{:S(2)}, u32[]{:S(2)}) collective-permute-start(bf16[160,1536]{1,0:T(8,128)(2,1)S(1)} %get-tuple-element.19), channel_id=1, source_target_pairs={{0,32},{32,64},{64,96},{96,128},{128,160},{160,192},{192,224},{224... | collective-permute-start | bytes 1474568 | tf_op jit(solution)/shard_map/ppermute | solution.py:311
  102.3 13.8 %collective-permute-start.10 = (bf16[160,1536]{1,0:T(8,128)(2,1)S(1)}, bf16[160,1536]{1,0:T(8,128)(2,1)S(1)}, u32[]{:S(2)}, u32[]{:S(2)}) collective-permute-start(bf16[160,1536]{1,0:T(8,128)(2,1)S(1)} %get-tuple-element.20), channel_id=1, source_target_pairs={{0,224},{32,0},{64,32},{96,64},{128,96},{160,128},{192,160},{224,1... | collective-permute-start | bytes 1474568 | tf_op jit(solution)/shard_map/ppermute | solution.py:312
  118.2 24.4 %copy-start.8 = (s32[128,6]{0,1:T(8,128)S(1)}, s32[128,6]{0,1:T(8,128)}, u32[]{:S(2)}) copy-start(s32[128,6]{0,1:T(8,128)} %param.7) | copy-start | bytes 9220
  118.2 24.5 %copy-start.9 = (f32[128,6]{0,1:T(8,128)S(1)}, f32[128,6]{0,1:T(8,128)}, u32[]{:S(2)}) copy-start(f32[128,6]{0,1:T(8,128)} %param.8) | copy-start | bytes 9220
  118.2 32.4 %copy-start.5 = (bf16[64,5120]{1,0:T(8,128)(2,1)S(1)}, bf16[64,5120]{1,0:T(8,128)(2,1)}, u32[]{:S(2)}) copy-start(bf16[64,5120]{1,0:T(8,128)(2,1)} %refs_3_.1) | copy-start | bytes 1966084
  118.2 36.2 %all-to-all-start.2 = ((bf16[64,48,128]{2,1,0:T(8,128)(2,1)}), bf16[64,48,128]{2,1,0:T(8,128)(2,1)S(1)}, u32[]{:S(2)}, u32[]{:S(2)}) async-start(bf16[64,48,128]{2,1,0:T(8,128)(2,1)} %shard_map.93), calls=%async_computation.2 | async-start | bytes 1572864 | tf_op jit(solution)/shard_map/all_to_all | solution.py:284
  130.0 9.0 %collective-permute-start.13 = (f32[80,128]{1,0:T(8,128)S(1)}, f32[80,128]{1,0:T(8,128)S(1)}, u32[]{:S(2)}, u32[]{:S(2)}) collective-permute-start(f32[80,128]{1,0:T(8,128)S(1)} %add.13.refs_4_), channel_id=1, source_target_pairs={{0,128},{32,160},{64,192},{96,224},{128,0},{160,32},{192,64},{224,... | collective-permute-start | bytes 122888 | tf_op jit(solution)/shard_map/ppermute | solution.py:281
  139.0 10.9 %collective-permute-start.14 = (f32[80,128]{1,0:T(8,128)S(1)}, f32[80,128]{1,0:T(8,128)S(1)}, u32[]{:S(2)}, u32[]{:S(2)}) collective-permute-start(f32[80,128]{1,0:T(8,128)S(1)} %add.14), channel_id=1, source_target_pairs={{0,256},{256,0},{1,257},{257,1},{2,258},{258,2},{3,259},{259,3},{4... | collective-permute-start | bytes 122888 | tf_op jit(solution)/shard_map/ppermute | solution.py:349
  152.2 1.2 copy-start
  153.4 1.0 copy-start.3
  154.4 1.4 copy-start.1
  155.8 1.3 copy-start.4

commit v4 on v3

--- a/solution.py
+++ b/solution.py
@@ -18,9 +18,10 @@
 
 VMEM = pl.BlockSpec(memory_space=pltpu.VMEM)
 SMEM = pl.BlockSpec(memory_space=pltpu.SMEM)
-
-
-def call(kernel, out_shape, in_specs, flops, moved, scratch=(), after=()):
+ANY = pl.BlockSpec(memory_space=pl.ANY)
+
+
+def call(kernel, out_shape, in_specs, flops, moved, scratch=(), after=(), out_spec=VMEM):
     taken = len(in_specs)
 
     def without(*refs):
@@ -29,8 +30,8 @@
     run = pl.pallas_call(
         without,
         out_shape=out_shape,
-        in_specs=list(in_specs) + [pl.BlockSpec(memory_space=pl.ANY)] * len(after),
-        out_specs=jax.tree.map(lambda _: VMEM, out_shape),
+        in_specs=list(in_specs) + [ANY] * len(after),
+        out_specs=jax.tree.map(lambda _: out_spec, out_shape),
         scratch_shapes=list(scratch),
         compiler_params=pltpu.CompilerParams(vmem_limit_bytes=16 * 1024 * 1024),
         cost_estimate=pl.CostEstimate(flops=flops, bytes_accessed=moved, transcendentals=0),
@@ -153,61 +154,43 @@
     ]
 
 
-def more_products_kernel(capacity, rows_ref, begun_ref, *refs):
+def more_products_kernel(capacity, held, rows_ref, begun_ref, *refs):
     weights, (out_ref, lines_ref) = refs[:-2], refs[-2:]
-    targets, lines, lanes = out_ref.shape
-    held = begun_ref.shape[1] // capacity * capacity
+    lines = out_ref.shape[1]
     lines_ref[:, : begun_ref.shape[1], :] = begun_ref[...].astype(jnp.float32)
     put_lines(capacity, rows_ref, weights, lines_ref, held, lines)
     out_ref[...] = lines_ref[...].astype(out_ref.dtype)
 
 
-def halves_kernel(half, low_ref, high_ref, low_out, high_out):
-    low_out[...] = low_ref[:half, :]
-    high_out[...] = high_ref[half:, :]
-
-
-def early_kernel(capacity, layout, late, z_ref, combine_ref, key_ref, rope_ref, *refs):
-    chunks, (held_ref, rest_ref, attention_ref, lines_ref) = refs[:-4], refs[-4:]
-    groups, tokens, piece = attention_ref.shape
-    pairs, ring = held_ref.shape[:2]
-    attention = jnp.dot(key_ref[...], rope_ref[...], preferred_element_type=jnp.float32)
-    for d in range(groups):
-        attention_ref[d] = attention[:, d * piece : (d + 1) * piece]
+def halves_kernel(half, low_ref, high_ref, low_out, high_out, semaphores):
+    copies = [
+        pltpu.make_async_copy(low_ref.at[:half], low_out, semaphores.at[0]),
+        pltpu.make_async_copy(high_ref.at[half:], high_out, semaphores.at[1]),
+    ]
+    for copy in copies:
+        copy.start()
+    for copy in copies:
+        copy.wait()
+
+
+def finish_kernel(capacity, layout, z_ref, combine_ref, key_ref, rope_ref, *refs):
+    chunks, (out_ref, pieces_ref, lines_ref) = refs[:-3], refs[-3:]
+    pairs, ring, tokens, piece = pieces_ref.shape
     z = z_ref[0]
-
-    def here(g, distance):
-        return attention_ref[g * ring + lax.rem(z + distance + ring, ring)]
-
     for chunk, distances in zip(chunks, layout):
         for g, routed in enumerate(routed_sums(capacity, combine_ref[...], chunk, lines_ref)):
-            for i, distance in enumerate(distances):
-                held_ref[g, distance % ring] = (
-                    routed[:, i * piece : (i + 1) * piece] + here(g, distance)
-                ).astype(held_ref.dtype)
+            for start, distance in distances:
+                pieces_ref[g, distance % ring] = routed[:, start : start + piece]
     for g in range(pairs):
-        for i, distance in enumerate(late):
-            held_ref[g, distance % ring] = jnp.zeros((tokens, piece), held_ref.dtype)
-            rest_ref[g, i] = here(g, distance)
-
-
-def late_kernel(
-    capacity, distances, early, z_ref, combine_ref, chunk_ref, held_ref, rest_ref, out_ref, pieces_ref, lines_ref
-):
-    pairs, ring, tokens, piece = held_ref.shape
-    z = z_ref[0]
-    for g, routed in enumerate(routed_sums(capacity, combine_ref[...], chunk_ref, lines_ref)):
-        for distance in early:
-            pieces_ref[distance % ring] = held_ref[g, distance % ring]
-        for i, distance in enumerate(distances):
-            pieces_ref[distance % ring] = (
-                routed[:, i * piece : (i + 1) * piece] + rest_ref[g, i]
-            ).astype(pieces_ref.dtype)
         for h in range(ring // 2):
-            left = pieces_ref[lax.rem(2 * h - z + ring, ring)]
-            right = pieces_ref[lax.rem(2 * h + 1 - z + ring, ring)]
+            left = pieces_ref[g, lax.rem(2 * h - z + ring, ring)]
+            right = pieces_ref[g, lax.rem(2 * h + 1 - z + ring, ring)]
             columns = slice((g * ring + 2 * h) * piece, (g * ring + 2 * h + 2) * piece)
-            out_ref[:, columns] = jnp.concatenate([left, right], axis=1)
+            attention = jnp.dot(
+                key_ref[...], rope_ref[:, columns], preferred_element_type=jnp.float32
+            )
+            routed = jnp.concatenate([left, right], axis=1)
+            out_ref[:, columns] = (routed + attention).astype(out_ref.dtype)
 
 
 def body(routes, route_weights, hidden_grads, expert_weight, normed, key_grad, rope_weight):
@@ -280,22 +263,40 @@
     def added(sums, bit):
         return sums + lax.ppermute(sums, "z", [(i, i ^ bit) for i in range(ring)])
 
+    def more_products(begun, columns, weights, flops, after=()):
+        shape = (pairs * experts_here, 48, 128)
+        return call(
+            functools.partial(more_products_kernel, capacity, -(-columns // 128) * capacity),
+            struct(shape, jnp.bfloat16),
+            [VMEM] * (2 + len(weights)),
+            flops,
+            3 * 10**6,
+            [pltpu.VMEM(shape, jnp.float32)],
+            after,
+        )(both, begun, *weights)
+
     def send(computed):
         return lax.all_to_all(computed, PLANE, split_axis=0, concat_axis=0, tiled=True)
 
-    layout = ((0, -1, 1), (-2, 2), (-3, 3, 4))
+    whole = -(-piece // 128) * 128
+    layout = (
+        ((0, 0), (whole, -1), (whole + piece, 1)),
+        ((0, -2), (piece, 2)),
+        ((0, -3), (piece, 3), (2 * piece, 4)),
+    )
     below, above = [projection], [projection]
     below.append(lax.ppermute(below[-1], "z", up))
     above.append(lax.ppermute(above[-1], "z", down))
-    below[1], above[1], other = lax.optimization_barrier((below[1], above[1], other))
     both = spaced_rows(other)
-    first = products([projection, below[1], above[1]], 2 * 10**9)
+    begun = products([projection], 1 * 10**9)
+    below[1], above[1], begun = lax.optimization_barrier((below[1], above[1], begun))
+    first = more_products(begun, piece, [below[1], above[1]], 2 * 10**9)
     first, mine = lax.optimization_barrier((first, mine))
     below.append(lax.ppermute(below[-1], "z", up))
     above.append(lax.ppermute(above[-1], "z", down))
     below[2], _ = lax.optimization_barrier((below[2], first))
     above[2], _ = lax.optimization_barrier((above[2], first))
-    second = products([below[2], above[2]], 25 * 10**9)
+    second = products([below[2], above[2]], 15 * 10**9)
     below.append(lax.ppermute(below[-1], "z", up))
     above.append(lax.ppermute(above[-1], "z", down))
     sent = [send(first)]
@@ -303,26 +304,19 @@
     half_low, half_high = call(
         functools.partial(halves_kernel, half),
         [struct((half, depth), jnp.bfloat16)] * 2,
-        [VMEM] * 2,
+        [ANY] * 2,
         0,
         3 * 10**6,
-        after=[second] + sent,
+        [pltpu.SemaphoreType.DMA((2,))],
+        [second] + sent,
+        ANY,
     )(below[-1], above[-1])
     last_low = lax.ppermute(half_low, "z", up)
     last_high = lax.ppermute(half_high, "z", down)
     sent.append(send(second))
     two = added(added(mine, 1), 2)
     begun = products([below[3], above[3]], 10 * 10**9)
-    shape = (pairs * experts_here, 48, 128)
-    third = call(
-        functools.partial(more_products_kernel, capacity),
-        struct(shape, jnp.bfloat16),
-        [VMEM] * 4,
-        1 * 10**9,
-        3 * 10**6,
-        [pltpu.VMEM(shape, jnp.float32)],
-        [two],
-    )(both, begun, last_low, last_high)
+    third = more_products(begun, 2 * piece, [last_low, last_high], 1 * 10**9, [two])
     chunks = sent + [send(third)]
 
     combine = call(
@@ -334,17 +328,6 @@
     )(routes, route_weights)
     most = max(chunk.shape[1] for chunk in chunks)
     lines = pltpu.VMEM((pairs * experts_here, most + PAD, 128), jnp.float32)
-    held, rest = call(
-        functools.partial(early_kernel, capacity, layout[:-1], layout[-1]),
-        [
-            struct((pairs, ring, tokens, piece), jnp.bfloat16),
-            struct((pairs, len(layout[-1]), tokens, piece), jnp.float32),
-        ],
-        [SMEM] + [VMEM] * (3 + len(chunks[:-1])),
-        4 * 10**8,
-        8 * 10**6,
-        [pltpu.VMEM((groups, tokens, piece), jnp.float32), lines],
-    )(z, combine, key_grad, rope_weight, *chunks[:-1])
     summed = added(two, 4)
     summed = summed + lax.ppermute(summed, "ylo", swap)
     scale_factor = (tokens * groups * experts_here) ** (-0.5)
@@ -357,13 +340,13 @@
     )(summed)
 
     token_grad = call(
-        functools.partial(late_kernel, capacity, layout[-1], sum(layout[:-1], ())),
+        functools.partial(finish_kernel, capacity, layout),
         struct((tokens, width), jnp.bfloat16),
-        [SMEM] + [VMEM] * 4,
-        4 * 10**7,
-        3 * 10**6,
-        [pltpu.VMEM((ring, tokens, piece), jnp.bfloat16), lines],
-    )(z, combine, chunks[-1], held, rest)
+        [SMEM] + [VMEM] * (3 + len(chunks)),
+        4 * 10**8,
+        6 * 10**6,
+        [pltpu.VMEM((pairs, ring, tokens, piece), jnp.float32), lines],
+    )(z, combine, key_grad, rope_weight, *chunks)
     return (token_grad, rope_grad)
 
 

time: 160 us -> 155 us (0.969)
  local copies, waits for them, and re-layouts: 7.87 us -> 3 us
  starting transfers between devices: 88.2 us -> 90.8 us
    unnamed x23 -> x15, local copies, waits for them, and re-layouts: 7.87 us -> 3 us
    all_to_all x1, waiting for transfers between devices: 0.9 us -> 4 us  [body(): lax.all_to_all(mine, ('x', 'yhi'), split_axis=0, concat_axis=0, tiled=True)]
    ppermute x3, starting transfers between devices: 7.5 us -> 9.34 us  [added(): return sums + lax.ppermute(sums, 'z', [(i, i ^ bit) for i in range(ring)])]
  transfers between devices with their start and end apart: 19 -> 19, of which waited for: 10 -> 11; matrix products, arithmetic and copies ran while one was open for 1% -> 1% of each run, Pallas kernels for 14% -> 13%
where the time goes in v4:
time: 155 us; the launch traced here: 154 us
  starting transfers between devices  90.8 us (59%)
  waiting for transfers between devices  35.9 us (23%)
  Pallas kernels  22.4 us (14%)
  local copies, waits for them, and re-layouts  3 us (2%)
    all_to_all x3, starting transfers between devices, send(): lax.all_to_all(computed, PLANE, split_axis=0, concat_axis=0, tiled=True)  29.9 us
    pallas_call x11, Pallas kernels, call(): return lambda *args: run(*args, *after)  22.4 us
    ppermute x3, starting transfers between devices, body(): above.append(lax.ppermute(above[-1], 'z', down))  12.5 us
    all_to_all x3, waiting for transfers between devices, send(): lax.all_to_all(computed, PLANE, split_axis=0, concat_axis=0, tiled=True)  9.42 us
    ppermute x3, starting transfers between devices, added(): return sums + lax.ppermute(sums, 'z', [(i, i ^ bit) for i in range(ring)])  9.34 us
    ppermute x1, starting transfers between devices, body(): lax.ppermute(normed, 'core', swap)  8.79 us
    all_to_all x1, starting transfers between devices, body(): lax.all_to_all(mine, ('x', 'yhi'), split_axis=0, concat_axis=0, tiled=True)  8.66 us
    ppermute x3, starting transfers between devices, body(): below.append(lax.ppermute(below[-1], 'z', up))  7.21 us
  transfers between devices with their start and end apart: 19, of which 11 were waited for; matrix products, arithmetic and copies ran while one was open for 1% of the time, Pallas kernels for 13%

profile of v4, /device:TPU:1, one launch (start us, length us, event | category | flops | bytes accessed | tf_op | source)
XLA Modules:
  0.0 154.2 jit_solution(4916943876334039739)
XLA Ops:
  0.6 8.8 %collective-permute-start.3 = (bf16[128,5120]{1,0:T(8,128)(2,1)}, bf16[128,5120]{1,0:T(8,128)(2,1)S(1)}, u32[]{:S(2)}, u32[]{:S(2)}) collective-permute-start(bf16[128,5120]{1,0:T(8,128)(2,1)} %refs_1_.2), channel_id=1, source_target_pairs={{0,1},{1,0},{2,3},{3,2},{4,5},{5,4},{6,7},{7,6},{8,9},{9,8},{10,11... | collective-permute-start | bytes 3932168 | tf_op jit(solution)/shard_map/ppermute | solution.py:232
  9.4 1.9 %collective-permute-start.1 = (bf16[320,1536]{1,0:T(8,128)(2,1)}, bf16[320,1536]{1,0:T(8,128)(2,1)}, u32[]{:S(2)}, u32[]{:S(2)}) collective-permute-start(bf16[320,1536]{1,0:T(8,128)(2,1)} %bitcast.13), channel_id=1, source_target_pairs={{0,32},{32,64},{64,96},{96,128},{128,160},{160,192},{192,224},{224... | collective-permute-start | bytes 2949128 | tf_op jit(solution)/shard_map/ppermute | solution.py:288
  11.4 5.3 %collective-permute-start.2 = (bf16[320,1536]{1,0:T(8,128)(2,1)}, bf16[320,1536]{1,0:T(8,128)(2,1)}, u32[]{:S(2)}, u32[]{:S(2)}) collective-permute-start(bf16[320,1536]{1,0:T(8,128)(2,1)} %bitcast.14), channel_id=1, source_target_pairs={{0,224},{32,0},{64,32},{96,64},{128,96},{160,128},{192,160},{224,1... | collective-permute-start | bytes 2949128 | tf_op jit(solution)/shard_map/ppermute | solution.py:289
  16.7 3.2 %collective-permute-start = (bf16[192,1536]{1,0:T(8,128)(2,1)}, bf16[192,1536]{1,0:T(8,128)(2,1)S(1)}, u32[]{:S(2)}, u32[]{:S(2)}) collective-permute-start(bf16[192,1536]{1,0:T(8,128)(2,1)} %bitcast.11), channel_id=1, source_target_pairs={{0,256},{256,0},{1,257},{257,1},{2,258},{258,2},{3,259},{259,3},{4... | collective-permute-start | bytes 1769480 | tf_op jit(solution)/shard_map/ppermute | solution.py:238
  20.7 2.5 %collective-permute-start.4 = (bf16[128,64]{1,0:T(8,128)(2,1)S(1)}, bf16[128,64]{1,0:T(8,128)(2,1)S(1)}, u32[]{:S(2)}, u32[]{:S(2)}) collective-permute-start(bf16[128,64]{1,0:T(8,128)(2,1)S(1)} %copy.13.refs_2_), channel_id=1, source_target_pairs={{0,1},{1,0},{2,3},{3,2},{4,5},{5,4},{6,7},{7,6},{8,9},{9,8},{10,11... | collective-permute-start | bytes 49160 | tf_op jit(solution)/shard_map/ppermute | solution.py:233
  27.1 8.7 %all-to-all-start = ((f32[16,80,128]{2,1,0:T(8,128)}), f32[16,80,128]{2,1,0:T(8,128)}, u32[]{:S(2)}, u32[]{:S(2)}) async-start(f32[16,80,128]{2,1,0:T(8,128)} %shard_map.90), calls=%async_computation | async-start | bytes 1310720 | tf_op jit(solution)/shard_map/all_to_all | solution.py:235
  38.1 5.3 %collective-permute-start.6 = (bf16[320,1536]{1,0:T(8,128)(2,1)}, bf16[320,1536]{1,0:T(8,128)(2,1)}, u32[]{:S(2)}, u32[]{:S(2)}) collective-permute-start(bf16[320,1536]{1,0:T(8,128)(2,1)} %collective-permute-done.2.refs_3_), channel_id=1, source_target_pairs={{0,224},{32,0},{64,32},{96,64},{128,96},{160,128},{192,160},{224,1... | collective-permute-start | bytes 2949128 | tf_op jit(solution)/shard_map/ppermute | solution.py:296
  43.4 1.9 %collective-permute-start.5 = (bf16[320,1536]{1,0:T(8,128)(2,1)}, bf16[320,1536]{1,0:T(8,128)(2,1)}, u32[]{:S(2)}, u32[]{:S(2)}) collective-permute-start(bf16[320,1536]{1,0:T(8,128)(2,1)} %collective-permute-done.1.refs_2_), channel_id=1, source_target_pairs={{0,32},{32,64},{64,96},{96,128},{128,160},{160,192},{192,224},{224... | collective-permute-start | bytes 2949128 | tf_op jit(solution)/shard_map/ppermute | solution.py:295
  45.4 4.4 %shard_map.89 = bf16[64,48,128]{2,1,0:T(8,128)(2,1)} custom-call(bf16[512,1536]{1,0:T(8,128)(2,1)S(1)} %bitcast.7, bf16[64,32,128]{2,1,0:T(8,128)(2,1)S(1)} %shard_map.88.refs_1_, bf16[320,1536]{1,0:T(8,128)(2,1)} %collective-permute-done.1.refs_2_, bf16[320,1536]{1,0:T(8,128)(2,1)} %collective-permute-done.2.refs_3_), custom_call_target="tpu_custom_call" | custom-call | flops 2000000000 | bytes 3000000 | tf_op jit(solution)/shard_map/pallas_call | solution.py:39
  49.7 4.0 %all-to-all-done = f32[16,80,128]{2,1,0:T(8,128)} async-done(((f32[16,80,128]{2,1,0:T(8,128)}), f32[16,80,128]{2,1,0:T(8,128)}, u32[]{:S(2)}, u32[]{:S(2)}) %all-to-all-start) | async-done | bytes 655392 | tf_op jit(solution)/shard_map/all_to_all | solution.py:235
  54.9 8.6 %all-to-all-start.1 = ((bf16[64,48,128]{2,1,0:T(8,128)(2,1)}), bf16[64,48,128]{2,1,0:T(8,128)(2,1)S(1)}, u32[]{:S(2)}, u32[]{:S(2)}) async-start(bf16[64,48,128]{2,1,0:T(8,128)(2,1)} %shard_map.89), calls=%async_computation.1 | async-start | bytes 1572864 | tf_op jit(solution)/shard_map/all_to_all | solution.py:279
  63.5 1.9 %collective-permute-start.11 = (f32[80,128]{1,0:T(8,128)S(1)}, f32[80,128]{1,0:T(8,128)S(1)}, u32[]{:S(2)}, u32[]{:S(2)}) collective-permute-start(f32[80,128]{1,0:T(8,128)S(1)} %reduce_sum.9), channel_id=1, source_target_pairs={{0,32},{32,0},{64,96},{96,64},{128,160},{160,128},{192,224},{224,1... | collective-permute-start | bytes 122888 | tf_op jit(solution)/shard_map/ppermute | solution.py:264
  65.4 3.6 %collective-permute-done.5.refs_1_ = bf16[320,1536]{1,0:T(8,128)(2,1)} collective-permute-done((bf16[320,1536]{1,0:T(8,128)(2,1)}, bf16[320,1536]{1,0:T(8,128)(2,1)}, u32[]{:S(2)}, u32[]{:S(2)}) %collective-permute-start.5) | collective-permute-done | bytes 983072 | tf_op jit(solution)/shard_map/ppermute | solution.py:295
  69.0 1.9 %collective-permute-start.8 = (bf16[320,1536]{1,0:T(8,128)(2,1)}, bf16[320,1536]{1,0:T(8,128)(2,1)}, u32[]{:S(2)}, u32[]{:S(2)}) collective-permute-start(bf16[320,1536]{1,0:T(8,128)(2,1)} %collective-permute-done.6.refs_2_), channel_id=1, source_target_pairs={{0,224},{32,0},{64,32},{96,64},{128,96},{160,128},{192,160},{224,1... | collective-permute-start | bytes 2949128 | tf_op jit(solution)/shard_map/ppermute | solution.py:301
  71.0 3.4 %collective-permute-start.7 = (bf16[320,1536]{1,0:T(8,128)(2,1)}, bf16[320,1536]{1,0:T(8,128)(2,1)}, u32[]{:S(2)}, u32[]{:S(2)}) collective-permute-start(bf16[320,1536]{1,0:T(8,128)(2,1)} %collective-permute-done.5.refs_1_), channel_id=1, source_target_pairs={{0,32},{32,64},{64,96},{96,128},{128,160},{160,192},{192,224},{224... | collective-permute-start | bytes 2949128 | tf_op jit(solution)/shard_map/ppermute | solution.py:300
  74.4 1.9 %collective-permute-start.12 = (f32[80,128]{1,0:T(8,128)S(1)}, f32[80,128]{1,0:T(8,128)S(1)}, u32[]{:S(2)}, u32[]{:S(2)}) collective-permute-start(f32[80,128]{1,0:T(8,128)S(1)} %add.12), channel_id=1, source_target_pairs={{0,64},{32,96},{64,0},{96,32},{128,192},{160,224},{192,128},{224,1... | collective-permute-start | bytes 122888 | tf_op jit(solution)/shard_map/ppermute | solution.py:264
  76.3 4.3 %shard_map.91.refs_2_ = bf16[64,32,128]{2,1,0:T(8,128)(2,1)} custom-call(bf16[512,1536]{1,0:T(8,128)(2,1)S(1)} %bitcast.8, bf16[320,1536]{1,0:T(8,128)(2,1)} %collective-permute-done.5.refs_1_, bf16[320,1536]{1,0:T(8,128)(2,1)} %collective-permute-done.6.refs_2_), custom_call_target="tpu_custom_call" | custom-call | flops 15000000512 | bytes 4000000 | tf_op jit(solution)/shard_map/pallas_call | solution.py:39
  80.6 6.4 %all-to-all-done.1.refs_3_.refs_4_ = bf16[64,48,128]{2,1,0:T(8,128)(2,1)S(1)} async-done(((bf16[64,48,128]{2,1,0:T(8,128)(2,1)}), bf16[64,48,128]{2,1,0:T(8,128)(2,1)S(1)}, u32[]{:S(2)}, u32[]{:S(2)}) %all-to-all-start.1) | async-done | bytes 786464 | tf_op jit(solution)/shard_map/all_to_all | solution.py:279
  87.0 6.2 %all-to-all-start.2 = ((bf16[64,32,128]{2,1,0:T(8,128)(2,1)}), bf16[64,32,128]{2,1,0:T(8,128)(2,1)S(1)}, u32[]{:S(2)}, u32[]{:S(2)}) async-start(bf16[64,32,128]{2,1,0:T(8,128)(2,1)} %shard_map.91.refs_2_), calls=%async_computation.2 | async-start | bytes 1048576 | tf_op jit(solution)/shard_map/all_to_all | solution.py:279
  96.8 2.4 %collective-permute-start.10 = (bf16[160,1536]{1,0:T(8,128)(2,1)S(1)}, bf16[160,1536]{1,0:T(8,128)(2,1)S(1)}, u32[]{:S(2)}, u32[]{:S(2)}) collective-permute-start(bf16[160,1536]{1,0:T(8,128)(2,1)S(1)} %get-tuple-element.18), channel_id=1, source_target_pairs={{0,224},{32,0},{64,32},{96,64},{128,96},{160,128},{192,160},{224,1... | collective-permute-start | bytes 1474568 | tf_op jit(solution)/shard_map/ppermute | solution.py:315
  99.2 2.9 %collective-permute-start.9 = (bf16[160,1536]{1,0:T(8,128)(2,1)S(1)}, bf16[160,1536]{1,0:T(8,128)(2,1)S(1)}, u32[]{:S(2)}, u32[]{:S(2)}) collective-permute-start(bf16[160,1536]{1,0:T(8,128)(2,1)S(1)} %get-tuple-element.17), channel_id=1, source_target_pairs={{0,32},{32,64},{64,96},{96,128},{128,160},{160,192},{192,224},{224... | collective-permute-start | bytes 1474568 | tf_op jit(solution)/shard_map/ppermute | solution.py:314
  102.1 3.5 %shard_map.92.refs_1_ = bf16[64,32,128]{2,1,0:T(8,128)(2,1)S(1)} custom-call(bf16[512,1536]{1,0:T(8,128)(2,1)S(1)} %bitcast.9, bf16[320,1536]{1,0:T(8,128)(2,1)} %collective-permute-done.7.refs_1_.refs_0_, bf16[320,1536]{1,0:T(8,128)(2,1)} %collective-permute-done.8.refs_2_.refs_1_), custom_call_target="tpu_custom_call" | custom-call | flops 10000000000 | bytes 4000000 | tf_op jit(solution)/shard_map/pallas_call | solution.py:39
  105.6 2.9 %collective-permute-done.10.refs_3_ = bf16[160,1536]{1,0:T(8,128)(2,1)S(1)} collective-permute-done((bf16[160,1536]{1,0:T(8,128)(2,1)S(1)}, bf16[160,1536]{1,0:T(8,128)(2,1)S(1)}, u32[]{:S(2)}, u32[]{:S(2)}) %collective-permute-start.10) | collective-permute-done | bytes 491552 | tf_op jit(solution)/shard_map/ppermute | solution.py:315
  108.5 2.7 %collective-permute-done.9.refs_2_ = bf16[160,1536]{1,0:T(8,128)(2,1)S(1)} collective-permute-done((bf16[160,1536]{1,0:T(8,128)(2,1)S(1)}, bf16[160,1536]{1,0:T(8,128)(2,1)S(1)}, u32[]{:S(2)}, u32[]{:S(2)}) %collective-permute-start.9) | collective-permute-done | bytes 491552 | tf_op jit(solution)/shard_map/ppermute | solution.py:314
  111.2 2.0 %shard_map.94 = bf16[64,48,128]{2,1,0:T(8,128)(2,1)} custom-call(bf16[512,1536]{1,0:T(8,128)(2,1)S(1)} %bitcast.10, bf16[64,32,128]{2,1,0:T(8,128)(2,1)S(1)} %shard_map.92.refs_1_, bf16[160,1536]{1,0:T(8,128)(2,1)S(1)} %collective-permute-done.9.refs_2_, bf16[160,1536]{1,0:T(8,128)(2,1)S(1)} %collective-permute-done.10.refs_3_, f32[80,128]{1,0:T(8,128)S(1)} %add.13.refs_4_), custom_call_target="tpu_custom_call" | custom-call | flops 1000000000 | bytes 3000000 | tf_op jit(solution)/shard_map/pallas_call | solution.py:39
  113.2 15.0 %all-to-all-start.3 = ((bf16[64,48,128]{2,1,0:T(8,128)(2,1)}), bf16[64,48,128]{2,1,0:T(8,128)(2,1)S(1)}, u32[]{:S(2)}, u32[]{:S(2)}) async-start(bf16[64,48,128]{2,1,0:T(8,128)(2,1)} %shard_map.94), calls=%async_computation.3 | async-start | bytes 1572864 | tf_op jit(solution)/shard_map/all_to_all | solution.py:279
  128.3 5.5 %collective-permute-start.13 = (f32[80,128]{1,0:T(8,128)S(1)}, f32[80,128]{1,0:T(8,128)S(1)}, u32[]{:S(2)}, u32[]{:S(2)}) collective-permute-start(f32[80,128]{1,0:T(8,128)S(1)} %add.13.refs_4_), channel_id=1, source_target_pairs={{0,128},{32,160},{64,192},{96,224},{128,0},{160,32},{192,64},{224,... | collective-permute-start | bytes 122888 | tf_op jit(solution)/shard_map/ppermute | solution.py:264
  133.8 3.9 %collective-permute-done.13 = f32[80,128]{1,0:T(8,128)S(1)} collective-permute-done((f32[80,128]{1,0:T(8,128)S(1)}, f32[80,128]{1,0:T(8,128)S(1)}, u32[]{:S(2)}, u32[]{:S(2)}) %collective-permute-start.13) | collective-permute-done | bytes 40992 | tf_op jit(solution)/shard_map/ppermute | solution.py:264
  137.7 3.5 %collective-permute-start.14 = (f32[80,128]{1,0:T(8,128)S(1)}, f32[80,128]{1,0:T(8,128)S(1)}, u32[]{:S(2)}, u32[]{:S(2)}) collective-permute-start(f32[80,128]{1,0:T(8,128)S(1)} %add.14), channel_id=1, source_target_pairs={{0,256},{256,0},{1,257},{257,1},{2,258},{258,2},{3,259},{259,3},{4... | collective-permute-start | bytes 122888 | tf_op jit(solution)/shard_map/ppermute | solution.py:332
  141.9 6.2 %collective-permute-done.14 = f32[80,128]{1,0:T(8,128)S(1)} collective-permute-done((f32[80,128]{1,0:T(8,128)S(1)}, f32[80,128]{1,0:T(8,128)S(1)}, u32[]{:S(2)}, u32[]{:S(2)}) %collective-permute-start.14) | collective-permute-done | bytes 40992 | tf_op jit(solution)/shard_map/ppermute | solution.py:332
  148.8 3.0 %all-to-all-done.3.refs_6_ = bf16[64,48,128]{2,1,0:T(8,128)(2,1)S(1)} async-done(((bf16[64,48,128]{2,1,0:T(8,128)(2,1)}), bf16[64,48,128]{2,1,0:T(8,128)(2,1)S(1)}, u32[]{:S(2)}, u32[]{:S(2)}) %all-to-all-start.3) | async-done | bytes 786464 | tf_op jit(solution)/shard_map/all_to_all | solution.py:279
  151.8 2.4 %shard_map.95 = bf16[128,5120]{1,0:T(8,128)(2,1)} custom-call(s32[1]{0:T(128)} %bitcast.refs_0_, bf16[128,256]{1,0:T(8,128)(2,1)S(1)} %shard_map.86.refs_1_, bf16[128,64]{1,0:T(8,128)(2,1)S(1)} %copy.13.refs_2_, bf16[64,5120]{1,0:T(8,128)(2,1)S(1)} %copy-done.1, bf16[64,48,128]{2,1,0:T(8,128)(2,1)S(1)} %all-to-all-done.1.refs_3_.refs_4_, ...), custom_call_target="tpu_custom_call" | custom-call | flops 400000000 | bytes 6000000 | tf_op jit(solution)/shard_map/pallas_call | solution.py:39
  (37 shorter events, 13.2 us)
Async XLA Ops:
  0.6 23.4 %collective-permute-start.3 = (bf16[128,5120]{1,0:T(8,128)(2,1)}, bf16[128,5120]{1,0:T(8,128)(2,1)S(1)}, u32[]{:S(2)}, u32[]{:S(2)}) collective-permute-start(bf16[128,5120]{1,0:T(8,128)(2,1)} %refs_1_.2), channel_id=1, source_target_pairs={{0,1},{1,0},{2,3},{3,2},{4,5},{5,4},{6,7},{7,6},{8,9},{9,8},{10,11... | collective-permute-start | bytes 3932168 | tf_op jit(solution)/shard_map/ppermute | solution.py:232
  9.4 28.7 %collective-permute-start.1 = (bf16[320,1536]{1,0:T(8,128)(2,1)}, bf16[320,1536]{1,0:T(8,128)(2,1)}, u32[]{:S(2)}, u32[]{:S(2)}) collective-permute-start(bf16[320,1536]{1,0:T(8,128)(2,1)} %bitcast.13), channel_id=1, source_target_pairs={{0,32},{32,64},{64,96},{96,128},{128,160},{160,192},{192,224},{224... | collective-permute-start | bytes 2949128 | tf_op jit(solution)/shard_map/ppermute | solution.py:288
  11.4 26.8 %collective-permute-start.2 = (bf16[320,1536]{1,0:T(8,128)(2,1)}, bf16[320,1536]{1,0:T(8,128)(2,1)}, u32[]{:S(2)}, u32[]{:S(2)}) collective-permute-start(bf16[320,1536]{1,0:T(8,128)(2,1)} %bitcast.14), channel_id=1, source_target_pairs={{0,224},{32,0},{64,32},{96,64},{128,96},{160,128},{192,160},{224,1... | collective-permute-start | bytes 2949128 | tf_op jit(solution)/shard_map/ppermute | solution.py:289
  16.7 19.2 %collective-permute-start = (bf16[192,1536]{1,0:T(8,128)(2,1)}, bf16[192,1536]{1,0:T(8,128)(2,1)S(1)}, u32[]{:S(2)}, u32[]{:S(2)}) collective-permute-start(bf16[192,1536]{1,0:T(8,128)(2,1)} %bitcast.11), channel_id=1, source_target_pairs={{0,256},{256,0},{1,257},{257,1},{2,258},{258,2},{3,259},{259,3},{4... | collective-permute-start | bytes 1769480 | tf_op jit(solution)/shard_map/ppermute | solution.py:238
  20.7 3.3 %collective-permute-start.4 = (bf16[128,64]{1,0:T(8,128)(2,1)S(1)}, bf16[128,64]{1,0:T(8,128)(2,1)S(1)}, u32[]{:S(2)}, u32[]{:S(2)}) collective-permute-start(bf16[128,64]{1,0:T(8,128)(2,1)S(1)} %copy.13.refs_2_), channel_id=1, source_target_pairs={{0,1},{1,0},{2,3},{3,2},{4,5},{5,4},{6,7},{7,6},{8,9},{9,8},{10,11... | collective-permute-start | bytes 49160 | tf_op jit(solution)/shard_map/ppermute | solution.py:233
  24.0 1.3 copy-start
  27.1 8.7 %copy-start.2 = (bf16[1,192,1536]{2,1,0:T(8,128)(2,1)S(1)}, bf16[1,192,1536]{2,1,0:T(8,128)(2,1)}, u32[]{:S(2)}) copy-start(bf16[1,192,1536]{2,1,0:T(8,128)(2,1)} %param.9) | copy-start | bytes 1769476
  27.1 26.6 %all-to-all-start = ((f32[16,80,128]{2,1,0:T(8,128)}), f32[16,80,128]{2,1,0:T(8,128)}, u32[]{:S(2)}, u32[]{:S(2)}) async-start(f32[16,80,128]{2,1,0:T(8,128)} %shard_map.90), calls=%async_computation | async-start | bytes 1310720 | tf_op jit(solution)/shard_map/all_to_all | solution.py:235
  35.8 1.2 copy-start.3
  38.1 27.3 %collective-permute-start.6 = (bf16[320,1536]{1,0:T(8,128)(2,1)}, bf16[320,1536]{1,0:T(8,128)(2,1)}, u32[]{:S(2)}, u32[]{:S(2)}) collective-permute-start(bf16[320,1536]{1,0:T(8,128)(2,1)} %collective-permute-done.2.refs_3_), channel_id=1, source_target_pairs={{0,224},{32,0},{64,32},{96,64},{128,96},{160,128},{192,160},{224,1... | collective-permute-start | bytes 2949128 | tf_op jit(solution)/shard_map/ppermute | solution.py:296
  43.4 25.6 %collective-permute-start.5 = (bf16[320,1536]{1,0:T(8,128)(2,1)}, bf16[320,1536]{1,0:T(8,128)(2,1)}, u32[]{:S(2)}, u32[]{:S(2)}) collective-permute-start(bf16[320,1536]{1,0:T(8,128)(2,1)} %collective-permute-done.1.refs_2_), channel_id=1, source_target_pairs={{0,32},{32,64},{64,96},{96,128},{128,160},{160,192},{192,224},{224... | collective-permute-start | bytes 2949128 | tf_op jit(solution)/shard_map/ppermute | solution.py:295
  54.9 32.2 %all-to-all-start.1 = ((bf16[64,48,128]{2,1,0:T(8,128)(2,1)}), bf16[64,48,128]{2,1,0:T(8,128)(2,1)S(1)}, u32[]{:S(2)}, u32[]{:S(2)}) async-start(bf16[64,48,128]{2,1,0:T(8,128)(2,1)} %shard_map.89), calls=%async_computation.1 | async-start | bytes 1572864 | tf_op jit(solution)/shard_map/all_to_all | solution.py:279
  63.5 10.9 %collective-permute-start.11 = (f32[80,128]{1,0:T(8,128)S(1)}, f32[80,128]{1,0:T(8,128)S(1)}, u32[]{:S(2)}, u32[]{:S(2)}) collective-permute-start(f32[80,128]{1,0:T(8,128)S(1)} %reduce_sum.9), channel_id=1, source_target_pairs={{0,32},{32,0},{64,96},{96,64},{128,160},{160,128},{192,224},{224,1... | collective-permute-start | bytes 122888 | tf_op jit(solution)/shard_map/ppermute | solution.py:264
  69.0 25.1 %collective-permute-start.8 = (bf16[320,1536]{1,0:T(8,128)(2,1)}, bf16[320,1536]{1,0:T(8,128)(2,1)}, u32[]{:S(2)}, u32[]{:S(2)}) collective-permute-start(bf16[320,1536]{1,0:T(8,128)(2,1)} %collective-permute-done.6.refs_2_), channel_id=1, source_target_pairs={{0,224},{32,0},{64,32},{96,64},{128,96},{160,128},{192,160},{224,1... | collective-permute-start | bytes 2949128 | tf_op jit(solution)/shard_map/ppermute | solution.py:301
  71.0 24.7 %collective-permute-start.7 = (bf16[320,1536]{1,0:T(8,128)(2,1)}, bf16[320,1536]{1,0:T(8,128)(2,1)}, u32[]{:S(2)}, u32[]{:S(2)}) collective-permute-start(bf16[320,1536]{1,0:T(8,128)(2,1)} %collective-permute-done.5.refs_1_), channel_id=1, source_target_pairs={{0,32},{32,64},{64,96},{96,128},{128,160},{160,192},{192,224},{224... | collective-permute-start | bytes 2949128 | tf_op jit(solution)/shard_map/ppermute | solution.py:300
  74.4 19.8 %collective-permute-start.12 = (f32[80,128]{1,0:T(8,128)S(1)}, f32[80,128]{1,0:T(8,128)S(1)}, u32[]{:S(2)}, u32[]{:S(2)}) collective-permute-start(f32[80,128]{1,0:T(8,128)S(1)} %add.12), channel_id=1, source_target_pairs={{0,64},{32,96},{64,0},{96,32},{128,192},{160,224},{192,128},{224,1... | collective-permute-start | bytes 122888 | tf_op jit(solution)/shard_map/ppermute | solution.py:264
  87.0 26.2 %all-to-all-start.2 = ((bf16[64,32,128]{2,1,0:T(8,128)(2,1)}), bf16[64,32,128]{2,1,0:T(8,128)(2,1)S(1)}, u32[]{:S(2)}, u32[]{:S(2)}) async-start(bf16[64,32,128]{2,1,0:T(8,128)(2,1)} %shard_map.91.refs_2_), calls=%async_computation.2 | async-start | bytes 1048576 | tf_op jit(solution)/shard_map/all_to_all | solution.py:279
  96.8 11.7 %collective-permute-start.10 = (bf16[160,1536]{1,0:T(8,128)(2,1)S(1)}, bf16[160,1536]{1,0:T(8,128)(2,1)S(1)}, u32[]{:S(2)}, u32[]{:S(2)}) collective-permute-start(bf16[160,1536]{1,0:T(8,128)(2,1)S(1)} %get-tuple-element.18), channel_id=1, source_target_pairs={{0,224},{32,0},{64,32},{96,64},{128,96},{160,128},{192,160},{224,1... | collective-permute-start | bytes 1474568 | tf_op jit(solution)/shard_map/ppermute | solution.py:315
  99.2 12.0 %collective-permute-start.9 = (bf16[160,1536]{1,0:T(8,128)(2,1)S(1)}, bf16[160,1536]{1,0:T(8,128)(2,1)S(1)}, u32[]{:S(2)}, u32[]{:S(2)}) collective-permute-start(bf16[160,1536]{1,0:T(8,128)(2,1)S(1)} %get-tuple-element.17), channel_id=1, source_target_pairs={{0,32},{32,64},{64,96},{96,128},{128,160},{160,192},{192,224},{224... | collective-permute-start | bytes 1474568 | tf_op jit(solution)/shard_map/ppermute | solution.py:314
  113.2 27.9 %copy-start.4 = (f32[128,6]{0,1:T(8,128)S(1)}, f32[128,6]{0,1:T(8,128)}, u32[]{:S(2)}) copy-start(f32[128,6]{0,1:T(8,128)} %param.8) | copy-start | bytes 9220
  113.2 28.0 %copy-start.5 = (s32[128,6]{0,1:T(8,128)S(1)}, s32[128,6]{0,1:T(8,128)}, u32[]{:S(2)}) copy-start(s32[128,6]{0,1:T(8,128)} %param.7) | copy-start | bytes 9220
  113.2 38.6 %copy-start.1 = (bf16[64,5120]{1,0:T(8,128)(2,1)S(1)}, bf16[64,5120]{1,0:T(8,128)(2,1)}, u32[]{:S(2)}) copy-start(bf16[64,5120]{1,0:T(8,128)(2,1)} %refs_3_.1) | copy-start | bytes 1966084
  113.2 38.6 %all-to-all-start.3 = ((bf16[64,48,128]{2,1,0:T(8,128)(2,1)}), bf16[64,48,128]{2,1,0:T(8,128)(2,1)S(1)}, u32[]{:S(2)}, u32[]{:S(2)}) async-start(bf16[64,48,128]{2,1,0:T(8,128)(2,1)} %shard_map.94), calls=%async_computation.3 | async-start | bytes 1572864 | tf_op jit(solution)/shard_map/all_to_all | solution.py:279
  128.3 9.4 %collective-permute-start.13 = (f32[80,128]{1,0:T(8,128)S(1)}, f32[80,128]{1,0:T(8,128)S(1)}, u32[]{:S(2)}, u32[]{:S(2)}) collective-permute-start(f32[80,128]{1,0:T(8,128)S(1)} %add.13.refs_4_), channel_id=1, source_target_pairs={{0,128},{32,160},{64,192},{96,224},{128,0},{160,32},{192,64},{224,... | collective-permute-start | bytes 122888 | tf_op jit(solution)/shard_map/ppermute | solution.py:264
  137.7 10.4 %collective-permute-start.14 = (f32[80,128]{1,0:T(8,128)S(1)}, f32[80,128]{1,0:T(8,128)S(1)}, u32[]{:S(2)}, u32[]{:S(2)}) collective-permute-start(f32[80,128]{1,0:T(8,128)S(1)} %add.14), channel_id=1, source_target_pairs={{0,256},{256,0},{1,257},{257,1},{2,258},{258,2},{3,259},{259,3},{4... | collective-permute-start | bytes 122888 | tf_op jit(solution)/shard_map/ppermute | solution.py:332

commit v5 on v4

--- a/solution.py
+++ b/solution.py
@@ -44,7 +44,7 @@
 
 
 def partial_kernel(places, core_ref, normed_ref, key_ref, other_normed_ref, other_key_ref, out_ref):
-    dims = (((0,), (0,)), ((), ()))
+    dims = (((1,), (0,)), ((), ()))
     product = lax.dot_general(
         key_ref[...], normed_ref[...], dims, preferred_element_type=jnp.float32
     ) + lax.dot_general(
@@ -177,17 +177,22 @@
     chunks, (out_ref, pieces_ref, lines_ref) = refs[:-3], refs[-3:]
     pairs, ring, tokens, piece = pieces_ref.shape
     z = z_ref[0]
+    side = 1 - 2 * lax.rem(z, 2)
     for chunk, distances in zip(chunks, layout):
         for g, routed in enumerate(routed_sums(capacity, combine_ref[...], chunk, lines_ref)):
             for start, distance in distances:
-                pieces_ref[g, distance % ring] = routed[:, start : start + piece]
+                there = lax.rem(distance * side + ring, ring)
+                pieces_ref[g, there] = routed[:, start : start + piece]
     for g in range(pairs):
         for h in range(ring // 2):
             left = pieces_ref[g, lax.rem(2 * h - z + ring, ring)]
             right = pieces_ref[g, lax.rem(2 * h + 1 - z + ring, ring)]
             columns = slice((g * ring + 2 * h) * piece, (g * ring + 2 * h + 2) * piece)
-            attention = jnp.dot(
-                key_ref[...], rope_ref[:, columns], preferred_element_type=jnp.float32
+            attention = lax.dot_general(
+                key_ref[...],
+                rope_ref[:, columns],
+                (((0,), (0,)), ((), ())),
+                preferred_element_type=jnp.float32,
             )
             routed = jnp.concatenate([left, right], axis=1)
             out_ref[:, columns] = (routed + attention).astype(out_ref.dtype)
@@ -204,14 +209,15 @@
     capacity = slot_rows.shape[0] // experts_here
     piece = projection.shape[0]
     tokens, key_size = key_grad.shape
+    key_lines = key_grad.T
     width = piece * groups
     share = width // experts_here
     last = ring // 2
     rows = experts_here * PAD
     z = lax.axis_index("z").astype(jnp.int32).reshape(1)
     low = (lax.axis_index("ylo") == 0).astype(jnp.int32).reshape(1)
-    up = [(i, (i + 1) % ring) for i in range(ring)]
-    down = [(i, (i - 1) % ring) for i in range(ring)]
+    inner = [(i, (i + 1 - 2 * (i % 2)) % ring) for i in range(ring)]
+    outer = [(i, (i - 1 + 2 * (i % 2)) % ring) for i in range(ring)]
 
     packed = key_size * share // 128
     cores = lax.axis_size("core")
@@ -228,12 +234,11 @@
     )(
         lax.axis_index("core").astype(jnp.int32).reshape(1),
         normed,
-        key_grad,
+        key_lines,
         lax.ppermute(normed, "core", swap),
-        lax.ppermute(key_grad, "core", swap),
+        lax.ppermute(key_lines, "core", swap),
     )
     terms = lax.all_to_all(mine, ("x", "yhi"), split_axis=0, concat_axis=0, tiled=True)
-    mine = jnp.sum(terms, axis=0)
 
     other = lax.ppermute(slot_rows, "ylo", swap)
 
@@ -284,21 +289,25 @@
         ((0, -2), (piece, 2)),
         ((0, -3), (piece, 3), (2 * piece, 4)),
     )
-    below, above = [projection], [projection]
-    below.append(lax.ppermute(below[-1], "z", up))
-    above.append(lax.ppermute(above[-1], "z", down))
+    paired, crossed = [projection], [projection]
+    came = lax.ppermute(crossed[-1], "z", inner), lax.ppermute(paired[-1], "z", outer)
+    paired.append(came[0])
+    crossed.append(came[1])
     both = spaced_rows(other)
     begun = products([projection], 1 * 10**9)
-    below[1], above[1], begun = lax.optimization_barrier((below[1], above[1], begun))
-    first = more_products(begun, piece, [below[1], above[1]], 2 * 10**9)
-    first, mine = lax.optimization_barrier((first, mine))
-    below.append(lax.ppermute(below[-1], "z", up))
-    above.append(lax.ppermute(above[-1], "z", down))
-    below[2], _ = lax.optimization_barrier((below[2], first))
-    above[2], _ = lax.optimization_barrier((above[2], first))
-    second = products([below[2], above[2]], 15 * 10**9)
-    below.append(lax.ppermute(below[-1], "z", up))
-    above.append(lax.ppermute(above[-1], "z", down))
+    crossed[1], paired[1], begun = lax.optimization_barrier((crossed[1], paired[1], begun))
+    first = more_products(begun, piece, [crossed[1], paired[1]], 2 * 10**9)
+    first, terms = lax.optimization_barrier((first, terms))
+    mine = jnp.sum(terms, axis=0)
+    came = lax.ppermute(crossed[-1], "z", inner), lax.ppermute(paired[-1], "z", outer)
+    paired.append(came[0])
+    crossed.append(came[1])
+    crossed[2], _ = lax.optimization_barrier((crossed[2], first))
+    paired[2], _ = lax.optimization_barrier((paired[2], first))
+    second = products([crossed[2], paired[2]], 15 * 10**9)
+    came = lax.ppermute(crossed[-1], "z", inner), lax.ppermute(paired[-1], "z", outer)
+    paired.append(came[0])
+    crossed.append(came[1])
     sent = [send(first)]
     half = piece // 2
     half_low, half_high = call(
@@ -310,12 +319,12 @@
         [pltpu.SemaphoreType.DMA((2,))],
         [second] + sent,
         ANY,
-    )(below[-1], above[-1])
-    last_low = lax.ppermute(half_low, "z", up)
-    last_high = lax.ppermute(half_high, "z", down)
+    )(crossed[-1], paired[-1])
+    last_low = lax.ppermute(half_low, "z", inner)
+    last_high = lax.ppermute(half_high, "z", outer)
     sent.append(send(second))
     two = added(added(mine, 1), 2)
-    begun = products([below[3], above[3]], 10 * 10**9)
+    begun = products([crossed[3], paired[3]], 10 * 10**9)
     third = more_products(begun, 2 * piece, [last_low, last_high], 1 * 10**9, [two])
     chunks = sent + [send(third)]
 
@@ -346,7 +355,7 @@
         4 * 10**8,
         6 * 10**6,
         [pltpu.VMEM((pairs, ring, tokens, piece), jnp.float32), lines],
-    )(z, combine, key_grad, rope_weight, *chunks)
+    )(z, combine, key_lines, rope_weight, *chunks)
     return (token_grad, rope_grad)
 
 

time: 155 us -> 155 us (level)
    ppermute x9, starting transfers between devices: 27.5 us -> 24.7 us  [the longest x3 9.33 us: body(): lax.ppermute(paired[-1], 'z', outer)]
    ppermute x9, waiting for transfers between devices: 11.5 us -> 9.23 us  [the longest x1 3.09 us: body(): last_low = lax.ppermute(half_low, 'z', inner)]
    ppermute x3, starting transfers between devices: 9.34 us -> 11 us  [added(): return sums + lax.ppermute(sums, 'z', [(i, i ^ bit) for i in range(ring)])]
  transfers between devices with their start and end apart: 19 -> 19, of which waited for: 11 -> 10; matrix products, arithmetic and copies ran while one was open for 1% -> 1% of each run, Pallas kernels for 13% -> 13%
where the time goes in v5:
time: 155 us; the launch traced here: 154 us
  starting transfers between devices  90.5 us (58%)
  waiting for transfers between devices  35.5 us (23%)
  Pallas kernels  22.5 us (15%)
  local copies, waits for them, and re-layouts  2.9 us (2%)
    all_to_all x3, starting transfers between devices, send(): lax.all_to_all(computed, PLANE, split_axis=0, concat_axis=0, tiled=True)  30.8 us
    pallas_call x11, Pallas kernels, call(): return lambda *args: run(*args, *after)  22.5 us
    ppermute x3, starting transfers between devices, added(): return sums + lax.ppermute(sums, 'z', [(i, i ^ bit) for i in range(ring)])  11 us
    ppermute x3, starting transfers between devices, body(): lax.ppermute(paired[-1], 'z', outer)  9.33 us
    ppermute x1, starting transfers between devices, body(): lax.ppermute(normed, 'core', swap)  8.79 us
    all_to_all x3, waiting for transfers between devices, send(): lax.all_to_all(computed, PLANE, split_axis=0, concat_axis=0, tiled=True)  8.74 us
    all_to_all x1, starting transfers between devices, body(): lax.all_to_all(mine, ('x', 'yhi'), split_axis=0, concat_axis=0, tiled=True)  8.67 us
    ppermute x1, waiting for transfers between devices, body(): summed = summed + lax.ppermute(summed, 'ylo', swap)  6.72 us
  transfers between devices with their start and end apart: 19, of which 10 were waited for; matrix products, arithmetic and copies ran while one was open for 1% of the time, Pallas kernels for 13%

profile of v5, /device:TPU:1, one launch (start us, length us, event | category | flops | bytes accessed | tf_op | source)
XLA Modules:
  0.0 153.6 jit_solution(5925091163596206987)
XLA Ops:
  0.6 8.8 %collective-permute-start.3 = (bf16[128,5120]{1,0:T(8,128)(2,1)}, bf16[128,5120]{1,0:T(8,128)(2,1)S(1)}, u32[]{:S(2)}, u32[]{:S(2)}) collective-permute-start(bf16[128,5120]{1,0:T(8,128)(2,1)} %refs_1_.2), channel_id=1, source_target_pairs={{0,1},{1,0},{2,3},{3,2},{4,5},{5,4},{6,7},{7,6},{8,9},{9,8},{10,11... | collective-permute-start | bytes 3932168 | tf_op jit(solution)/shard_map/ppermute | solution.py:238
  9.4 5.3 %collective-permute-start.1 = (bf16[320,1536]{1,0:T(8,128)(2,1)}, bf16[320,1536]{1,0:T(8,128)(2,1)}, u32[]{:S(2)}, u32[]{:S(2)}) collective-permute-start(bf16[320,1536]{1,0:T(8,128)(2,1)} %bitcast.17), channel_id=1, source_target_pairs={{0,224},{32,64},{64,32},{96,128},{128,96},{160,192},{192,160},{224... | collective-permute-start | bytes 2949128 | tf_op jit(solution)/shard_map/ppermute | solution.py:293
  14.7 1.9 %collective-permute-start.2 = (bf16[320,1536]{1,0:T(8,128)(2,1)}, bf16[320,1536]{1,0:T(8,128)(2,1)}, u32[]{:S(2)}, u32[]{:S(2)}) collective-permute-start(bf16[320,1536]{1,0:T(8,128)(2,1)} %bitcast.18), channel_id=1, source_target_pairs={{0,32},{32,0},{64,96},{96,64},{128,160},{160,128},{192,224},{224,1... | collective-permute-start | bytes 2949128 | tf_op jit(solution)/shard_map/ppermute | solution.py:293
  16.7 3.2 %collective-permute-start = (bf16[192,1536]{1,0:T(8,128)(2,1)}, bf16[192,1536]{1,0:T(8,128)(2,1)S(1)}, u32[]{:S(2)}, u32[]{:S(2)}) collective-permute-start(bf16[192,1536]{1,0:T(8,128)(2,1)} %bitcast.12), channel_id=1, source_target_pairs={{0,256},{256,0},{1,257},{257,1},{2,258},{258,2},{3,259},{259,3},{4... | collective-permute-start | bytes 1769480 | tf_op jit(solution)/shard_map/ppermute | solution.py:243
  19.9 2.5 %collective-permute-start.4 = (bf16[64,128]{1,0:T(8,128)(2,1)}, bf16[64,128]{1,0:T(8,128)(2,1)S(1)}, u32[]{:S(2)}, u32[]{:S(2)}) collective-permute-start(bf16[64,128]{1,0:T(8,128)(2,1)} %bitcast.14), channel_id=1, source_target_pairs={{0,1},{1,0},{2,3},{3,2},{4,5},{5,4},{6,7},{7,6},{8,9},{9,8},{10,11... | collective-permute-start | bytes 49160 | tf_op jit(solution)/shard_map/ppermute | solution.py:239
  27.2 8.7 %all-to-all-start = ((f32[16,80,128]{2,1,0:T(8,128)}), f32[16,80,128]{2,1,0:T(8,128)}, u32[]{:S(2)}, u32[]{:S(2)}) async-start(f32[16,80,128]{2,1,0:T(8,128)} %shard_map.90), calls=%async_computation | async-start | bytes 1310720 | tf_op jit(solution)/shard_map/all_to_all | solution.py:241
  38.2 1.8 %collective-permute-done.2.refs_3_ = bf16[320,1536]{1,0:T(8,128)(2,1)} collective-permute-done((bf16[320,1536]{1,0:T(8,128)(2,1)}, bf16[320,1536]{1,0:T(8,128)(2,1)}, u32[]{:S(2)}, u32[]{:S(2)}) %collective-permute-start.2) | collective-permute-done | bytes 983072 | tf_op jit(solution)/shard_map/ppermute | solution.py:293
  40.0 2.2 %collective-permute-start.6 = (bf16[320,1536]{1,0:T(8,128)(2,1)}, bf16[320,1536]{1,0:T(8,128)(2,1)}, u32[]{:S(2)}, u32[]{:S(2)}) collective-permute-start(bf16[320,1536]{1,0:T(8,128)(2,1)} %collective-permute-done.1.refs_2_), channel_id=1, source_target_pairs={{0,32},{32,0},{64,96},{96,64},{128,160},{160,128},{192,224},{224,1... | collective-permute-start | bytes 2949128 | tf_op jit(solution)/shard_map/ppermute | solution.py:302
  42.2 2.1 %collective-permute-start.5 = (bf16[320,1536]{1,0:T(8,128)(2,1)}, bf16[320,1536]{1,0:T(8,128)(2,1)}, u32[]{:S(2)}, u32[]{:S(2)}) collective-permute-start(bf16[320,1536]{1,0:T(8,128)(2,1)} %collective-permute-done.2.refs_3_), channel_id=1, source_target_pairs={{0,224},{32,64},{64,32},{96,128},{128,96},{160,192},{192,160},{224... | collective-permute-start | bytes 2949128 | tf_op jit(solution)/shard_map/ppermute | solution.py:302
  44.4 4.4 %shard_map.89 = bf16[64,48,128]{2,1,0:T(8,128)(2,1)} custom-call(bf16[512,1536]{1,0:T(8,128)(2,1)S(1)} %bitcast.8, bf16[64,32,128]{2,1,0:T(8,128)(2,1)S(1)} %shard_map.88.refs_1_, bf16[320,1536]{1,0:T(8,128)(2,1)} %collective-permute-done.1.refs_2_, bf16[320,1536]{1,0:T(8,128)(2,1)} %collective-permute-done.2.refs_3_), custom_call_target="tpu_custom_call" | custom-call | flops 2000000000 | bytes 3000000 | tf_op jit(solution)/shard_map/pallas_call | solution.py:39
  48.7 5.1 %all-to-all-done = f32[16,80,128]{2,1,0:T(8,128)} async-done(((f32[16,80,128]{2,1,0:T(8,128)}), f32[16,80,128]{2,1,0:T(8,128)}, u32[]{:S(2)}, u32[]{:S(2)}) %all-to-all-start) | async-done | bytes 655392 | tf_op jit(solution)/shard_map/all_to_all | solution.py:241
  53.8 8.6 %all-to-all-start.1 = ((bf16[64,48,128]{2,1,0:T(8,128)(2,1)}), bf16[64,48,128]{2,1,0:T(8,128)(2,1)S(1)}, u32[]{:S(2)}, u32[]{:S(2)}) async-start(bf16[64,48,128]{2,1,0:T(8,128)(2,1)} %shard_map.89), calls=%async_computation.1 | async-start | bytes 1572864 | tf_op jit(solution)/shard_map/all_to_all | solution.py:284
  63.5 3.6 %collective-permute-start.11 = (f32[80,128]{1,0:T(8,128)S(1)}, f32[80,128]{1,0:T(8,128)S(1)}, u32[]{:S(2)}, u32[]{:S(2)}) collective-permute-start(f32[80,128]{1,0:T(8,128)S(1)} %reduce_sum.9), channel_id=1, source_target_pairs={{0,32},{32,0},{64,96},{96,64},{128,160},{160,128},{192,224},{224,1... | collective-permute-start | bytes 122888 | tf_op jit(solution)/shard_map/ppermute | solution.py:269
  67.8 1.9 %collective-permute-start.7 = (bf16[320,1536]{1,0:T(8,128)(2,1)}, bf16[320,1536]{1,0:T(8,128)(2,1)}, u32[]{:S(2)}, u32[]{:S(2)}) collective-permute-start(bf16[320,1536]{1,0:T(8,128)(2,1)} %collective-permute-done.6.refs_2_), channel_id=1, source_target_pairs={{0,224},{32,64},{64,32},{96,128},{128,96},{160,192},{192,160},{224... | collective-permute-start | bytes 2949128 | tf_op jit(solution)/shard_map/ppermute | solution.py:308
  69.7 1.9 %collective-permute-start.8 = (bf16[320,1536]{1,0:T(8,128)(2,1)}, bf16[320,1536]{1,0:T(8,128)(2,1)}, u32[]{:S(2)}, u32[]{:S(2)}) collective-permute-start(bf16[320,1536]{1,0:T(8,128)(2,1)} %collective-permute-done.5.refs_1_), channel_id=1, source_target_pairs={{0,32},{32,0},{64,96},{96,64},{128,160},{160,128},{192,224},{224,1... | collective-permute-start | bytes 2949128 | tf_op jit(solution)/shard_map/ppermute | solution.py:308
  71.7 4.2 %collective-permute-start.12 = (f32[80,128]{1,0:T(8,128)S(1)}, f32[80,128]{1,0:T(8,128)S(1)}, u32[]{:S(2)}, u32[]{:S(2)}) collective-permute-start(f32[80,128]{1,0:T(8,128)S(1)} %add.12), channel_id=1, source_target_pairs={{0,64},{32,96},{64,0},{96,32},{128,192},{160,224},{192,128},{224,1... | collective-permute-start | bytes 122888 | tf_op jit(solution)/shard_map/ppermute | solution.py:269
  75.9 4.3 %shard_map.91.refs_2_ = bf16[64,32,128]{2,1,0:T(8,128)(2,1)} custom-call(bf16[512,1536]{1,0:T(8,128)(2,1)S(1)} %bitcast.9, bf16[320,1536]{1,0:T(8,128)(2,1)} %collective-permute-done.5.refs_1_, bf16[320,1536]{1,0:T(8,128)(2,1)} %collective-permute-done.6.refs_2_), custom_call_target="tpu_custom_call" | custom-call | flops 15000000512 | bytes 4000000 | tf_op jit(solution)/shard_map/pallas_call | solution.py:39
  80.1 5.8 %all-to-all-done.1.refs_3_.refs_4_ = bf16[64,48,128]{2,1,0:T(8,128)(2,1)S(1)} async-done(((bf16[64,48,128]{2,1,0:T(8,128)(2,1)}), bf16[64,48,128]{2,1,0:T(8,128)(2,1)S(1)}, u32[]{:S(2)}, u32[]{:S(2)}) %all-to-all-start.1) | async-done | bytes 786464 | tf_op jit(solution)/shard_map/all_to_all | solution.py:284
  85.9 7.5 %all-to-all-start.2 = ((bf16[64,32,128]{2,1,0:T(8,128)(2,1)}), bf16[64,32,128]{2,1,0:T(8,128)(2,1)S(1)}, u32[]{:S(2)}, u32[]{:S(2)}) async-start(bf16[64,32,128]{2,1,0:T(8,128)(2,1)} %shard_map.91.refs_2_), calls=%async_computation.2 | async-start | bytes 1048576 | tf_op jit(solution)/shard_map/all_to_all | solution.py:284
  94.7 4.9 %collective-permute-start.10 = (bf16[160,1536]{1,0:T(8,128)(2,1)S(1)}, bf16[160,1536]{1,0:T(8,128)(2,1)S(1)}, u32[]{:S(2)}, u32[]{:S(2)}) collective-permute-start(bf16[160,1536]{1,0:T(8,128)(2,1)S(1)} %get-tuple-element.18), channel_id=1, source_target_pairs={{0,224},{32,64},{64,32},{96,128},{128,96},{160,192},{192,160},{224... | collective-permute-start | bytes 1474568 | tf_op jit(solution)/shard_map/ppermute | solution.py:324
  99.6 1.9 %collective-permute-start.9 = (bf16[160,1536]{1,0:T(8,128)(2,1)S(1)}, bf16[160,1536]{1,0:T(8,128)(2,1)S(1)}, u32[]{:S(2)}, u32[]{:S(2)}) collective-permute-start(bf16[160,1536]{1,0:T(8,128)(2,1)S(1)} %get-tuple-element.17), channel_id=1, source_target_pairs={{0,32},{32,0},{64,96},{96,64},{128,160},{160,128},{192,224},{224,1... | collective-permute-start | bytes 1474568 | tf_op jit(solution)/shard_map/ppermute | solution.py:323
  101.5 3.5 %shard_map.92.refs_1_ = bf16[64,32,128]{2,1,0:T(8,128)(2,1)S(1)} custom-call(bf16[512,1536]{1,0:T(8,128)(2,1)S(1)} %bitcast.10, bf16[320,1536]{1,0:T(8,128)(2,1)} %collective-permute-done.7.refs_1_.refs_0_, bf16[320,1536]{1,0:T(8,128)(2,1)} %collective-permute-done.8.refs_2_.refs_1_), custom_call_target="tpu_custom_call" | custom-call | flops 10000000000 | bytes 4000000 | tf_op jit(solution)/shard_map/pallas_call | solution.py:39
  105.0 2.6 %collective-permute-done.10.refs_3_ = bf16[160,1536]{1,0:T(8,128)(2,1)S(1)} collective-permute-done((bf16[160,1536]{1,0:T(8,128)(2,1)S(1)}, bf16[160,1536]{1,0:T(8,128)(2,1)S(1)}, u32[]{:S(2)}, u32[]{:S(2)}) %collective-permute-start.10) | collective-permute-done | bytes 491552 | tf_op jit(solution)/shard_map/ppermute | solution.py:324
  107.6 3.1 %collective-permute-done.9.refs_2_ = bf16[160,1536]{1,0:T(8,128)(2,1)S(1)} collective-permute-done((bf16[160,1536]{1,0:T(8,128)(2,1)S(1)}, bf16[160,1536]{1,0:T(8,128)(2,1)S(1)}, u32[]{:S(2)}, u32[]{:S(2)}) %collective-permute-start.9) | collective-permute-done | bytes 491552 | tf_op jit(solution)/shard_map/ppermute | solution.py:323
  110.7 2.0 %shard_map.94 = bf16[64,48,128]{2,1,0:T(8,128)(2,1)} custom-call(bf16[512,1536]{1,0:T(8,128)(2,1)S(1)} %bitcast.11, bf16[64,32,128]{2,1,0:T(8,128)(2,1)S(1)} %shard_map.92.refs_1_, bf16[160,1536]{1,0:T(8,128)(2,1)S(1)} %collective-permute-done.9.refs_2_, bf16[160,1536]{1,0:T(8,128)(2,1)S(1)} %collective-permute-done.10.refs_3_, f32[80,128]{1,0:T(8,128)S(1)} %add.13.refs_4_), custom_call_target="tpu_custom_call" | custom-call | flops 1000000000 | bytes 3000000 | tf_op jit(solution)/shard_map/pallas_call | solution.py:39
  112.8 14.7 %all-to-all-start.3 = ((bf16[64,48,128]{2,1,0:T(8,128)(2,1)}), bf16[64,48,128]{2,1,0:T(8,128)(2,1)S(1)}, u32[]{:S(2)}, u32[]{:S(2)}) async-start(bf16[64,48,128]{2,1,0:T(8,128)(2,1)} %shard_map.94), calls=%async_computation.3 | async-start | bytes 1572864 | tf_op jit(solution)/shard_map/all_to_all | solution.py:284
  127.4 3.2 %collective-permute-start.13 = (f32[80,128]{1,0:T(8,128)S(1)}, f32[80,128]{1,0:T(8,128)S(1)}, u32[]{:S(2)}, u32[]{:S(2)}) collective-permute-start(f32[80,128]{1,0:T(8,128)S(1)} %add.13.refs_4_), channel_id=1, source_target_pairs={{0,128},{32,160},{64,192},{96,224},{128,0},{160,32},{192,64},{224,... | collective-permute-start | bytes 122888 | tf_op jit(solution)/shard_map/ppermute | solution.py:269
  130.6 5.7 %collective-permute-done.13 = f32[80,128]{1,0:T(8,128)S(1)} collective-permute-done((f32[80,128]{1,0:T(8,128)S(1)}, f32[80,128]{1,0:T(8,128)S(1)}, u32[]{:S(2)}, u32[]{:S(2)}) %collective-permute-start.13) | collective-permute-done | bytes 40992 | tf_op jit(solution)/shard_map/ppermute | solution.py:269
  136.4 3.4 %collective-permute-start.14 = (f32[80,128]{1,0:T(8,128)S(1)}, f32[80,128]{1,0:T(8,128)S(1)}, u32[]{:S(2)}, u32[]{:S(2)}) collective-permute-start(f32[80,128]{1,0:T(8,128)S(1)} %add.14), channel_id=1, source_target_pairs={{0,256},{256,0},{1,257},{257,1},{2,258},{258,2},{3,259},{259,3},{4... | collective-permute-start | bytes 122888 | tf_op jit(solution)/shard_map/ppermute | solution.py:341
  140.5 6.7 %collective-permute-done.14 = f32[80,128]{1,0:T(8,128)S(1)} collective-permute-done((f32[80,128]{1,0:T(8,128)S(1)}, f32[80,128]{1,0:T(8,128)S(1)}, u32[]{:S(2)}, u32[]{:S(2)}) %collective-permute-start.14) | collective-permute-done | bytes 40992 | tf_op jit(solution)/shard_map/ppermute | solution.py:341
  148.0 3.0 %all-to-all-done.3.refs_6_ = bf16[64,48,128]{2,1,0:T(8,128)(2,1)S(1)} async-done(((bf16[64,48,128]{2,1,0:T(8,128)(2,1)}), bf16[64,48,128]{2,1,0:T(8,128)(2,1)S(1)}, u32[]{:S(2)}, u32[]{:S(2)}) %all-to-all-start.3) | async-done | bytes 786464 | tf_op jit(solution)/shard_map/all_to_all | solution.py:284
  151.0 2.6 %shard_map.95 = bf16[128,5120]{1,0:T(8,128)(2,1)} custom-call(s32[1]{0:T(128)} %bitcast.refs_0_, bf16[128,256]{1,0:T(8,128)(2,1)S(1)} %shard_map.86.refs_1_, bf16[64,128]{1,0:T(8,128)(2,1)S(1)} %bitcast.16, bf16[64,5120]{1,0:T(8,128)(2,1)S(1)} %copy-done.1, bf16[64,48,128]{2,1,0:T(8,128)(2,1)S(1)} %all-to-all-done.1.refs_3_.refs_4_, ...), custom_call_target="tpu_custom_call" | custom-call | flops 400000000 | bytes 6000000 | tf_op jit(solution)/shard_map/pallas_call | solution.py:39
  (40 shorter events, 11.6 us)
Async XLA Ops:
  0.6 22.8 %collective-permute-start.3 = (bf16[128,5120]{1,0:T(8,128)(2,1)}, bf16[128,5120]{1,0:T(8,128)(2,1)S(1)}, u32[]{:S(2)}, u32[]{:S(2)}) collective-permute-start(bf16[128,5120]{1,0:T(8,128)(2,1)} %refs_1_.2), channel_id=1, source_target_pairs={{0,1},{1,0},{2,3},{3,2},{4,5},{5,4},{6,7},{7,6},{8,9},{9,8},{10,11... | collective-permute-start | bytes 3932168 | tf_op jit(solution)/shard_map/ppermute | solution.py:238
  9.4 28.7 %collective-permute-start.1 = (bf16[320,1536]{1,0:T(8,128)(2,1)}, bf16[320,1536]{1,0:T(8,128)(2,1)}, u32[]{:S(2)}, u32[]{:S(2)}) collective-permute-start(bf16[320,1536]{1,0:T(8,128)(2,1)} %bitcast.17), channel_id=1, source_target_pairs={{0,224},{32,64},{64,32},{96,128},{128,96},{160,192},{192,160},{224... | collective-permute-start | bytes 2949128 | tf_op jit(solution)/shard_map/ppermute | solution.py:293
  14.7 25.3 %collective-permute-start.2 = (bf16[320,1536]{1,0:T(8,128)(2,1)}, bf16[320,1536]{1,0:T(8,128)(2,1)}, u32[]{:S(2)}, u32[]{:S(2)}) collective-permute-start(bf16[320,1536]{1,0:T(8,128)(2,1)} %bitcast.18), channel_id=1, source_target_pairs={{0,32},{32,0},{64,96},{96,64},{128,160},{160,128},{192,224},{224,1... | collective-permute-start | bytes 2949128 | tf_op jit(solution)/shard_map/ppermute | solution.py:293
  16.7 19.2 %collective-permute-start = (bf16[192,1536]{1,0:T(8,128)(2,1)}, bf16[192,1536]{1,0:T(8,128)(2,1)S(1)}, u32[]{:S(2)}, u32[]{:S(2)}) collective-permute-start(bf16[192,1536]{1,0:T(8,128)(2,1)} %bitcast.12), channel_id=1, source_target_pairs={{0,256},{256,0},{1,257},{257,1},{2,258},{258,2},{3,259},{259,3},{4... | collective-permute-start | bytes 1769480 | tf_op jit(solution)/shard_map/ppermute | solution.py:243
  19.9 3.5 %collective-permute-start.4 = (bf16[64,128]{1,0:T(8,128)(2,1)}, bf16[64,128]{1,0:T(8,128)(2,1)S(1)}, u32[]{:S(2)}, u32[]{:S(2)}) collective-permute-start(bf16[64,128]{1,0:T(8,128)(2,1)} %bitcast.14), channel_id=1, source_target_pairs={{0,1},{1,0},{2,3},{3,2},{4,5},{5,4},{6,7},{7,6},{8,9},{9,8},{10,11... | collective-permute-start | bytes 49160 | tf_op jit(solution)/shard_map/ppermute | solution.py:239
  23.4 1.3 copy-start
  24.7 0.7 copy-start.3
  27.2 8.7 %copy-start.2 = (bf16[1,192,1536]{2,1,0:T(8,128)(2,1)S(1)}, bf16[1,192,1536]{2,1,0:T(8,128)(2,1)}, u32[]{:S(2)}) copy-start(bf16[1,192,1536]{2,1,0:T(8,128)(2,1)} %param.9) | copy-start | bytes 1769476
  27.2 26.6 %all-to-all-start = ((f32[16,80,128]{2,1,0:T(8,128)}), f32[16,80,128]{2,1,0:T(8,128)}, u32[]{:S(2)}, u32[]{:S(2)}) async-start(f32[16,80,128]{2,1,0:T(8,128)} %shard_map.90), calls=%async_computation | async-start | bytes 1310720 | tf_op jit(solution)/shard_map/all_to_all | solution.py:241
  35.9 1.2 copy-start.5
  40.0 27.2 %collective-permute-start.6 = (bf16[320,1536]{1,0:T(8,128)(2,1)}, bf16[320,1536]{1,0:T(8,128)(2,1)}, u32[]{:S(2)}, u32[]{:S(2)}) collective-permute-start(bf16[320,1536]{1,0:T(8,128)(2,1)} %collective-permute-done.1.refs_2_), channel_id=1, source_target_pairs={{0,32},{32,0},{64,96},{96,64},{128,160},{160,128},{192,224},{224,1... | collective-permute-start | bytes 2949128 | tf_op jit(solution)/shard_map/ppermute | solution.py:302
  42.2 25.6 %collective-permute-start.5 = (bf16[320,1536]{1,0:T(8,128)(2,1)}, bf16[320,1536]{1,0:T(8,128)(2,1)}, u32[]{:S(2)}, u32[]{:S(2)}) collective-permute-start(bf16[320,1536]{1,0:T(8,128)(2,1)} %collective-permute-done.2.refs_3_), channel_id=1, source_target_pairs={{0,224},{32,64},{64,32},{96,128},{128,96},{160,192},{192,160},{224... | collective-permute-start | bytes 2949128 | tf_op jit(solution)/shard_map/ppermute | solution.py:302
  53.8 32.1 %all-to-all-start.1 = ((bf16[64,48,128]{2,1,0:T(8,128)(2,1)}), bf16[64,48,128]{2,1,0:T(8,128)(2,1)S(1)}, u32[]{:S(2)}, u32[]{:S(2)}) async-start(bf16[64,48,128]{2,1,0:T(8,128)(2,1)} %shard_map.89), calls=%async_computation.1 | async-start | bytes 1572864 | tf_op jit(solution)/shard_map/all_to_all | solution.py:284
  63.5 8.2 %collective-permute-start.11 = (f32[80,128]{1,0:T(8,128)S(1)}, f32[80,128]{1,0:T(8,128)S(1)}, u32[]{:S(2)}, u32[]{:S(2)}) collective-permute-start(f32[80,128]{1,0:T(8,128)S(1)} %reduce_sum.9), channel_id=1, source_target_pairs={{0,32},{32,0},{64,96},{96,64},{128,160},{160,128},{192,224},{224,1... | collective-permute-start | bytes 122888 | tf_op jit(solution)/shard_map/ppermute | solution.py:269
  67.8 25.6 %collective-permute-start.7 = (bf16[320,1536]{1,0:T(8,128)(2,1)}, bf16[320,1536]{1,0:T(8,128)(2,1)}, u32[]{:S(2)}, u32[]{:S(2)}) collective-permute-start(bf16[320,1536]{1,0:T(8,128)(2,1)} %collective-permute-done.6.refs_2_), channel_id=1, source_target_pairs={{0,224},{32,64},{64,32},{96,128},{128,96},{160,192},{192,160},{224... | collective-permute-start | bytes 2949128 | tf_op jit(solution)/shard_map/ppermute | solution.py:308
  69.7 23.7 %collective-permute-start.8 = (bf16[320,1536]{1,0:T(8,128)(2,1)}, bf16[320,1536]{1,0:T(8,128)(2,1)}, u32[]{:S(2)}, u32[]{:S(2)}) collective-permute-start(bf16[320,1536]{1,0:T(8,128)(2,1)} %collective-permute-done.5.refs_1_), channel_id=1, source_target_pairs={{0,32},{32,0},{64,96},{96,64},{128,160},{160,128},{192,224},{224,1... | collective-permute-start | bytes 2949128 | tf_op jit(solution)/shard_map/ppermute | solution.py:308
  71.7 21.7 %collective-permute-start.12 = (f32[80,128]{1,0:T(8,128)S(1)}, f32[80,128]{1,0:T(8,128)S(1)}, u32[]{:S(2)}, u32[]{:S(2)}) collective-permute-start(f32[80,128]{1,0:T(8,128)S(1)} %add.12), channel_id=1, source_target_pairs={{0,64},{32,96},{64,0},{96,32},{128,192},{160,224},{192,128},{224,1... | collective-permute-start | bytes 122888 | tf_op jit(solution)/shard_map/ppermute | solution.py:269
  85.9 26.9 %all-to-all-start.2 = ((bf16[64,32,128]{2,1,0:T(8,128)(2,1)}), bf16[64,32,128]{2,1,0:T(8,128)(2,1)S(1)}, u32[]{:S(2)}, u32[]{:S(2)}) async-start(bf16[64,32,128]{2,1,0:T(8,128)(2,1)} %shard_map.91.refs_2_), calls=%async_computation.2 | async-start | bytes 1048576 | tf_op jit(solution)/shard_map/all_to_all | solution.py:284
  94.7 12.9 %collective-permute-start.10 = (bf16[160,1536]{1,0:T(8,128)(2,1)S(1)}, bf16[160,1536]{1,0:T(8,128)(2,1)S(1)}, u32[]{:S(2)}, u32[]{:S(2)}) collective-permute-start(bf16[160,1536]{1,0:T(8,128)(2,1)S(1)} %get-tuple-element.18), channel_id=1, source_target_pairs={{0,224},{32,64},{64,32},{96,128},{128,96},{160,192},{192,160},{224... | collective-permute-start | bytes 1474568 | tf_op jit(solution)/shard_map/ppermute | solution.py:324
  99.6 11.1 %collective-permute-start.9 = (bf16[160,1536]{1,0:T(8,128)(2,1)S(1)}, bf16[160,1536]{1,0:T(8,128)(2,1)S(1)}, u32[]{:S(2)}, u32[]{:S(2)}) collective-permute-start(bf16[160,1536]{1,0:T(8,128)(2,1)S(1)} %get-tuple-element.17), channel_id=1, source_target_pairs={{0,32},{32,0},{64,96},{96,64},{128,160},{160,128},{192,224},{224,1... | collective-permute-start | bytes 1474568 | tf_op jit(solution)/shard_map/ppermute | solution.py:323
  112.7 27.0 %copy-start.6 = (f32[128,6]{0,1:T(8,128)S(1)}, f32[128,6]{0,1:T(8,128)}, u32[]{:S(2)}) copy-start(f32[128,6]{0,1:T(8,128)} %param.8) | copy-start | bytes 9220
  112.7 27.2 %copy-start.7 = (s32[128,6]{0,1:T(8,128)S(1)}, s32[128,6]{0,1:T(8,128)}, u32[]{:S(2)}) copy-start(s32[128,6]{0,1:T(8,128)} %param.7) | copy-start | bytes 9220
  112.7 38.2 %copy-start.1 = (bf16[64,5120]{1,0:T(8,128)(2,1)S(1)}, bf16[64,5120]{1,0:T(8,128)(2,1)}, u32[]{:S(2)}) copy-start(bf16[64,5120]{1,0:T(8,128)(2,1)} %refs_3_.1) | copy-start | bytes 1966084
  112.7 38.2 %copy-start.4 = (bf16[128,64]{0,1:T(8,128)(2,1)S(1)}, bf16[128,64]{0,1:T(8,128)(2,1)}, u32[]{:S(2)}) copy-start(bf16[128,64]{0,1:T(8,128)(2,1)} %param.12) | copy-start | bytes 49156
  112.8 38.2 %all-to-all-start.3 = ((bf16[64,48,128]{2,1,0:T(8,128)(2,1)}), bf16[64,48,128]{2,1,0:T(8,128)(2,1)S(1)}, u32[]{:S(2)}, u32[]{:S(2)}) async-start(bf16[64,48,128]{2,1,0:T(8,128)(2,1)} %shard_map.94), calls=%async_computation.3 | async-start | bytes 1572864 | tf_op jit(solution)/shard_map/all_to_all | solution.py:284
  127.4 8.9 %collective-permute-start.13 = (f32[80,128]{1,0:T(8,128)S(1)}, f32[80,128]{1,0:T(8,128)S(1)}, u32[]{:S(2)}, u32[]{:S(2)}) collective-permute-start(f32[80,128]{1,0:T(8,128)S(1)} %add.13.refs_4_), channel_id=1, source_target_pairs={{0,128},{32,160},{64,192},{96,224},{128,0},{160,32},{192,64},{224,... | collective-permute-start | bytes 122888 | tf_op jit(solution)/shard_map/ppermute | solution.py:269
  136.4 10.9 %collective-permute-start.14 = (f32[80,128]{1,0:T(8,128)S(1)}, f32[80,128]{1,0:T(8,128)S(1)}, u32[]{:S(2)}, u32[]{:S(2)}) collective-permute-start(f32[80,128]{1,0:T(8,128)S(1)} %add.14), channel_id=1, source_target_pairs={{0,256},{256,0},{1,257},{257,1},{2,258},{258,2},{3,259},{259,3},{4... | collective-permute-start | bytes 122888 | tf_op jit(solution)/shard_map/ppermute | solution.py:341

commit v6 on v5

--- a/solution.py
+++ b/solution.py
@@ -174,7 +174,7 @@
 
 
 def finish_kernel(capacity, layout, z_ref, combine_ref, key_ref, rope_ref, *refs):
-    chunks, (out_ref, pieces_ref, lines_ref) = refs[:-3], refs[-3:]
+    chunks, (out_ref, pieces_ref, lines_ref, ready_ref, semaphores) = refs[:-5], refs[-5:]
     pairs, ring, tokens, piece = pieces_ref.shape
     z = z_ref[0]
     side = 1 - 2 * lax.rem(z, 2)
@@ -183,6 +183,7 @@
             for start, distance in distances:
                 there = lax.rem(distance * side + ring, ring)
                 pieces_ref[g, there] = routed[:, start : start + piece]
+    copies = []
     for g in range(pairs):
         for h in range(ring // 2):
             left = pieces_ref[g, lax.rem(2 * h - z + ring, ring)]
@@ -195,7 +196,14 @@
                 preferred_element_type=jnp.float32,
             )
             routed = jnp.concatenate([left, right], axis=1)
-            out_ref[:, columns] = (routed + attention).astype(out_ref.dtype)
+            ready_ref[:, columns] = (routed + attention).astype(ready_ref.dtype)
+            copy = pltpu.make_async_copy(
+                ready_ref.at[:, columns], out_ref.at[:, columns], semaphores.at[len(copies)]
+            )
+            copy.start()
+            copies.append(copy)
+    for copy in copies:
+        copy.wait()
 
 
 def body(routes, route_weights, hidden_grads, expert_weight, normed, key_grad, rope_weight):
@@ -354,7 +362,14 @@
         [SMEM] + [VMEM] * (3 + len(chunks)),
         4 * 10**8,
         6 * 10**6,
-        [pltpu.VMEM((pairs, ring, tokens, piece), jnp.float32), lines],
+        [
+            pltpu.VMEM((pairs, ring, tokens, piece), jnp.float32),
+            lines,
+            pltpu.VMEM((tokens, width), jnp.bfloat16),
+            pltpu.SemaphoreType.DMA((pairs * ring // 2,)),
+        ],
+        (),
+        ANY,
     )(z, combine, key_lines, rope_weight, *chunks)
     return (token_grad, rope_grad)
 

time: 155 us -> 154 us (level)
  no operation moved by 1% of the time
where the time goes in v6:
time: 154 us; the launch traced here: 153 us
  starting transfers between devices  90.5 us (59%)
  waiting for transfers between devices  35.5 us (23%)
  Pallas kernels  22.2 us (14%)
  local copies, waits for them, and re-layouts  2.9 us (2%)
    all_to_all x3, starting transfers between devices, send(): lax.all_to_all(computed, PLANE, split_axis=0, concat_axis=0, tiled=True)  30.8 us
    pallas_call x11, Pallas kernels, call(): return lambda *args: run(*args, *after)  22.2 us
    ppermute x3, starting transfers between devices, added(): return sums + lax.ppermute(sums, 'z', [(i, i ^ bit) for i in range(ring)])  11 us
    ppermute x3, starting transfers between devices, body(): lax.ppermute(paired[-1], 'z', outer)  9.33 us
    ppermute x1, starting transfers between devices, body(): lax.ppermute(normed, 'core', swap)  8.79 us
    all_to_all x3, waiting for transfers between devices, send(): lax.all_to_all(computed, PLANE, split_axis=0, concat_axis=0, tiled=True)  8.74 us
    all_to_all x1, starting transfers between devices, body(): lax.all_to_all(mine, ('x', 'yhi'), split_axis=0, concat_axis=0, tiled=True)  8.67 us
    ppermute x1, waiting for transfers between devices, body(): summed = summed + lax.ppermute(summed, 'ylo', swap)  6.72 us
  transfers between devices with their start and end apart: 19, of which 10 were waited for; matrix products, arithmetic and copies ran while one was open for 1% of the time, Pallas kernels for 13%

profile of v6, /device:TPU:1, one launch (start us, length us, event | category | flops | bytes accessed | tf_op | source)
XLA Modules:
  0.0 153.3 jit_solution(7508529133212514813)
XLA Ops:
  0.6 8.8 %collective-permute-start.3 = (bf16[128,5120]{1,0:T(8,128)(2,1)}, bf16[128,5120]{1,0:T(8,128)(2,1)S(1)}, u32[]{:S(2)}, u32[]{:S(2)}) collective-permute-start(bf16[128,5120]{1,0:T(8,128)(2,1)} %refs_1_.2), channel_id=1, source_target_pairs={{0,1},{1,0},{2,3},{3,2},{4,5},{5,4},{6,7},{7,6},{8,9},{9,8},{10,11... | collective-permute-start | bytes 3932168 | tf_op jit(solution)/shard_map/ppermute | solution.py:246
  9.4 5.3 %collective-permute-start.1 = (bf16[320,1536]{1,0:T(8,128)(2,1)}, bf16[320,1536]{1,0:T(8,128)(2,1)}, u32[]{:S(2)}, u32[]{:S(2)}) collective-permute-start(bf16[320,1536]{1,0:T(8,128)(2,1)} %bitcast.17), channel_id=1, source_target_pairs={{0,224},{32,64},{64,32},{96,128},{128,96},{160,192},{192,160},{224... | collective-permute-start | bytes 2949128 | tf_op jit(solution)/shard_map/ppermute | solution.py:301
  14.7 1.9 %collective-permute-start.2 = (bf16[320,1536]{1,0:T(8,128)(2,1)}, bf16[320,1536]{1,0:T(8,128)(2,1)}, u32[]{:S(2)}, u32[]{:S(2)}) collective-permute-start(bf16[320,1536]{1,0:T(8,128)(2,1)} %bitcast.18), channel_id=1, source_target_pairs={{0,32},{32,0},{64,96},{96,64},{128,160},{160,128},{192,224},{224,1... | collective-permute-start | bytes 2949128 | tf_op jit(solution)/shard_map/ppermute | solution.py:301
  16.7 3.2 %collective-permute-start = (bf16[192,1536]{1,0:T(8,128)(2,1)}, bf16[192,1536]{1,0:T(8,128)(2,1)S(1)}, u32[]{:S(2)}, u32[]{:S(2)}) collective-permute-start(bf16[192,1536]{1,0:T(8,128)(2,1)} %bitcast.12), channel_id=1, source_target_pairs={{0,256},{256,0},{1,257},{257,1},{2,258},{258,2},{3,259},{259,3},{4... | collective-permute-start | bytes 1769480 | tf_op jit(solution)/shard_map/ppermute | solution.py:251
  19.9 2.5 %collective-permute-start.4 = (bf16[64,128]{1,0:T(8,128)(2,1)}, bf16[64,128]{1,0:T(8,128)(2,1)S(1)}, u32[]{:S(2)}, u32[]{:S(2)}) collective-permute-start(bf16[64,128]{1,0:T(8,128)(2,1)} %bitcast.14), channel_id=1, source_target_pairs={{0,1},{1,0},{2,3},{3,2},{4,5},{5,4},{6,7},{7,6},{8,9},{9,8},{10,11... | collective-permute-start | bytes 49160 | tf_op jit(solution)/shard_map/ppermute | solution.py:247
  27.2 8.7 %all-to-all-start = ((f32[16,80,128]{2,1,0:T(8,128)}), f32[16,80,128]{2,1,0:T(8,128)}, u32[]{:S(2)}, u32[]{:S(2)}) async-start(f32[16,80,128]{2,1,0:T(8,128)} %shard_map.90), calls=%async_computation | async-start | bytes 1310720 | tf_op jit(solution)/shard_map/all_to_all | solution.py:249
  38.2 1.8 %collective-permute-done.2.refs_3_ = bf16[320,1536]{1,0:T(8,128)(2,1)} collective-permute-done((bf16[320,1536]{1,0:T(8,128)(2,1)}, bf16[320,1536]{1,0:T(8,128)(2,1)}, u32[]{:S(2)}, u32[]{:S(2)}) %collective-permute-start.2) | collective-permute-done | bytes 983072 | tf_op jit(solution)/shard_map/ppermute | solution.py:301
  40.0 2.2 %collective-permute-start.6 = (bf16[320,1536]{1,0:T(8,128)(2,1)}, bf16[320,1536]{1,0:T(8,128)(2,1)}, u32[]{:S(2)}, u32[]{:S(2)}) collective-permute-start(bf16[320,1536]{1,0:T(8,128)(2,1)} %collective-permute-done.1.refs_2_), channel_id=1, source_target_pairs={{0,32},{32,0},{64,96},{96,64},{128,160},{160,128},{192,224},{224,1... | collective-permute-start | bytes 2949128 | tf_op jit(solution)/shard_map/ppermute | solution.py:310
  42.2 2.1 %collective-permute-start.5 = (bf16[320,1536]{1,0:T(8,128)(2,1)}, bf16[320,1536]{1,0:T(8,128)(2,1)}, u32[]{:S(2)}, u32[]{:S(2)}) collective-permute-start(bf16[320,1536]{1,0:T(8,128)(2,1)} %collective-permute-done.2.refs_3_), channel_id=1, source_target_pairs={{0,224},{32,64},{64,32},{96,128},{128,96},{160,192},{192,160},{224... | collective-permute-start | bytes 2949128 | tf_op jit(solution)/shard_map/ppermute | solution.py:310
  44.4 4.4 %shard_map.89 = bf16[64,48,128]{2,1,0:T(8,128)(2,1)} custom-call(bf16[512,1536]{1,0:T(8,128)(2,1)S(1)} %bitcast.8, bf16[64,32,128]{2,1,0:T(8,128)(2,1)S(1)} %shard_map.88.refs_1_, bf16[320,1536]{1,0:T(8,128)(2,1)} %collective-permute-done.1.refs_2_, bf16[320,1536]{1,0:T(8,128)(2,1)} %collective-permute-done.2.refs_3_), custom_call_target="tpu_custom_call" | custom-call | flops 2000000000 | bytes 3000000 | tf_op jit(solution)/shard_map/pallas_call | solution.py:39
  48.7 5.1 %all-to-all-done = f32[16,80,128]{2,1,0:T(8,128)} async-done(((f32[16,80,128]{2,1,0:T(8,128)}), f32[16,80,128]{2,1,0:T(8,128)}, u32[]{:S(2)}, u32[]{:S(2)}) %all-to-all-start) | async-done | bytes 655392 | tf_op jit(solution)/shard_map/all_to_all | solution.py:249
  53.8 8.6 %all-to-all-start.1 = ((bf16[64,48,128]{2,1,0:T(8,128)(2,1)}), bf16[64,48,128]{2,1,0:T(8,128)(2,1)S(1)}, u32[]{:S(2)}, u32[]{:S(2)}) async-start(bf16[64,48,128]{2,1,0:T(8,128)(2,1)} %shard_map.89), calls=%async_computation.1 | async-start | bytes 1572864 | tf_op jit(solution)/shard_map/all_to_all | solution.py:292
  63.5 3.6 %collective-permute-start.11 = (f32[80,128]{1,0:T(8,128)S(1)}, f32[80,128]{1,0:T(8,128)S(1)}, u32[]{:S(2)}, u32[]{:S(2)}) collective-permute-start(f32[80,128]{1,0:T(8,128)S(1)} %reduce_sum.9), channel_id=1, source_target_pairs={{0,32},{32,0},{64,96},{96,64},{128,160},{160,128},{192,224},{224,1... | collective-permute-start | bytes 122888 | tf_op jit(solution)/shard_map/ppermute | solution.py:277
  67.8 1.9 %collective-permute-start.7 = (bf16[320,1536]{1,0:T(8,128)(2,1)}, bf16[320,1536]{1,0:T(8,128)(2,1)}, u32[]{:S(2)}, u32[]{:S(2)}) collective-permute-start(bf16[320,1536]{1,0:T(8,128)(2,1)} %collective-permute-done.6.refs_2_), channel_id=1, source_target_pairs={{0,224},{32,64},{64,32},{96,128},{128,96},{160,192},{192,160},{224... | collective-permute-start | bytes 2949128 | tf_op jit(solution)/shard_map/ppermute | solution.py:316
  69.7 1.9 %collective-permute-start.8 = (bf16[320,1536]{1,0:T(8,128)(2,1)}, bf16[320,1536]{1,0:T(8,128)(2,1)}, u32[]{:S(2)}, u32[]{:S(2)}) collective-permute-start(bf16[320,1536]{1,0:T(8,128)(2,1)} %collective-permute-done.5.refs_1_), channel_id=1, source_target_pairs={{0,32},{32,0},{64,96},{96,64},{128,160},{160,128},{192,224},{224,1... | collective-permute-start | bytes 2949128 | tf_op jit(solution)/shard_map/ppermute | solution.py:316
  71.7 4.2 %collective-permute-start.12 = (f32[80,128]{1,0:T(8,128)S(1)}, f32[80,128]{1,0:T(8,128)S(1)}, u32[]{:S(2)}, u32[]{:S(2)}) collective-permute-start(f32[80,128]{1,0:T(8,128)S(1)} %add.12), channel_id=1, source_target_pairs={{0,64},{32,96},{64,0},{96,32},{128,192},{160,224},{192,128},{224,1... | collective-permute-start | bytes 122888 | tf_op jit(solution)/shard_map/ppermute | solution.py:277
  75.9 4.3 %shard_map.91.refs_2_ = bf16[64,32,128]{2,1,0:T(8,128)(2,1)} custom-call(bf16[512,1536]{1,0:T(8,128)(2,1)S(1)} %bitcast.9, bf16[320,1536]{1,0:T(8,128)(2,1)} %collective-permute-done.5.refs_1_, bf16[320,1536]{1,0:T(8,128)(2,1)} %collective-permute-done.6.refs_2_), custom_call_target="tpu_custom_call" | custom-call | flops 15000000512 | bytes 4000000 | tf_op jit(solution)/shard_map/pallas_call | solution.py:39
  80.1 5.8 %all-to-all-done.1.refs_3_.refs_4_ = bf16[64,48,128]{2,1,0:T(8,128)(2,1)S(1)} async-done(((bf16[64,48,128]{2,1,0:T(8,128)(2,1)}), bf16[64,48,128]{2,1,0:T(8,128)(2,1)S(1)}, u32[]{:S(2)}, u32[]{:S(2)}) %all-to-all-start.1) | async-done | bytes 786464 | tf_op jit(solution)/shard_map/all_to_all | solution.py:292
  85.9 7.5 %all-to-all-start.2 = ((bf16[64,32,128]{2,1,0:T(8,128)(2,1)}), bf16[64,32,128]{2,1,0:T(8,128)(2,1)S(1)}, u32[]{:S(2)}, u32[]{:S(2)}) async-start(bf16[64,32,128]{2,1,0:T(8,128)(2,1)} %shard_map.91.refs_2_), calls=%async_computation.2 | async-start | bytes 1048576 | tf_op jit(solution)/shard_map/all_to_all | solution.py:292
  94.7 4.9 %collective-permute-start.10 = (bf16[160,1536]{1,0:T(8,128)(2,1)S(1)}, bf16[160,1536]{1,0:T(8,128)(2,1)S(1)}, u32[]{:S(2)}, u32[]{:S(2)}) collective-permute-start(bf16[160,1536]{1,0:T(8,128)(2,1)S(1)} %get-tuple-element.18), channel_id=1, source_target_pairs={{0,224},{32,64},{64,32},{96,128},{128,96},{160,192},{192,160},{224... | collective-permute-start | bytes 1474568 | tf_op jit(solution)/shard_map/ppermute | solution.py:332
  99.6 1.9 %collective-permute-start.9 = (bf16[160,1536]{1,0:T(8,128)(2,1)S(1)}, bf16[160,1536]{1,0:T(8,128)(2,1)S(1)}, u32[]{:S(2)}, u32[]{:S(2)}) collective-permute-start(bf16[160,1536]{1,0:T(8,128)(2,1)S(1)} %get-tuple-element.17), channel_id=1, source_target_pairs={{0,32},{32,0},{64,96},{96,64},{128,160},{160,128},{192,224},{224,1... | collective-permute-start | bytes 1474568 | tf_op jit(solution)/shard_map/ppermute | solution.py:331
  101.5 3.5 %shard_map.92.refs_1_ = bf16[64,32,128]{2,1,0:T(8,128)(2,1)S(1)} custom-call(bf16[512,1536]{1,0:T(8,128)(2,1)S(1)} %bitcast.10, bf16[320,1536]{1,0:T(8,128)(2,1)} %collective-permute-done.7.refs_1_.refs_0_, bf16[320,1536]{1,0:T(8,128)(2,1)} %collective-permute-done.8.refs_2_.refs_1_), custom_call_target="tpu_custom_call" | custom-call | flops 10000000000 | bytes 4000000 | tf_op jit(solution)/shard_map/pallas_call | solution.py:39
  105.0 2.6 %collective-permute-done.10.refs_3_ = bf16[160,1536]{1,0:T(8,128)(2,1)S(1)} collective-permute-done((bf16[160,1536]{1,0:T(8,128)(2,1)S(1)}, bf16[160,1536]{1,0:T(8,128)(2,1)S(1)}, u32[]{:S(2)}, u32[]{:S(2)}) %collective-permute-start.10) | collective-permute-done | bytes 491552 | tf_op jit(solution)/shard_map/ppermute | solution.py:332
  107.6 3.1 %collective-permute-done.9.refs_2_ = bf16[160,1536]{1,0:T(8,128)(2,1)S(1)} collective-permute-done((bf16[160,1536]{1,0:T(8,128)(2,1)S(1)}, bf16[160,1536]{1,0:T(8,128)(2,1)S(1)}, u32[]{:S(2)}, u32[]{:S(2)}) %collective-permute-start.9) | collective-permute-done | bytes 491552 | tf_op jit(solution)/shard_map/ppermute | solution.py:331
  110.7 2.0 %shard_map.94 = bf16[64,48,128]{2,1,0:T(8,128)(2,1)} custom-call(bf16[512,1536]{1,0:T(8,128)(2,1)S(1)} %bitcast.11, bf16[64,32,128]{2,1,0:T(8,128)(2,1)S(1)} %shard_map.92.refs_1_, bf16[160,1536]{1,0:T(8,128)(2,1)S(1)} %collective-permute-done.9.refs_2_, bf16[160,1536]{1,0:T(8,128)(2,1)S(1)} %collective-permute-done.10.refs_3_, f32[80,128]{1,0:T(8,128)S(1)} %add.13.refs_4_), custom_call_target="tpu_custom_call" | custom-call | flops 1000000000 | bytes 3000000 | tf_op jit(solution)/shard_map/pallas_call | solution.py:39
  112.8 14.7 %all-to-all-start.3 = ((bf16[64,48,128]{2,1,0:T(8,128)(2,1)}), bf16[64,48,128]{2,1,0:T(8,128)(2,1)S(1)}, u32[]{:S(2)}, u32[]{:S(2)}) async-start(bf16[64,48,128]{2,1,0:T(8,128)(2,1)} %shard_map.94), calls=%async_computation.3 | async-start | bytes 1572864 | tf_op jit(solution)/shard_map/all_to_all | solution.py:292
  127.4 3.2 %collective-permute-start.13 = (f32[80,128]{1,0:T(8,128)S(1)}, f32[80,128]{1,0:T(8,128)S(1)}, u32[]{:S(2)}, u32[]{:S(2)}) collective-permute-start(f32[80,128]{1,0:T(8,128)S(1)} %add.13.refs_4_), channel_id=1, source_target_pairs={{0,128},{32,160},{64,192},{96,224},{128,0},{160,32},{192,64},{224,... | collective-permute-start | bytes 122888 | tf_op jit(solution)/shard_map/ppermute | solution.py:277
  130.6 5.7 %collective-permute-done.13 = f32[80,128]{1,0:T(8,128)S(1)} collective-permute-done((f32[80,128]{1,0:T(8,128)S(1)}, f32[80,128]{1,0:T(8,128)S(1)}, u32[]{:S(2)}, u32[]{:S(2)}) %collective-permute-start.13) | collective-permute-done | bytes 40992 | tf_op jit(solution)/shard_map/ppermute | solution.py:277
  136.4 3.4 %collective-permute-start.14 = (f32[80,128]{1,0:T(8,128)S(1)}, f32[80,128]{1,0:T(8,128)S(1)}, u32[]{:S(2)}, u32[]{:S(2)}) collective-permute-start(f32[80,128]{1,0:T(8,128)S(1)} %add.14), channel_id=1, source_target_pairs={{0,256},{256,0},{1,257},{257,1},{2,258},{258,2},{3,259},{259,3},{4... | collective-permute-start | bytes 122888 | tf_op jit(solution)/shard_map/ppermute | solution.py:349
  140.5 6.7 %collective-permute-done.14 = f32[80,128]{1,0:T(8,128)S(1)} collective-permute-done((f32[80,128]{1,0:T(8,128)S(1)}, f32[80,128]{1,0:T(8,128)S(1)}, u32[]{:S(2)}, u32[]{:S(2)}) %collective-permute-start.14) | collective-permute-done | bytes 40992 | tf_op jit(solution)/shard_map/ppermute | solution.py:349
  148.0 3.0 %all-to-all-done.3.refs_6_ = bf16[64,48,128]{2,1,0:T(8,128)(2,1)S(1)} async-done(((bf16[64,48,128]{2,1,0:T(8,128)(2,1)}), bf16[64,48,128]{2,1,0:T(8,128)(2,1)S(1)}, u32[]{:S(2)}, u32[]{:S(2)}) %all-to-all-start.3) | async-done | bytes 786464 | tf_op jit(solution)/shard_map/all_to_all | solution.py:292
  151.0 2.3 %shard_map.95 = bf16[128,5120]{1,0:T(8,128)(2,1)} custom-call(s32[1]{0:T(128)} %bitcast.refs_0_, bf16[128,256]{1,0:T(8,128)(2,1)S(1)} %shard_map.86.refs_1_, bf16[64,128]{1,0:T(8,128)(2,1)S(1)} %bitcast.16, bf16[64,5120]{1,0:T(8,128)(2,1)S(1)} %copy-done.1, bf16[64,48,128]{2,1,0:T(8,128)(2,1)S(1)} %all-to-all-done.1.refs_3_.refs_4_, ...), custom_call_target="tpu_custom_call" | custom-call | flops 400000000 | bytes 6000000 | tf_op jit(solution)/shard_map/pallas_call | solution.py:39
  (40 shorter events, 11.6 us)
Async XLA Ops:
  0.6 22.8 %collective-permute-start.3 = (bf16[128,5120]{1,0:T(8,128)(2,1)}, bf16[128,5120]{1,0:T(8,128)(2,1)S(1)}, u32[]{:S(2)}, u32[]{:S(2)}) collective-permute-start(bf16[128,5120]{1,0:T(8,128)(2,1)} %refs_1_.2), channel_id=1, source_target_pairs={{0,1},{1,0},{2,3},{3,2},{4,5},{5,4},{6,7},{7,6},{8,9},{9,8},{10,11... | collective-permute-start | bytes 3932168 | tf_op jit(solution)/shard_map/ppermute | solution.py:246
  9.4 28.7 %collective-permute-start.1 = (bf16[320,1536]{1,0:T(8,128)(2,1)}, bf16[320,1536]{1,0:T(8,128)(2,1)}, u32[]{:S(2)}, u32[]{:S(2)}) collective-permute-start(bf16[320,1536]{1,0:T(8,128)(2,1)} %bitcast.17), channel_id=1, source_target_pairs={{0,224},{32,64},{64,32},{96,128},{128,96},{160,192},{192,160},{224... | collective-permute-start | bytes 2949128 | tf_op jit(solution)/shard_map/ppermute | solution.py:301
  14.7 25.3 %collective-permute-start.2 = (bf16[320,1536]{1,0:T(8,128)(2,1)}, bf16[320,1536]{1,0:T(8,128)(2,1)}, u32[]{:S(2)}, u32[]{:S(2)}) collective-permute-start(bf16[320,1536]{1,0:T(8,128)(2,1)} %bitcast.18), channel_id=1, source_target_pairs={{0,32},{32,0},{64,96},{96,64},{128,160},{160,128},{192,224},{224,1... | collective-permute-start | bytes 2949128 | tf_op jit(solution)/shard_map/ppermute | solution.py:301
  16.7 19.2 %collective-permute-start = (bf16[192,1536]{1,0:T(8,128)(2,1)}, bf16[192,1536]{1,0:T(8,128)(2,1)S(1)}, u32[]{:S(2)}, u32[]{:S(2)}) collective-permute-start(bf16[192,1536]{1,0:T(8,128)(2,1)} %bitcast.12), channel_id=1, source_target_pairs={{0,256},{256,0},{1,257},{257,1},{2,258},{258,2},{3,259},{259,3},{4... | collective-permute-start | bytes 1769480 | tf_op jit(solution)/shard_map/ppermute | solution.py:251
  19.9 3.5 %collective-permute-start.4 = (bf16[64,128]{1,0:T(8,128)(2,1)}, bf16[64,128]{1,0:T(8,128)(2,1)S(1)}, u32[]{:S(2)}, u32[]{:S(2)}) collective-permute-start(bf16[64,128]{1,0:T(8,128)(2,1)} %bitcast.14), channel_id=1, source_target_pairs={{0,1},{1,0},{2,3},{3,2},{4,5},{5,4},{6,7},{7,6},{8,9},{9,8},{10,11... | collective-permute-start | bytes 49160 | tf_op jit(solution)/shard_map/ppermute | solution.py:247
  23.4 1.3 copy-start
  24.7 0.7 copy-start.3
  27.2 8.7 %copy-start.2 = (bf16[1,192,1536]{2,1,0:T(8,128)(2,1)S(1)}, bf16[1,192,1536]{2,1,0:T(8,128)(2,1)}, u32[]{:S(2)}) copy-start(bf16[1,192,1536]{2,1,0:T(8,128)(2,1)} %param.9) | copy-start | bytes 1769476
  27.2 26.6 %all-to-all-start = ((f32[16,80,128]{2,1,0:T(8,128)}), f32[16,80,128]{2,1,0:T(8,128)}, u32[]{:S(2)}, u32[]{:S(2)}) async-start(f32[16,80,128]{2,1,0:T(8,128)} %shard_map.90), calls=%async_computation | async-start | bytes 1310720 | tf_op jit(solution)/shard_map/all_to_all | solution.py:249
  35.9 1.2 copy-start.5
  40.0 27.2 %collective-permute-start.6 = (bf16[320,1536]{1,0:T(8,128)(2,1)}, bf16[320,1536]{1,0:T(8,128)(2,1)}, u32[]{:S(2)}, u32[]{:S(2)}) collective-permute-start(bf16[320,1536]{1,0:T(8,128)(2,1)} %collective-permute-done.1.refs_2_), channel_id=1, source_target_pairs={{0,32},{32,0},{64,96},{96,64},{128,160},{160,128},{192,224},{224,1... | collective-permute-start | bytes 2949128 | tf_op jit(solution)/shard_map/ppermute | solution.py:310
  42.2 25.6 %collective-permute-start.5 = (bf16[320,1536]{1,0:T(8,128)(2,1)}, bf16[320,1536]{1,0:T(8,128)(2,1)}, u32[]{:S(2)}, u32[]{:S(2)}) collective-permute-start(bf16[320,1536]{1,0:T(8,128)(2,1)} %collective-permute-done.2.refs_3_), channel_id=1, source_target_pairs={{0,224},{32,64},{64,32},{96,128},{128,96},{160,192},{192,160},{224... | collective-permute-start | bytes 2949128 | tf_op jit(solution)/shard_map/ppermute | solution.py:310
  53.8 32.1 %all-to-all-start.1 = ((bf16[64,48,128]{2,1,0:T(8,128)(2,1)}), bf16[64,48,128]{2,1,0:T(8,128)(2,1)S(1)}, u32[]{:S(2)}, u32[]{:S(2)}) async-start(bf16[64,48,128]{2,1,0:T(8,128)(2,1)} %shard_map.89), calls=%async_computation.1 | async-start | bytes 1572864 | tf_op jit(solution)/shard_map/all_to_all | solution.py:292
  63.5 8.2 %collective-permute-start.11 = (f32[80,128]{1,0:T(8,128)S(1)}, f32[80,128]{1,0:T(8,128)S(1)}, u32[]{:S(2)}, u32[]{:S(2)}) collective-permute-start(f32[80,128]{1,0:T(8,128)S(1)} %reduce_sum.9), channel_id=1, source_target_pairs={{0,32},{32,0},{64,96},{96,64},{128,160},{160,128},{192,224},{224,1... | collective-permute-start | bytes 122888 | tf_op jit(solution)/shard_map/ppermute | solution.py:277
  67.8 25.6 %collective-permute-start.7 = (bf16[320,1536]{1,0:T(8,128)(2,1)}, bf16[320,1536]{1,0:T(8,128)(2,1)}, u32[]{:S(2)}, u32[]{:S(2)}) collective-permute-start(bf16[320,1536]{1,0:T(8,128)(2,1)} %collective-permute-done.6.refs_2_), channel_id=1, source_target_pairs={{0,224},{32,64},{64,32},{96,128},{128,96},{160,192},{192,160},{224... | collective-permute-start | bytes 2949128 | tf_op jit(solution)/shard_map/ppermute | solution.py:316
  69.7 23.7 %collective-permute-start.8 = (bf16[320,1536]{1,0:T(8,128)(2,1)}, bf16[320,1536]{1,0:T(8,128)(2,1)}, u32[]{:S(2)}, u32[]{:S(2)}) collective-permute-start(bf16[320,1536]{1,0:T(8,128)(2,1)} %collective-permute-done.5.refs_1_), channel_id=1, source_target_pairs={{0,32},{32,0},{64,96},{96,64},{128,160},{160,128},{192,224},{224,1... | collective-permute-start | bytes 2949128 | tf_op jit(solution)/shard_map/ppermute | solution.py:316
  71.7 21.7 %collective-permute-start.12 = (f32[80,128]{1,0:T(8,128)S(1)}, f32[80,128]{1,0:T(8,128)S(1)}, u32[]{:S(2)}, u32[]{:S(2)}) collective-permute-start(f32[80,128]{1,0:T(8,128)S(1)} %add.12), channel_id=1, source_target_pairs={{0,64},{32,96},{64,0},{96,32},{128,192},{160,224},{192,128},{224,1... | collective-permute-start | bytes 122888 | tf_op jit(solution)/shard_map/ppermute | solution.py:277
  85.9 26.9 %all-to-all-start.2 = ((bf16[64,32,128]{2,1,0:T(8,128)(2,1)}), bf16[64,32,128]{2,1,0:T(8,128)(2,1)S(1)}, u32[]{:S(2)}, u32[]{:S(2)}) async-start(bf16[64,32,128]{2,1,0:T(8,128)(2,1)} %shard_map.91.refs_2_), calls=%async_computation.2 | async-start | bytes 1048576 | tf_op jit(solution)/shard_map/all_to_all | solution.py:292
  94.7 12.9 %collective-permute-start.10 = (bf16[160,1536]{1,0:T(8,128)(2,1)S(1)}, bf16[160,1536]{1,0:T(8,128)(2,1)S(1)}, u32[]{:S(2)}, u32[]{:S(2)}) collective-permute-start(bf16[160,1536]{1,0:T(8,128)(2,1)S(1)} %get-tuple-element.18), channel_id=1, source_target_pairs={{0,224},{32,64},{64,32},{96,128},{128,96},{160,192},{192,160},{224... | collective-permute-start | bytes 1474568 | tf_op jit(solution)/shard_map/ppermute | solution.py:332
  99.6 11.1 %collective-permute-start.9 = (bf16[160,1536]{1,0:T(8,128)(2,1)S(1)}, bf16[160,1536]{1,0:T(8,128)(2,1)S(1)}, u32[]{:S(2)}, u32[]{:S(2)}) collective-permute-start(bf16[160,1536]{1,0:T(8,128)(2,1)S(1)} %get-tuple-element.17), channel_id=1, source_target_pairs={{0,32},{32,0},{64,96},{96,64},{128,160},{160,128},{192,224},{224,1... | collective-permute-start | bytes 1474568 | tf_op jit(solution)/shard_map/ppermute | solution.py:331
  112.7 27.0 %copy-start.6 = (f32[128,6]{0,1:T(8,128)S(1)}, f32[128,6]{0,1:T(8,128)}, u32[]{:S(2)}) copy-start(f32[128,6]{0,1:T(8,128)} %param.8) | copy-start | bytes 9220
  112.7 27.2 %copy-start.7 = (s32[128,6]{0,1:T(8,128)S(1)}, s32[128,6]{0,1:T(8,128)}, u32[]{:S(2)}) copy-start(s32[128,6]{0,1:T(8,128)} %param.7) | copy-start | bytes 9220
  112.7 38.2 %copy-start.1 = (bf16[64,5120]{1,0:T(8,128)(2,1)S(1)}, bf16[64,5120]{1,0:T(8,128)(2,1)}, u32[]{:S(2)}) copy-start(bf16[64,5120]{1,0:T(8,128)(2,1)} %refs_3_.1) | copy-start | bytes 1966084
  112.7 38.2 %copy-start.4 = (bf16[128,64]{0,1:T(8,128)(2,1)S(1)}, bf16[128,64]{0,1:T(8,128)(2,1)}, u32[]{:S(2)}) copy-start(bf16[128,64]{0,1:T(8,128)(2,1)} %param.12) | copy-start | bytes 49156
  112.8 38.2 %all-to-all-start.3 = ((bf16[64,48,128]{2,1,0:T(8,128)(2,1)}), bf16[64,48,128]{2,1,0:T(8,128)(2,1)S(1)}, u32[]{:S(2)}, u32[]{:S(2)}) async-start(bf16[64,48,128]{2,1,0:T(8,128)(2,1)} %shard_map.94), calls=%async_computation.3 | async-start | bytes 1572864 | tf_op jit(solution)/shard_map/all_to_all | solution.py:292
  127.4 8.9 %collective-permute-start.13 = (f32[80,128]{1,0:T(8,128)S(1)}, f32[80,128]{1,0:T(8,128)S(1)}, u32[]{:S(2)}, u32[]{:S(2)}) collective-permute-start(f32[80,128]{1,0:T(8,128)S(1)} %add.13.refs_4_), channel_id=1, source_target_pairs={{0,128},{32,160},{64,192},{96,224},{128,0},{160,32},{192,64},{224,... | collective-permute-start | bytes 122888 | tf_op jit(solution)/shard_map/ppermute | solution.py:277
  136.4 10.9 %collective-permute-start.14 = (f32[80,128]{1,0:T(8,128)S(1)}, f32[80,128]{1,0:T(8,128)S(1)}, u32[]{:S(2)}, u32[]{:S(2)}) collective-permute-start(f32[80,128]{1,0:T(8,128)S(1)} %add.14), channel_id=1, source_target_pairs={{0,256},{256,0},{1,257},{257,1},{2,258},{258,2},{3,259},{259,3},{4... | collective-permute-start | bytes 122888 | tf_op jit(solution)/shard_map/ppermute | solution.py:349

commit v7 on v6

--- a/solution.py
+++ b/solution.py
@@ -162,15 +162,10 @@
     out_ref[...] = lines_ref[...].astype(out_ref.dtype)
 
 
-def halves_kernel(half, low_ref, high_ref, low_out, high_out, semaphores):
-    copies = [
-        pltpu.make_async_copy(low_ref.at[:half], low_out, semaphores.at[0]),
-        pltpu.make_async_copy(high_ref.at[half:], high_out, semaphores.at[1]),
-    ]
-    for copy in copies:
-        copy.start()
-    for copy in copies:
-        copy.wait()
+def cut_kernel(start, rows_ref, out_ref, semaphore):
+    copy = pltpu.make_async_copy(rows_ref.at[start : start + out_ref.shape[0]], out_ref, semaphore)
+    copy.start()
+    copy.wait()
 
 
 def finish_kernel(capacity, layout, z_ref, combine_ref, key_ref, rope_ref, *refs):
@@ -318,16 +313,20 @@
     crossed.append(came[1])
     sent = [send(first)]
     half = piece // 2
-    half_low, half_high = call(
-        functools.partial(halves_kernel, half),
-        [struct((half, depth), jnp.bfloat16)] * 2,
-        [ANY] * 2,
-        0,
-        3 * 10**6,
-        [pltpu.SemaphoreType.DMA((2,))],
-        [second] + sent,
-        ANY,
-    )(crossed[-1], paired[-1])
+
+    def cut(array, start):
+        return call(
+            functools.partial(cut_kernel, start),
+            struct((half, depth), jnp.bfloat16),
+            [ANY],
+            0,
+            10**6,
+            [pltpu.SemaphoreType.DMA],
+            [second] + sent,
+            ANY,
+        )(array)
+
+    half_low, half_high = cut(crossed[-1], 0), cut(paired[-1], half)
     last_low = lax.ppermute(half_low, "z", inner)
     last_high = lax.ppermute(half_high, "z", outer)
     sent.append(send(second))

time: 154 us -> 155 us (level)
    ppermute x1, starting transfers between devices: 4.9 us -> 1.92 us  [body(): last_high = lax.ppermute(half_high, 'z', outer)]
    ppermute x3, starting transfers between devices: 11 us -> 13.4 us  [added(): return sums + lax.ppermute(sums, 'z', [(i, i ^ bit) for i in range(ring)])]
    ppermute x1, waiting for transfers between devices: 2.62 us -> 4.32 us  [body(): last_high = lax.ppermute(half_high, 'z', outer)]
    pallas_call x11 -> x12, Pallas kernels: 22.2 us -> 23.2 us  [call(): return lambda *args: run(*args, *after)]
  transfers between devices with their start and end apart: 19 -> 19, of which waited for: 10 -> 11; matrix products, arithmetic and copies ran while one was open for 1% -> 1% of each run, Pallas kernels for 13% -> 14%
where the time goes in v7:
time: 155 us; the launch traced here: 154 us
  starting transfers between devices  90 us (58%)
  waiting for transfers between devices  35.4 us (23%)
  Pallas kernels  23.2 us (15%)
  local copies, waits for them, and re-layouts  2.9 us (2%)
    all_to_all x3, starting transfers between devices, send(): lax.all_to_all(computed, PLANE, split_axis=0, concat_axis=0, tiled=True)  30.6 us
    pallas_call x12, Pallas kernels, call(): return lambda *args: run(*args, *after)  23.2 us
    ppermute x3, starting transfers between devices, added(): return sums + lax.ppermute(sums, 'z', [(i, i ^ bit) for i in range(ring)])  13.4 us
    ppermute x3, starting transfers between devices, body(): lax.ppermute(paired[-1], 'z', outer)  9.57 us
    ppermute x1, starting transfers between devices, body(): lax.ppermute(normed, 'core', swap)  8.79 us
    all_to_all x1, starting transfers between devices, body(): lax.all_to_all(mine, ('x', 'yhi'), split_axis=0, concat_axis=0, tiled=True)  8.67 us
    all_to_all x3, waiting for transfers between devices, send(): lax.all_to_all(computed, PLANE, split_axis=0, concat_axis=0, tiled=True)  8.36 us
    ppermute x1, waiting for transfers between devices, body(): summed = summed + lax.ppermute(summed, 'ylo', swap)  6.72 us
  transfers between devices with their start and end apart: 19, of which 11 were waited for; matrix products, arithmetic and copies ran while one was open for 1% of the time, Pallas kernels for 14%

profile of v7, /device:TPU:1, one launch (start us, length us, event | category | flops | bytes accessed | tf_op | source)
XLA Modules:
  0.0 153.6 jit_solution(15232384053977483335)
XLA Ops:
  0.6 8.8 %collective-permute-start.3 = (bf16[128,5120]{1,0:T(8,128)(2,1)}, bf16[128,5120]{1,0:T(8,128)(2,1)S(1)}, u32[]{:S(2)}, u32[]{:S(2)}) collective-permute-start(bf16[128,5120]{1,0:T(8,128)(2,1)} %refs_1_.2), channel_id=1, source_target_pairs={{0,1},{1,0},{2,3},{3,2},{4,5},{5,4},{6,7},{7,6},{8,9},{9,8},{10,11... | collective-permute-start | bytes 3932168 | tf_op jit(solution)/shard_map/ppermute | solution.py:241
  9.4 5.3 %collective-permute-start.1 = (bf16[320,1536]{1,0:T(8,128)(2,1)}, bf16[320,1536]{1,0:T(8,128)(2,1)}, u32[]{:S(2)}, u32[]{:S(2)}) collective-permute-start(bf16[320,1536]{1,0:T(8,128)(2,1)} %bitcast.17), channel_id=1, source_target_pairs={{0,224},{32,64},{64,32},{96,128},{128,96},{160,192},{192,160},{224... | collective-permute-start | bytes 2949128 | tf_op jit(solution)/shard_map/ppermute | solution.py:296
  14.7 1.9 %collective-permute-start.2 = (bf16[320,1536]{1,0:T(8,128)(2,1)}, bf16[320,1536]{1,0:T(8,128)(2,1)}, u32[]{:S(2)}, u32[]{:S(2)}) collective-permute-start(bf16[320,1536]{1,0:T(8,128)(2,1)} %bitcast.18), channel_id=1, source_target_pairs={{0,32},{32,0},{64,96},{96,64},{128,160},{160,128},{192,224},{224,1... | collective-permute-start | bytes 2949128 | tf_op jit(solution)/shard_map/ppermute | solution.py:296
  16.7 3.2 %collective-permute-start = (bf16[192,1536]{1,0:T(8,128)(2,1)}, bf16[192,1536]{1,0:T(8,128)(2,1)S(1)}, u32[]{:S(2)}, u32[]{:S(2)}) collective-permute-start(bf16[192,1536]{1,0:T(8,128)(2,1)} %bitcast.12), channel_id=1, source_target_pairs={{0,256},{256,0},{1,257},{257,1},{2,258},{258,2},{3,259},{259,3},{4... | collective-permute-start | bytes 1769480 | tf_op jit(solution)/shard_map/ppermute | solution.py:246
  19.9 2.5 %collective-permute-start.4 = (bf16[64,128]{1,0:T(8,128)(2,1)}, bf16[64,128]{1,0:T(8,128)(2,1)S(1)}, u32[]{:S(2)}, u32[]{:S(2)}) collective-permute-start(bf16[64,128]{1,0:T(8,128)(2,1)} %bitcast.14), channel_id=1, source_target_pairs={{0,1},{1,0},{2,3},{3,2},{4,5},{5,4},{6,7},{7,6},{8,9},{9,8},{10,11... | collective-permute-start | bytes 49160 | tf_op jit(solution)/shard_map/ppermute | solution.py:242
  27.2 8.7 %all-to-all-start = ((f32[16,80,128]{2,1,0:T(8,128)}), f32[16,80,128]{2,1,0:T(8,128)}, u32[]{:S(2)}, u32[]{:S(2)}) async-start(f32[16,80,128]{2,1,0:T(8,128)} %shard_map.90), calls=%async_computation | async-start | bytes 1310720 | tf_op jit(solution)/shard_map/all_to_all | solution.py:244
  38.2 1.8 %collective-permute-done.2.refs_3_ = bf16[320,1536]{1,0:T(8,128)(2,1)} collective-permute-done((bf16[320,1536]{1,0:T(8,128)(2,1)}, bf16[320,1536]{1,0:T(8,128)(2,1)}, u32[]{:S(2)}, u32[]{:S(2)}) %collective-permute-start.2) | collective-permute-done | bytes 983072 | tf_op jit(solution)/shard_map/ppermute | solution.py:296
  40.0 2.2 %collective-permute-start.6 = (bf16[320,1536]{1,0:T(8,128)(2,1)}, bf16[320,1536]{1,0:T(8,128)(2,1)}, u32[]{:S(2)}, u32[]{:S(2)}) collective-permute-start(bf16[320,1536]{1,0:T(8,128)(2,1)} %collective-permute-done.1.refs_2_), channel_id=1, source_target_pairs={{0,32},{32,0},{64,96},{96,64},{128,160},{160,128},{192,224},{224,1... | collective-permute-start | bytes 2949128 | tf_op jit(solution)/shard_map/ppermute | solution.py:305
  42.2 2.1 %collective-permute-start.5 = (bf16[320,1536]{1,0:T(8,128)(2,1)}, bf16[320,1536]{1,0:T(8,128)(2,1)}, u32[]{:S(2)}, u32[]{:S(2)}) collective-permute-start(bf16[320,1536]{1,0:T(8,128)(2,1)} %collective-permute-done.2.refs_3_), channel_id=1, source_target_pairs={{0,224},{32,64},{64,32},{96,128},{128,96},{160,192},{192,160},{224... | collective-permute-start | bytes 2949128 | tf_op jit(solution)/shard_map/ppermute | solution.py:305
  44.4 4.4 %shard_map.89 = bf16[64,48,128]{2,1,0:T(8,128)(2,1)} custom-call(bf16[512,1536]{1,0:T(8,128)(2,1)S(1)} %bitcast.8, bf16[64,32,128]{2,1,0:T(8,128)(2,1)S(1)} %shard_map.88.refs_1_, bf16[320,1536]{1,0:T(8,128)(2,1)} %collective-permute-done.1.refs_2_, bf16[320,1536]{1,0:T(8,128)(2,1)} %collective-permute-done.2.refs_3_), custom_call_target="tpu_custom_call" | custom-call | flops 2000000000 | bytes 3000000 | tf_op jit(solution)/shard_map/pallas_call | solution.py:39
  48.7 5.1 %all-to-all-done = f32[16,80,128]{2,1,0:T(8,128)} async-done(((f32[16,80,128]{2,1,0:T(8,128)}), f32[16,80,128]{2,1,0:T(8,128)}, u32[]{:S(2)}, u32[]{:S(2)}) %all-to-all-start) | async-done | bytes 655392 | tf_op jit(solution)/shard_map/all_to_all | solution.py:244
  53.8 8.6 %all-to-all-start.1 = ((bf16[64,48,128]{2,1,0:T(8,128)(2,1)}), bf16[64,48,128]{2,1,0:T(8,128)(2,1)S(1)}, u32[]{:S(2)}, u32[]{:S(2)}) async-start(bf16[64,48,128]{2,1,0:T(8,128)(2,1)} %shard_map.89), calls=%async_computation.1 | async-start | bytes 1572864 | tf_op jit(solution)/shard_map/all_to_all | solution.py:287
  63.5 3.6 %collective-permute-start.11 = (f32[80,128]{1,0:T(8,128)S(1)}, f32[80,128]{1,0:T(8,128)S(1)}, u32[]{:S(2)}, u32[]{:S(2)}) collective-permute-start(f32[80,128]{1,0:T(8,128)S(1)} %reduce_sum.9), channel_id=1, source_target_pairs={{0,32},{32,0},{64,96},{96,64},{128,160},{160,128},{192,224},{224,1... | collective-permute-start | bytes 122888 | tf_op jit(solution)/shard_map/ppermute | solution.py:272
  67.8 1.9 %collective-permute-start.8 = (bf16[320,1536]{1,0:T(8,128)(2,1)}, bf16[320,1536]{1,0:T(8,128)(2,1)}, u32[]{:S(2)}, u32[]{:S(2)}) collective-permute-start(bf16[320,1536]{1,0:T(8,128)(2,1)} %collective-permute-done.5.refs_1_), channel_id=1, source_target_pairs={{0,32},{32,0},{64,96},{96,64},{128,160},{160,128},{192,224},{224,1... | collective-permute-start | bytes 2949128 | tf_op jit(solution)/shard_map/ppermute | solution.py:311
  69.7 2.2 %collective-permute-start.7 = (bf16[320,1536]{1,0:T(8,128)(2,1)}, bf16[320,1536]{1,0:T(8,128)(2,1)}, u32[]{:S(2)}, u32[]{:S(2)}) collective-permute-start(bf16[320,1536]{1,0:T(8,128)(2,1)} %collective-permute-done.6.refs_2_), channel_id=1, source_target_pairs={{0,224},{32,64},{64,32},{96,128},{128,96},{160,192},{192,160},{224... | collective-permute-start | bytes 2949128 | tf_op jit(solution)/shard_map/ppermute | solution.py:311
  71.9 4.3 %collective-permute-start.12 = (f32[80,128]{1,0:T(8,128)S(1)}, f32[80,128]{1,0:T(8,128)S(1)}, u32[]{:S(2)}, u32[]{:S(2)}) collective-permute-start(f32[80,128]{1,0:T(8,128)S(1)} %add.12), channel_id=1, source_target_pairs={{0,64},{32,96},{64,0},{96,32},{128,192},{160,224},{192,128},{224,1... | collective-permute-start | bytes 122888 | tf_op jit(solution)/shard_map/ppermute | solution.py:272
  76.2 4.3 %shard_map.91.refs_1_ = bf16[64,32,128]{2,1,0:T(8,128)(2,1)} custom-call(bf16[512,1536]{1,0:T(8,128)(2,1)S(1)} %bitcast.9, bf16[320,1536]{1,0:T(8,128)(2,1)} %collective-permute-done.5.refs_1_, bf16[320,1536]{1,0:T(8,128)(2,1)} %collective-permute-done.6.refs_2_), custom_call_target="tpu_custom_call" | custom-call | flops 15000000512 | bytes 4000000 | tf_op jit(solution)/shard_map/pallas_call | solution.py:39
  80.5 5.4 %all-to-all-done.1.refs_2_.refs_4_ = bf16[64,48,128]{2,1,0:T(8,128)(2,1)S(1)} async-done(((bf16[64,48,128]{2,1,0:T(8,128)(2,1)}), bf16[64,48,128]{2,1,0:T(8,128)(2,1)S(1)}, u32[]{:S(2)}, u32[]{:S(2)}) %all-to-all-start.1) | async-done | bytes 786464 | tf_op jit(solution)/shard_map/all_to_all | solution.py:287
  85.9 7.6 %all-to-all-start.2 = ((bf16[64,32,128]{2,1,0:T(8,128)(2,1)}), bf16[64,32,128]{2,1,0:T(8,128)(2,1)S(1)}, u32[]{:S(2)}, u32[]{:S(2)}) async-start(bf16[64,32,128]{2,1,0:T(8,128)(2,1)} %shard_map.91.refs_1_), calls=%async_computation.2 | async-start | bytes 1048576 | tf_op jit(solution)/shard_map/all_to_all | solution.py:287
  93.5 2.4 %collective-permute-done.12 = f32[80,128]{1,0:T(8,128)S(1)} collective-permute-done((f32[80,128]{1,0:T(8,128)S(1)}, f32[80,128]{1,0:T(8,128)S(1)}, u32[]{:S(2)}, u32[]{:S(2)}) %collective-permute-start.12) | collective-permute-done | bytes 40992 | tf_op jit(solution)/shard_map/ppermute | solution.py:272
  96.9 1.9 %collective-permute-start.10 = (bf16[160,1536]{1,0:T(8,128)(2,1)S(1)}, bf16[160,1536]{1,0:T(8,128)(2,1)S(1)}, u32[]{:S(2)}, u32[]{:S(2)}) collective-permute-start(bf16[160,1536]{1,0:T(8,128)(2,1)S(1)} %shard_map.94), channel_id=1, source_target_pairs={{0,224},{32,64},{64,32},{96,128},{128,96},{160,192},{192,160},{224... | collective-permute-start | bytes 1474568 | tf_op jit(solution)/shard_map/ppermute | solution.py:331
  99.9 1.9 %collective-permute-start.9 = (bf16[160,1536]{1,0:T(8,128)(2,1)S(1)}, bf16[160,1536]{1,0:T(8,128)(2,1)S(1)}, u32[]{:S(2)}, u32[]{:S(2)}) collective-permute-start(bf16[160,1536]{1,0:T(8,128)(2,1)S(1)} %shard_map.93), channel_id=1, source_target_pairs={{0,32},{32,0},{64,96},{96,64},{128,160},{160,128},{192,224},{224,1... | collective-permute-start | bytes 1474568 | tf_op jit(solution)/shard_map/ppermute | solution.py:330
  101.8 3.5 %shard_map.92.refs_1_ = bf16[64,32,128]{2,1,0:T(8,128)(2,1)S(1)} custom-call(bf16[512,1536]{1,0:T(8,128)(2,1)S(1)} %bitcast.10, bf16[320,1536]{1,0:T(8,128)(2,1)} %collective-permute-done.7.refs_1_.refs_0_, bf16[320,1536]{1,0:T(8,128)(2,1)} %collective-permute-done.8.refs_2_.refs_0_), custom_call_target="tpu_custom_call" | custom-call | flops 10000000000 | bytes 4000000 | tf_op jit(solution)/shard_map/pallas_call | solution.py:39
  105.3 4.3 %collective-permute-done.10.refs_3_ = bf16[160,1536]{1,0:T(8,128)(2,1)S(1)} collective-permute-done((bf16[160,1536]{1,0:T(8,128)(2,1)S(1)}, bf16[160,1536]{1,0:T(8,128)(2,1)S(1)}, u32[]{:S(2)}, u32[]{:S(2)}) %collective-permute-start.10) | collective-permute-done | bytes 491552 | tf_op jit(solution)/shard_map/ppermute | solution.py:331
  111.3 2.0 %shard_map.95 = bf16[64,48,128]{2,1,0:T(8,128)(2,1)} custom-call(bf16[512,1536]{1,0:T(8,128)(2,1)S(1)} %bitcast.11, bf16[64,32,128]{2,1,0:T(8,128)(2,1)S(1)} %shard_map.92.refs_1_, bf16[160,1536]{1,0:T(8,128)(2,1)S(1)} %collective-permute-done.9.refs_2_, bf16[160,1536]{1,0:T(8,128)(2,1)S(1)} %collective-permute-done.10.refs_3_, f32[80,128]{1,0:T(8,128)S(1)} %add.13.refs_4_), custom_call_target="tpu_custom_call" | custom-call | flops 1000000000 | bytes 3000000 | tf_op jit(solution)/shard_map/pallas_call | solution.py:39
  113.3 14.4 %all-to-all-start.3 = ((bf16[64,48,128]{2,1,0:T(8,128)(2,1)}), bf16[64,48,128]{2,1,0:T(8,128)(2,1)S(1)}, u32[]{:S(2)}, u32[]{:S(2)}) async-start(bf16[64,48,128]{2,1,0:T(8,128)(2,1)} %shard_map.95), calls=%async_computation.3 | async-start | bytes 1572864 | tf_op jit(solution)/shard_map/all_to_all | solution.py:287
  127.7 5.5 %collective-permute-start.13 = (f32[80,128]{1,0:T(8,128)S(1)}, f32[80,128]{1,0:T(8,128)S(1)}, u32[]{:S(2)}, u32[]{:S(2)}) collective-permute-start(f32[80,128]{1,0:T(8,128)S(1)} %add.13.refs_4_), channel_id=1, source_target_pairs={{0,128},{32,160},{64,192},{96,224},{128,0},{160,32},{192,64},{224,... | collective-permute-start | bytes 122888 | tf_op jit(solution)/shard_map/ppermute | solution.py:272
  133.2 3.5 %collective-permute-done.13 = f32[80,128]{1,0:T(8,128)S(1)} collective-permute-done((f32[80,128]{1,0:T(8,128)S(1)}, f32[80,128]{1,0:T(8,128)S(1)}, u32[]{:S(2)}, u32[]{:S(2)}) %collective-permute-start.13) | collective-permute-done | bytes 40992 | tf_op jit(solution)/shard_map/ppermute | solution.py:272
  136.7 3.4 %collective-permute-start.14 = (f32[80,128]{1,0:T(8,128)S(1)}, f32[80,128]{1,0:T(8,128)S(1)}, u32[]{:S(2)}, u32[]{:S(2)}) collective-permute-start(f32[80,128]{1,0:T(8,128)S(1)} %add.14), channel_id=1, source_target_pairs={{0,256},{256,0},{1,257},{257,1},{2,258},{258,2},{3,259},{259,3},{4... | collective-permute-start | bytes 122888 | tf_op jit(solution)/shard_map/ppermute | solution.py:348
  140.8 6.7 %collective-permute-done.14 = f32[80,128]{1,0:T(8,128)S(1)} collective-permute-done((f32[80,128]{1,0:T(8,128)S(1)}, f32[80,128]{1,0:T(8,128)S(1)}, u32[]{:S(2)}, u32[]{:S(2)}) %collective-permute-start.14) | collective-permute-done | bytes 40992 | tf_op jit(solution)/shard_map/ppermute | solution.py:348
  148.3 3.0 %all-to-all-done.3.refs_6_ = bf16[64,48,128]{2,1,0:T(8,128)(2,1)S(1)} async-done(((bf16[64,48,128]{2,1,0:T(8,128)(2,1)}), bf16[64,48,128]{2,1,0:T(8,128)(2,1)S(1)}, u32[]{:S(2)}, u32[]{:S(2)}) %all-to-all-start.3) | async-done | bytes 786464 | tf_op jit(solution)/shard_map/all_to_all | solution.py:287
  151.3 2.3 %shard_map.96 = bf16[128,5120]{1,0:T(8,128)(2,1)} custom-call(s32[1]{0:T(128)} %bitcast.refs_0_, bf16[128,256]{1,0:T(8,128)(2,1)S(1)} %shard_map.86.refs_1_, bf16[64,128]{1,0:T(8,128)(2,1)S(1)} %bitcast.16, bf16[64,5120]{1,0:T(8,128)(2,1)S(1)} %copy-done.1, bf16[64,48,128]{2,1,0:T(8,128)(2,1)S(1)} %all-to-all-done.1.refs_2_.refs_4_, ...), custom_call_target="tpu_custom_call" | custom-call | flops 400000000 | bytes 6000000 | tf_op jit(solution)/shard_map/pallas_call | solution.py:39
  (41 shorter events, 14.1 us)
Async XLA Ops:
  0.6 22.8 %collective-permute-start.3 = (bf16[128,5120]{1,0:T(8,128)(2,1)}, bf16[128,5120]{1,0:T(8,128)(2,1)S(1)}, u32[]{:S(2)}, u32[]{:S(2)}) collective-permute-start(bf16[128,5120]{1,0:T(8,128)(2,1)} %refs_1_.2), channel_id=1, source_target_pairs={{0,1},{1,0},{2,3},{3,2},{4,5},{5,4},{6,7},{7,6},{8,9},{9,8},{10,11... | collective-permute-start | bytes 3932168 | tf_op jit(solution)/shard_map/ppermute | solution.py:241
  9.4 28.8 %collective-permute-start.1 = (bf16[320,1536]{1,0:T(8,128)(2,1)}, bf16[320,1536]{1,0:T(8,128)(2,1)}, u32[]{:S(2)}, u32[]{:S(2)}) collective-permute-start(bf16[320,1536]{1,0:T(8,128)(2,1)} %bitcast.17), channel_id=1, source_target_pairs={{0,224},{32,64},{64,32},{96,128},{128,96},{160,192},{192,160},{224... | collective-permute-start | bytes 2949128 | tf_op jit(solution)/shard_map/ppermute | solution.py:296
  14.7 25.3 %collective-permute-start.2 = (bf16[320,1536]{1,0:T(8,128)(2,1)}, bf16[320,1536]{1,0:T(8,128)(2,1)}, u32[]{:S(2)}, u32[]{:S(2)}) collective-permute-start(bf16[320,1536]{1,0:T(8,128)(2,1)} %bitcast.18), channel_id=1, source_target_pairs={{0,32},{32,0},{64,96},{96,64},{128,160},{160,128},{192,224},{224,1... | collective-permute-start | bytes 2949128 | tf_op jit(solution)/shard_map/ppermute | solution.py:296
  16.7 19.2 %collective-permute-start = (bf16[192,1536]{1,0:T(8,128)(2,1)}, bf16[192,1536]{1,0:T(8,128)(2,1)S(1)}, u32[]{:S(2)}, u32[]{:S(2)}) collective-permute-start(bf16[192,1536]{1,0:T(8,128)(2,1)} %bitcast.12), channel_id=1, source_target_pairs={{0,256},{256,0},{1,257},{257,1},{2,258},{258,2},{3,259},{259,3},{4... | collective-permute-start | bytes 1769480 | tf_op jit(solution)/shard_map/ppermute | solution.py:246
  19.9 3.5 %collective-permute-start.4 = (bf16[64,128]{1,0:T(8,128)(2,1)}, bf16[64,128]{1,0:T(8,128)(2,1)S(1)}, u32[]{:S(2)}, u32[]{:S(2)}) collective-permute-start(bf16[64,128]{1,0:T(8,128)(2,1)} %bitcast.14), channel_id=1, source_target_pairs={{0,1},{1,0},{2,3},{3,2},{4,5},{5,4},{6,7},{7,6},{8,9},{9,8},{10,11... | collective-permute-start | bytes 49160 | tf_op jit(solution)/shard_map/ppermute | solution.py:242
  23.4 1.3 copy-start
  24.7 0.7 copy-start.3
  27.2 8.7 %copy-start.2 = (bf16[1,192,1536]{2,1,0:T(8,128)(2,1)S(1)}, bf16[1,192,1536]{2,1,0:T(8,128)(2,1)}, u32[]{:S(2)}) copy-start(bf16[1,192,1536]{2,1,0:T(8,128)(2,1)} %param.9) | copy-start | bytes 1769476
  27.2 26.6 %all-to-all-start = ((f32[16,80,128]{2,1,0:T(8,128)}), f32[16,80,128]{2,1,0:T(8,128)}, u32[]{:S(2)}, u32[]{:S(2)}) async-start(f32[16,80,128]{2,1,0:T(8,128)} %shard_map.90), calls=%async_computation | async-start | bytes 1310720 | tf_op jit(solution)/shard_map/all_to_all | solution.py:244
  35.9 1.2 copy-start.5
  40.0 27.2 %collective-permute-start.6 = (bf16[320,1536]{1,0:T(8,128)(2,1)}, bf16[320,1536]{1,0:T(8,128)(2,1)}, u32[]{:S(2)}, u32[]{:S(2)}) collective-permute-start(bf16[320,1536]{1,0:T(8,128)(2,1)} %collective-permute-done.1.refs_2_), channel_id=1, source_target_pairs={{0,32},{32,0},{64,96},{96,64},{128,160},{160,128},{192,224},{224,1... | collective-permute-start | bytes 2949128 | tf_op jit(solution)/shard_map/ppermute | solution.py:305
  42.2 25.6 %collective-permute-start.5 = (bf16[320,1536]{1,0:T(8,128)(2,1)}, bf16[320,1536]{1,0:T(8,128)(2,1)}, u32[]{:S(2)}, u32[]{:S(2)}) collective-permute-start(bf16[320,1536]{1,0:T(8,128)(2,1)} %collective-permute-done.2.refs_3_), channel_id=1, source_target_pairs={{0,224},{32,64},{64,32},{96,128},{128,96},{160,192},{192,160},{224... | collective-permute-start | bytes 2949128 | tf_op jit(solution)/shard_map/ppermute | solution.py:305
  53.8 32.1 %all-to-all-start.1 = ((bf16[64,48,128]{2,1,0:T(8,128)(2,1)}), bf16[64,48,128]{2,1,0:T(8,128)(2,1)S(1)}, u32[]{:S(2)}, u32[]{:S(2)}) async-start(bf16[64,48,128]{2,1,0:T(8,128)(2,1)} %shard_map.89), calls=%async_computation.1 | async-start | bytes 1572864 | tf_op jit(solution)/shard_map/all_to_all | solution.py:287
  63.5 8.4 %collective-permute-start.11 = (f32[80,128]{1,0:T(8,128)S(1)}, f32[80,128]{1,0:T(8,128)S(1)}, u32[]{:S(2)}, u32[]{:S(2)}) collective-permute-start(f32[80,128]{1,0:T(8,128)S(1)} %reduce_sum.9), channel_id=1, source_target_pairs={{0,32},{32,0},{64,96},{96,64},{128,160},{160,128},{192,224},{224,1... | collective-permute-start | bytes 122888 | tf_op jit(solution)/shard_map/ppermute | solution.py:272
  67.8 28.0 %collective-permute-start.8 = (bf16[320,1536]{1,0:T(8,128)(2,1)}, bf16[320,1536]{1,0:T(8,128)(2,1)}, u32[]{:S(2)}, u32[]{:S(2)}) collective-permute-start(bf16[320,1536]{1,0:T(8,128)(2,1)} %collective-permute-done.5.refs_1_), channel_id=1, source_target_pairs={{0,32},{32,0},{64,96},{96,64},{128,160},{160,128},{192,224},{224,1... | collective-permute-start | bytes 2949128 | tf_op jit(solution)/shard_map/ppermute | solution.py:311
  69.7 29.1 %collective-permute-start.7 = (bf16[320,1536]{1,0:T(8,128)(2,1)}, bf16[320,1536]{1,0:T(8,128)(2,1)}, u32[]{:S(2)}, u32[]{:S(2)}) collective-permute-start(bf16[320,1536]{1,0:T(8,128)(2,1)} %collective-permute-done.6.refs_2_), channel_id=1, source_target_pairs={{0,224},{32,64},{64,32},{96,128},{128,96},{160,192},{192,160},{224... | collective-permute-start | bytes 2949128 | tf_op jit(solution)/shard_map/ppermute | solution.py:311
  71.9 23.9 %collective-permute-start.12 = (f32[80,128]{1,0:T(8,128)S(1)}, f32[80,128]{1,0:T(8,128)S(1)}, u32[]{:S(2)}, u32[]{:S(2)}) collective-permute-start(f32[80,128]{1,0:T(8,128)S(1)} %add.12), channel_id=1, source_target_pairs={{0,64},{32,96},{64,0},{96,32},{128,192},{160,224},{192,128},{224,1... | collective-permute-start | bytes 122888 | tf_op jit(solution)/shard_map/ppermute | solution.py:272
  85.9 27.4 %all-to-all-start.2 = ((bf16[64,32,128]{2,1,0:T(8,128)(2,1)}), bf16[64,32,128]{2,1,0:T(8,128)(2,1)S(1)}, u32[]{:S(2)}, u32[]{:S(2)}) async-start(bf16[64,32,128]{2,1,0:T(8,128)(2,1)} %shard_map.91.refs_1_), calls=%async_computation.2 | async-start | bytes 1048576 | tf_op jit(solution)/shard_map/all_to_all | solution.py:287
  96.9 12.7 %collective-permute-start.10 = (bf16[160,1536]{1,0:T(8,128)(2,1)S(1)}, bf16[160,1536]{1,0:T(8,128)(2,1)S(1)}, u32[]{:S(2)}, u32[]{:S(2)}) collective-permute-start(bf16[160,1536]{1,0:T(8,128)(2,1)S(1)} %shard_map.94), channel_id=1, source_target_pairs={{0,224},{32,64},{64,32},{96,128},{128,96},{160,192},{192,160},{224... | collective-permute-start | bytes 1474568 | tf_op jit(solution)/shard_map/ppermute | solution.py:331
  99.9 11.3 %collective-permute-start.9 = (bf16[160,1536]{1,0:T(8,128)(2,1)S(1)}, bf16[160,1536]{1,0:T(8,128)(2,1)S(1)}, u32[]{:S(2)}, u32[]{:S(2)}) collective-permute-start(bf16[160,1536]{1,0:T(8,128)(2,1)S(1)} %shard_map.93), channel_id=1, source_target_pairs={{0,32},{32,0},{64,96},{96,64},{128,160},{160,128},{192,224},{224,1... | collective-permute-start | bytes 1474568 | tf_op jit(solution)/shard_map/ppermute | solution.py:330
  113.3 26.8 %copy-start.6 = (f32[128,6]{0,1:T(8,128)S(1)}, f32[128,6]{0,1:T(8,128)}, u32[]{:S(2)}) copy-start(f32[128,6]{0,1:T(8,128)} %param.8) | copy-start | bytes 9220
  113.3 26.9 %copy-start.7 = (s32[128,6]{0,1:T(8,128)S(1)}, s32[128,6]{0,1:T(8,128)}, u32[]{:S(2)}) copy-start(s32[128,6]{0,1:T(8,128)} %param.7) | copy-start | bytes 9220
  113.3 38.0 %copy-start.1 = (bf16[64,5120]{1,0:T(8,128)(2,1)S(1)}, bf16[64,5120]{1,0:T(8,128)(2,1)}, u32[]{:S(2)}) copy-start(bf16[64,5120]{1,0:T(8,128)(2,1)} %refs_3_.1) | copy-start | bytes 1966084
  113.3 38.0 %copy-start.4 = (bf16[128,64]{0,1:T(8,128)(2,1)S(1)}, bf16[128,64]{0,1:T(8,128)(2,1)}, u32[]{:S(2)}) copy-start(bf16[128,64]{0,1:T(8,128)(2,1)} %param.12) | copy-start | bytes 49156
  113.3 38.0 %all-to-all-start.3 = ((bf16[64,48,128]{2,1,0:T(8,128)(2,1)}), bf16[64,48,128]{2,1,0:T(8,128)(2,1)S(1)}, u32[]{:S(2)}, u32[]{:S(2)}) async-start(bf16[64,48,128]{2,1,0:T(8,128)(2,1)} %shard_map.95), calls=%async_computation.3 | async-start | bytes 1572864 | tf_op jit(solution)/shard_map/all_to_all | solution.py:287
  127.7 8.9 %collective-permute-start.13 = (f32[80,128]{1,0:T(8,128)S(1)}, f32[80,128]{1,0:T(8,128)S(1)}, u32[]{:S(2)}, u32[]{:S(2)}) collective-permute-start(f32[80,128]{1,0:T(8,128)S(1)} %add.13.refs_4_), channel_id=1, source_target_pairs={{0,128},{32,160},{64,192},{96,224},{128,0},{160,32},{192,64},{224,... | collective-permute-start | bytes 122888 | tf_op jit(solution)/shard_map/ppermute | solution.py:272
  136.7 10.9 %collective-permute-start.14 = (f32[80,128]{1,0:T(8,128)S(1)}, f32[80,128]{1,0:T(8,128)S(1)}, u32[]{:S(2)}, u32[]{:S(2)}) collective-permute-start(f32[80,128]{1,0:T(8,128)S(1)} %add.14), channel_id=1, source_target_pairs={{0,256},{256,0},{1,257},{257,1},{2,258},{258,2},{3,259},{259,3},{4... | collective-permute-start | bytes 122888 | tf_op jit(solution)/shard_map/ppermute | solution.py:348
